TPU v7x, 32 devices: a whole 2x2x4 slice. The times are simulated.
32 devices in a mesh: shard: 4 (over y, core), rep: 8 (over z, x).
Axes of the slice: x: 2, y: 2, z: 4, core: 2. Of those that a mesh axis runs over, the one named last changes fastest.
Arguments:
- inputs: bfloat16 [16384, 1088], P(('shard', 'rep')), may hold values from -6 to 6
- lengths: int32 [32, 8], P(('shard', 'rep')), may hold values from 0 to 512, as said below
- query_weight: bfloat16 [1088, 1088], P('shard'), may hold values from -0.1875 to 0.1875
- key_weight: bfloat16 [1088, 1088], P('shard'), may hold values from -0.1875 to 0.1875
- value_weight: bfloat16 [1088, 1088], P('shard'), may hold values from -0.1875 to 0.1875
- out_weight: bfloat16 [1088, 1088], P('shard'), may hold values from -0.75 to 0.75
- up_weight: bfloat16 [1088, 4352], P('shard'), may hold values from -0.1875 to 0.1875
- down_weight: bfloat16 [4352, 1088], P('shard'), may hold values from -0.09375 to 0.09375
- query_bias: bfloat16 [1088], P('shard'), may hold values from -1 to 1
- value_bias: bfloat16 [1088], P('shard'), may hold values from -1 to 1
- out_bias: bfloat16 [1088], P('shard'), may hold values from -1 to 1
- up_bias: bfloat16 [4352], P('shard'), may hold values from -1 to 1
- down_bias: bfloat16 [1088], P('shard'), may hold values from -1 to 1
- gain_one: bfloat16 [1088], P('shard'), may hold values from 0.5 to 1.5
- bias_one: bfloat16 [1088], P('shard'), may hold values from -1 to 1
- gain_two: bfloat16 [1088], P('shard'), may hold values from 0.5 to 1.5
- bias_two: bfloat16 [1088], P('shard'), may hold values from -1 to 1
- cotangent: bfloat16 [16384, 1088], P(('shard', 'rep')), may hold values from -6 to 6
Outputs:
- outputs: bfloat16 [16384, 1088], P(('shard', 'rep'))
- grad_inputs: bfloat16 [16384, 1088], P(('shard', 'rep'))
- grad_query: float32 [1088, 1088], P('shard')
- grad_key: float32 [1088, 1088], P('shard')
- grad_value: float32 [1088, 1088], P('shard')
- grad_out: float32 [1088, 1088], P('shard')
- grad_up: float32 [1088, 4352], P('shard')
- grad_down: float32 [4352, 1088], P('shard')
- grad_query_bias: float32 [1088], P('shard')
- grad_value_bias: float32 [1088], P('shard')
- grad_out_bias: float32 [1088], P('shard')
- grad_up_bias: float32 [4352], P('shard')
- grad_down_bias: float32 [1088], P('shard')
- grad_gain_one: float32 [1088], P('shard')
- grad_bias_one: float32 [1088], P('shard')
- grad_gain_two: float32 [1088], P('shard')
- grad_bias_two: float32 [1088], P('shard')
Inputs may be any that keep to these rules, and one draw needn't show every extreme that they name: Row j lists the lengths of the sequences packed into block j of 512 rows, in order, zeros for empty slots; a row sums to at most 512; in every draw some row holds one sequence of exactly 512.
All inputs are finite; a program needn't handle non-finite values.
Results may differ from a plain program's by a relative error of at most 0.017.
Values may be sent and summed in bfloat16 or wider, within the bound.
A program may use at most 192 MiB of HBM per device.

v0:
```python
from functools import partial

import jax
import jax.numpy as jnp
from jax import lax
from jax.sharding import PartitionSpec as P

H = 17
HD = 64


epsilon = 1e-05


def normalize(values, gain, shift):
    center = values - jnp.mean(values, axis=-1, keepdims=True)
    spread = jnp.mean(center * center, axis=-1, keepdims=True)
    return center * lax.rsqrt(spread + epsilon) * gain + shift


def arrange(lengths, count):
    ends = jnp.cumsum(lengths)
    rowids = jnp.arange(count, dtype=jnp.int32)
    segment = jnp.sum((rowids[:, None] >= ends[None, :]).astype(jnp.int32), axis=1)
    inside = rowids < ends[-1]
    segment = jnp.where(inside, segment, lengths.shape[0] + rowids)
    return (segment, inside.astype(jnp.float32))


def outer(left, right):
    return lax.dot_general(
        left, right, (((0,), (0,)), ((), ())), preferred_element_type=jnp.float32
    )


def inner(left, right):
    return lax.dot_general(
        left, right, (((1,), (1,)), ((), ())), preferred_element_type=jnp.float32
    )


def block_scores(query_block, key_heads, query_segment, segment, start, width):
    key_rows = jnp.arange(segment.shape[0], dtype=jnp.int32)
    query_rows = start + jnp.arange(width, dtype=jnp.int32)
    allowed = (query_segment[:, None] == segment[None, :]) & (
        query_rows[:, None] >= key_rows[None, :]
    )
    scores = (
        jnp.einsum("qhd,khd->hqk", query_block, key_heads, preferred_element_type=jnp.float32)
        * 0.125
    )
    return jnp.where(allowed[None], scores, -1e30)


def attend_forward(queries, keys, values, segment):
    count = queries.shape[0]
    width = min(512, count)
    query_heads = queries.reshape(count, H, HD)
    key_heads = keys.reshape(count, H, HD)
    value_heads = values.reshape(count, H, HD)

    def block(index):
        start = index * width
        scores = block_scores(query_heads, key_heads, segment, segment, start, width)
        highest = jnp.max(scores, axis=-1, keepdims=True)
        expo = jnp.exp(scores - highest)
        total = jnp.sum(expo, axis=-1, keepdims=True)
        weights = (expo / total).astype(jnp.bfloat16)
        result = jnp.einsum(
            "hqk,khd->qhd", weights, value_heads, preferred_element_type=jnp.float32
        )
        return (result, (highest + jnp.log(total))[..., 0])

    results, logsums = lax.map(block, jnp.arange(count // width, dtype=jnp.int32))
    return (results.reshape(count, H * HD), logsums)


def attend_backward(queries, keys, values, segment, logsums, grad_mixed):
    count = queries.shape[0]
    width = min(512, count)
    query_heads = queries.reshape(count, H, HD)
    key_heads = keys.reshape(count, H, HD)
    value_heads = values.reshape(count, H, HD)
    grad_heads = grad_mixed.reshape(count, H, HD)

    def block(carry, index):
        grad_keys, grad_values = carry
        start = index * width
        scores = block_scores(query_heads, key_heads, segment, segment, start, width)
        probs = jnp.exp(scores - logsums[index][:, :, None])
        grad_values = grad_values + jnp.einsum(
            "hqk,qhd->khd",
            probs.astype(jnp.bfloat16),
            grad_heads,
            preferred_element_type=jnp.float32,
        )
        grad_probs = jnp.einsum(
            "qhd,khd->hqk", grad_heads, value_heads, preferred_element_type=jnp.float32
        )
        grad_scores = probs * (grad_probs - jnp.sum(probs * grad_probs, axis=-1, keepdims=True))
        grad_scores = (grad_scores * 0.125).astype(jnp.bfloat16)
        grad_query_block = jnp.einsum(
            "hqk,khd->qhd", grad_scores, key_heads, preferred_element_type=jnp.float32
        )
        grad_keys = grad_keys + jnp.einsum(
            "hqk,qhd->khd", grad_scores, query_heads, preferred_element_type=jnp.float32
        )
        return ((grad_keys, grad_values), grad_query_block)

    start_value = jnp.zeros((count, H, HD), jnp.float32)
    (grad_keys, grad_values), grad_queries = lax.scan(
        block, (start_value, start_value), jnp.arange(count // width, dtype=jnp.int32)
    )
    return (
        grad_queries.reshape(count, H * HD).astype(jnp.bfloat16),
        grad_keys.reshape(count, H * HD).astype(jnp.bfloat16),
        grad_values.reshape(count, H * HD).astype(jnp.bfloat16),
    )


def column_sum(values):
    return jnp.sum(values.astype(jnp.float32), axis=0)


def shards(
    inputs,
    lengths,
    query_weight,
    key_weight,
    value_weight,
    out_weight,
    up_weight,
    down_weight,
    query_bias,
    value_bias,
    out_bias,
    up_bias,
    down_bias,
    gain_one,
    bias_one,
    gain_two,
    bias_two,
    cotangent,
):
    segment, inside = arrange(lengths[0], inputs.shape[0])
    attention_parts = (
        lax.all_gather(query_weight, "shard", axis=0, tiled=True),
        lax.all_gather(key_weight, "shard", axis=0, tiled=True),
        lax.all_gather(value_weight, "shard", axis=0, tiled=True),
        lax.all_gather(out_weight, "shard", axis=0, tiled=True),
        lax.all_gather(query_bias, "shard", axis=0, tiled=True),
        lax.all_gather(value_bias, "shard", axis=0, tiled=True),
        lax.all_gather(out_bias, "shard", axis=0, tiled=True),
        lax.all_gather(gain_one, "shard", axis=0, tiled=True),
        lax.all_gather(bias_one, "shard", axis=0, tiled=True),
    )
    full_query, full_key, full_value, full_out = (
        attention_parts[0],
        attention_parts[1],
        attention_parts[2],
        attention_parts[3],
    )
    query_shift = attention_parts[4].astype(jnp.float32)
    value_shift = attention_parts[5].astype(jnp.float32)
    out_shift = attention_parts[6].astype(jnp.float32)
    first_gain = attention_parts[7].astype(jnp.float32)
    first_shift = attention_parts[8].astype(jnp.float32)
    residual = inputs.astype(jnp.float32)
    normed_one = normalize(residual, first_gain, first_shift).astype(jnp.bfloat16)
    queries = (
        jnp.dot(normed_one, full_query, preferred_element_type=jnp.float32) + query_shift
    ).astype(jnp.bfloat16)
    keys = jnp.dot(normed_one, full_key, preferred_element_type=jnp.float32).astype(jnp.bfloat16)
    values = (
        jnp.dot(normed_one, full_value, preferred_element_type=jnp.float32) + value_shift
    ).astype(jnp.bfloat16)
    mixed_float, logsums = attend_forward(queries, keys, values, segment)
    mixed = mixed_float.astype(jnp.bfloat16)
    middle = residual + jnp.dot(mixed, full_out, preferred_element_type=jnp.float32) + out_shift
    network_parts = (
        lax.all_gather(up_weight, "shard", axis=0, tiled=True),
        lax.all_gather(down_weight, "shard", axis=0, tiled=True),
        lax.all_gather(up_bias, "shard", axis=0, tiled=True),
        lax.all_gather(down_bias, "shard", axis=0, tiled=True),
        lax.all_gather(gain_two, "shard", axis=0, tiled=True),
        lax.all_gather(bias_two, "shard", axis=0, tiled=True),
    )
    full_up, full_down = (network_parts[0], network_parts[1])
    up_shift = network_parts[2].astype(jnp.float32)
    down_shift = network_parts[3].astype(jnp.float32)
    second_gain = network_parts[4].astype(jnp.float32)
    second_shift = network_parts[5].astype(jnp.float32)
    normed_two = normalize(middle, second_gain, second_shift).astype(jnp.bfloat16)
    pre_hidden = jnp.dot(normed_two, full_up, preferred_element_type=jnp.float32) + up_shift
    hidden = jax.nn.gelu(pre_hidden, approximate=False).astype(jnp.bfloat16)
    result = middle + jnp.dot(hidden, full_down, preferred_element_type=jnp.float32) + down_shift
    outputs = (result * inside[:, None]).astype(jnp.bfloat16)
    network_back = (
        lax.all_gather(up_weight, "shard", axis=0, tiled=True),
        lax.all_gather(down_weight, "shard", axis=0, tiled=True),
    )
    back_up, back_down = (network_back[0], network_back[1])
    upstream = cotangent.astype(jnp.float32) * inside[:, None]
    upstream_low = upstream.astype(jnp.bfloat16)
    grad_down_term = outer(hidden, upstream_low)
    grad_hidden = inner(upstream_low, back_down)
    _, gelu_pull = jax.vjp(partial(jax.nn.gelu, approximate=False), pre_hidden)
    grad_pre = gelu_pull(grad_hidden)[0].astype(jnp.bfloat16)
    grad_up_term = outer(normed_two, grad_pre)
    grad_normed_two = inner(grad_pre, back_up)
    _, second_pull = jax.vjp(normalize, middle, second_gain, second_shift)
    grad_middle_norm, grad_second_gain, grad_second_shift = second_pull(grad_normed_two)
    grad_middle = upstream + grad_middle_norm
    network_owned = (
        lax.psum_scatter(
            grad_up_term.astype(jnp.bfloat16), "shard", scatter_dimension=0, tiled=True
        ).astype(jnp.float32),
        lax.psum_scatter(
            grad_down_term.astype(jnp.bfloat16), "shard", scatter_dimension=0, tiled=True
        ).astype(jnp.float32),
        lax.psum_scatter(
            column_sum(grad_pre).astype(jnp.bfloat16), "shard", scatter_dimension=0, tiled=True
        ).astype(jnp.float32),
        lax.psum_scatter(
            column_sum(upstream_low).astype(jnp.bfloat16), "shard", scatter_dimension=0, tiled=True
        ).astype(jnp.float32),
        lax.psum_scatter(
            grad_second_gain.astype(jnp.bfloat16), "shard", scatter_dimension=0, tiled=True
        ).astype(jnp.float32),
        lax.psum_scatter(
            grad_second_shift.astype(jnp.bfloat16), "shard", scatter_dimension=0, tiled=True
        ).astype(jnp.float32),
    )
    network_total = lax.psum(
        (
            network_owned[0],
            network_owned[1],
            network_owned[2],
            network_owned[3],
            network_owned[4],
            network_owned[5],
        ),
        "rep",
    )
    attention_back = (
        lax.all_gather(query_weight, "shard", axis=0, tiled=True),
        lax.all_gather(key_weight, "shard", axis=0, tiled=True),
        lax.all_gather(value_weight, "shard", axis=0, tiled=True),
        lax.all_gather(out_weight, "shard", axis=0, tiled=True),
    )
    back_query, back_key, back_value, back_out = (
        attention_back[0],
        attention_back[1],
        attention_back[2],
        attention_back[3],
    )
    grad_branch = grad_middle.astype(jnp.bfloat16)
    grad_out_term = outer(mixed, grad_branch)
    grad_mixed = inner(grad_branch, back_out).astype(jnp.bfloat16)
    grad_queries, grad_keys, grad_values = attend_backward(
        queries, keys, values, segment, logsums, grad_mixed
    )
    grad_query_term = outer(normed_one, grad_queries)
    grad_key_term = outer(normed_one, grad_keys)
    grad_value_term = outer(normed_one, grad_values)
    grad_normed_one = (
        inner(grad_queries, back_query)
        + inner(grad_keys, back_key)
        + inner(grad_values, back_value)
    )
    _, first_pull = jax.vjp(normalize, residual, first_gain, first_shift)
    grad_residual_norm, grad_first_gain, grad_first_shift = first_pull(grad_normed_one)
    grad_inputs = (grad_middle + grad_residual_norm).astype(jnp.bfloat16)
    attention_owned = (
        lax.psum_scatter(
            grad_query_term.astype(jnp.bfloat16), "shard", scatter_dimension=0, tiled=True
        ).astype(jnp.float32),
        lax.psum_scatter(
            grad_key_term.astype(jnp.bfloat16), "shard", scatter_dimension=0, tiled=True
        ).astype(jnp.float32),
        lax.psum_scatter(
            grad_value_term.astype(jnp.bfloat16), "shard", scatter_dimension=0, tiled=True
        ).astype(jnp.float32),
        lax.psum_scatter(
            grad_out_term.astype(jnp.bfloat16), "shard", scatter_dimension=0, tiled=True
        ).astype(jnp.float32),
        lax.psum_scatter(
            column_sum(grad_queries).astype(jnp.bfloat16), "shard", scatter_dimension=0, tiled=True
        ).astype(jnp.float32),
        lax.psum_scatter(
            column_sum(grad_values).astype(jnp.bfloat16), "shard", scatter_dimension=0, tiled=True
        ).astype(jnp.float32),
        lax.psum_scatter(
            column_sum(grad_branch).astype(jnp.bfloat16), "shard", scatter_dimension=0, tiled=True
        ).astype(jnp.float32),
        lax.psum_scatter(
            grad_first_gain.astype(jnp.bfloat16), "shard", scatter_dimension=0, tiled=True
        ).astype(jnp.float32),
        lax.psum_scatter(
            grad_first_shift.astype(jnp.bfloat16), "shard", scatter_dimension=0, tiled=True
        ).astype(jnp.float32),
    )
    attention_total = lax.psum(
        (
            attention_owned[0],
            attention_owned[1],
            attention_owned[2],
            attention_owned[3],
            attention_owned[4],
            attention_owned[5],
            attention_owned[6],
            attention_owned[7],
            attention_owned[8],
        ),
        "rep",
    )
    return (
        outputs,
        grad_inputs,
        attention_total[0],
        attention_total[1],
        attention_total[2],
        attention_total[3],
        network_total[0],
        network_total[1],
        attention_total[4],
        attention_total[5],
        attention_total[6],
        network_total[2],
        network_total[3],
        attention_total[7],
        attention_total[8],
        network_total[4],
        network_total[5],
    )


def solution(mesh):
    return jax.shard_map(
        shards,
        mesh=mesh,
        in_specs=(
            P(("shard", "rep"), None),
            P(("shard", "rep"), None),
            P("shard", None),
            P("shard", None),
            P("shard", None),
            P("shard", None),
            P("shard", None),
            P("shard", None),
            P("shard"),
            P("shard"),
            P("shard"),
            P("shard"),
            P("shard"),
            P("shard"),
            P("shard"),
            P("shard"),
            P("shard"),
            P(("shard", "rep"), None),
        ),
        out_specs=(
            P(("shard", "rep"), None),
            P(("shard", "rep"), None),
            P("shard", None),
            P("shard", None),
            P("shard", None),
            P("shard", None),
            P("shard", None),
            P("shard", None),
            P("shard"),
            P("shard"),
            P("shard"),
            P("shard"),
            P("shard"),
            P("shard"),
            P("shard"),
            P("shard"),
            P("shard"),
        ),
        check_vma=False,
    )
```

profile of v0, /device:TPU:0, one launch (start us, length us, event | category | flops | bytes accessed | tf_op | source)
XLA Modules:
  0.0 1172.8 jit_solution(3022360393119888842)
XLA Ops:
  7.2 0.7 all-gather.11.cloned.1.call-update
  8.0 0.7 all-gather.9.cloned.1.call-update
  8.7 0.7 all-gather.7.cloned.1.call-update
  16.0 15.1 %all-reduce.20 = (bf16[1088]{0:T(1024)(128)(2,1)S(1)}, bf16[1088]{0:T(1024)(128)(2,1)S(1)}, bf16[1088]{0:T(1024)(128)(2,1)S(1)}, bf16[1088]{0:T(1024)(128)(2,1)S...) all-reduce(bf16[1088]{0:T(1024)(128)(2,1)S(1)} %dynamic-update-slic, ...), channel_id=1, replica_groups=mesh['shard'=4,'rep'=8] {'shard'}, use_global_device_ids=true, to_apply=%add.2 | all-reduce | flops 11968 | bytes 47872
  31.2 0.7 fusion.60
  32.6 0.7 add_select_fusion
  33.2 0.9 fusion.52
  34.1 3.9 all-gather.11.cloned.1.call-done
  38.0 3.6 convolution_convert_fusion.7
  41.6 22.9 %all-gather.9.cloned.1.call-done = bf16[1088,1088]{1,0:T(8,128)(2,1)} async-done(((bf16[272,1088]{1,0:T(8,128)(2,1)}), bf16[1088,1088]{1,0:T(8,128)(2,1)}) %all-gather.9.cloned.1.call-update) | async-done | bytes 2367504 | tf_op jit(solution)/shard_map/all_gather | solution.py:147
  64.5 3.6 fusion.31
  68.2 22.9 %all-gather.7.cloned.1.call-done = bf16[1088,1088]{1,0:T(8,128)(2,1)} async-done(((bf16[272,1088]{1,0:T(8,128)(2,1)}), bf16[1088,1088]{1,0:T(8,128)(2,1)}) %all-gather.7.cloned.1.call-update) | async-done | bytes 2367504 | tf_op jit(solution)/shard_map/all_gather | solution.py:149
  91.0 4.7 fusion.30
  95.7 8.1 fusion.80
  103.8 9.0 fusion.2
  112.8 9.1 fusion.41
  121.9 3.8 fusion.81
  126.0 57.2 %all-gather.15.cloned.1.call-done = bf16[1088,4352]{1,0:T(8,128)(2,1)} async-done(((bf16[272,4352]{1,0:T(8,128)(2,1)}), bf16[1088,4352]{1,0:T(8,128)(2,1)}) %all-gather.15.cloned.1.call-update) | async-done | bytes 9469968 | tf_op jit(solution)/shard_map/all_gather | solution.py:181
  183.3 32.0 %multiply_convert_fusion.1 = (bf16[512,4352]{1,0:T(8,128)(2,1)}, f32[512,4352]{1,0:T(8,128)}, f32[512,4352]{1,0:T(8,128)}) fusion(f32[4352]{0:T(1024)S(1)} %convert_element_type.234, bf16[1088,4352]{1,0:T(8,128)(2,1)} %all-gather.15.cloned.1.call-done, f32[512,1088]{0,1:T(8,128)S(1)} %get-tuple-element.120, f32[1088]{0:T(1024)S(1)} %convert_element_type.232, ...), kind=kOutput, calls=%fused_computation.18 | convolution fusion | flops 4998463488 | bytes 34010624 | tf_op jit(solution)/shard_map/dot_general | solution.py:194
  215.3 37.0 %all-gather.17.cloned.1.call-done = bf16[4352,1088]{1,0:T(8,128)(2,1)} async-done(((bf16[1088,1088]{1,0:T(8,128)(2,1)}), bf16[4352,1088]{1,0:T(8,128)(2,1)}) %all-gather.17.cloned.1.call-update) | async-done | bytes 9469968 | tf_op jit(solution)/shard_map/all_gather | solution.py:182
  252.3 15.2 %fusion.86 = (bf16[4352]{0:T(1024)(128)(2,1)S(1)}, bf16[512,4352]{1,0:T(8,128)(2,1)}) fusion(f32[512,4352]{1,0:T(8,128)} %get-tuple-element.113, bf16[4352,1088]{1,0:T(8,128)(2,1)} %all-gather.17.cloned.1.call-done, bf16[512,1088]{0,1:T(8,128)(2,1)} %param.35, f32[512]{0:T(512)S(1)} %fusion.60, f32[512,4352]{1,0:T(8,128)} %get-tuple-element.121, ...), kind=kOutput, calls=%fused_computation.124 | convolution fusion | flops 4885934080 | bytes 32894464 | tf_op jit(solution)/shard_map/dot_general | solution.py:37
  267.5 10.6 multiply_reduce_fusion.1
  278.1 2.3 fusion.77
  280.5 0.7 fusion.75
  281.2 1.0 copy-done.11
  282.2 3.1 convolution_convert_fusion.2
  285.8 3.6 convolution_convert_fusion.6
  289.4 10.6 fusion.85
  300.1 1.0 copy-done.7
  301.1 3.2 convolution_convert_fusion.3
  304.4 10.2 fusion.87
  314.6 26.7 %fusion.48 = bf16[17,64,512]{2,1,0:T(8,128)(2,1)} fusion(bf16[512,17,64]{0,2,1:T(8,128)(2,1)} %bitcast.63, f32[17,512,512]{1,2,0:T(8,128)} %fusion.87, f32[17,512,512]{1,2,0:T(8,128)} %get-tuple-element.118, f32[17,512]{1,0:T(8,128)S(1)} %log_add_fusion), kind=kOutput, calls=%fused_computation.79 | convolution fusion | flops 602186752 | bytes 37914624 | tf_op jit(solution)/shard_map/while/body/eval_jaxpr/hqk,qhd->khd/dot_general | solution.py:105
  341.3 4.5 convolution_convert_fusion.4
  346.0 26.5 %fusion.82 = (bf16[17,64]{1,0:T(8,128)(2,1)S(1)}, bf16[17,64,512]{2,1,0:T(8,128)(2,1)}) fusion(bf16[512,17,64]{0,2,1:T(8,128)(2,1)} %bitcast.59, f32[17,512,512]{1,2,0:T(8,128)} %fusion.87, f32[17,512,512]{1,2,0:T(8,128)} %get-tuple-element.118, f32[17,512]{1,0:T(8,128)S(1)} %log_add_fusion), kind=kOutput, calls=%fused_computation.122 | convolution fusion | flops 602742720 | bytes 37916800 | tf_op jit(solution)/shard_map/while/body/eval_jaxpr/hqk,khd->qhd/dot_general | solution.py:102
  372.6 4.5 convolution_convert_fusion.5
  377.7 10.4 convolution_convert_fusion.1
  388.4 10.5 convolution_convert_fusion
  400.6 3.8 fusion.88
  404.5 1.6 convolution_add_fusion.1
  406.6 2.0 fusion.74
  408.7 1.3 copy-done.3
  410.0 1.1 fusion.37
  411.1 12.8 %all-reduce.19 = (bf16[1088]{0:T(1024)(128)(2,1)S(1)}, bf16[1088]{0:T(1024)(128)(2,1)S(1)}, bf16[1088]{0:T(1024)(128)(2,1)S(1)}, bf16[1088]{0:T(1024)(128)(2,1)S...) all-reduce(bf16[1088]{0:T(1024)(128)(2,1)S(1)} %dynamic-update-slic, ...), channel_id=1, replica_groups=mesh['shard'=4,'rep'=8] {'shard'}, use_global_device_ids=true, to_apply=%add.8 | all-reduce | flops 14144 | bytes 56576
  424.3 4.1 add_convert_fusion.1
  428.4 13.3 %fusion.32 = bf16[512,1088]{0,1:T(8,128)(2,1)} fusion(f32[512,1088]{0,1:T(8,128)S(1)} %copy-done.2, bf16[512,4352]{1,0:T(8,128)(2,1)} %get-tuple-element.112, bf16[4352,1088]{1,0:T(8,128)(2,1)} %all-gather.17.cloned.1.call-done, f32[512]{0:T(512)S(1)} %fusion.60, f32[1088]{0:T(1024)S(1)} %convert_element_type.236), kind=kOutput, calls=%fused_computation.60 | convolution fusion | flops 4850843648 | bytes 17275136 | tf_op jit(solution)/shard_map/dot_general | solution.py:196
  441.7 69.6 %reduce-scatter.15.cloned.1.call-done = bf16[272,4352]{1,0:T(8,128)(2,1)} async-done(((bf16[1088,4352]{1,0:T(8,128)(2,1)}), bf16[272,4352]{1,0:T(8,128)(2,1)}) %reduce-scatter.15.cloned.1.call-update) | async-done | bytes 2367504 | tf_op jit(solution)/shard_map/reduce_scatter | solution.py:215
  511.4 84.8 %reduce-scatter.17.cloned.1.call-done = bf16[1088,1088]{1,0:T(8,128)(2,1)} async-done(((bf16[4352,1088]{1,0:T(8,128)(2,1)}), bf16[1088,1088]{1,0:T(8,128)(2,1)}) %reduce-scatter.17.cloned.1.call-update) | async-done | bytes 2367504 | tf_op jit(solution)/shard_map/reduce_scatter | solution.py:218
  596.2 569.5 %all-reduce.22 = (f32[272,1088]{1,0:T(8,128)}, f32[272,1088]{1,0:T(8,128)}, f32[272,1088]{1,0:T(8,128)}, f32[272,1088]{1,0:T(8,128)}, f32[272,4352]{1,0:T(8,128)...) all-reduce(bf16[272,1088]{1,0:T(8,128)(2,1)} %reduce-scatter.7.clon, ...), channel_id=1, replica_groups=mesh['shard'=4,'rep'=8] {'rep'}, use_global_device_ids=true, to_apply=%region_14.15 | all-reduce | flops 3554496 | bytes 21333504 | tf_op jit(solution)/shard_map/psum | solution.py:303
  (143 shorter events, 9.5 us)
Async XLA Ops:
  7.2 30.8 %all-gather.11.cloned.1.call-start = ((), (), s32[]{:S(2)}) async-start(), calls=%async_computation.8 | async-start | bytes 3133440 | tf_op jit(solution)/shard_map/all_gather | solution.py:148
  7.9 56.6 %all-gather.9.cloned.1.call-start = ((), (), s32[]{:S(2)}) async-start(), calls=%async_computation.7 | async-start | bytes 3133440 | tf_op jit(solution)/shard_map/all_gather | solution.py:147
  8.7 82.4 %all-gather.7.cloned.1.call-start = ((), (), s32[]{:S(2)}) async-start(), calls=%async_computation.6 | async-start | bytes 3133440 | tf_op jit(solution)/shard_map/all_gather | solution.py:149
  9.4 112.5 %all-gather.13.cloned.1.call-start = ((), (), s32[]{:S(2)}) async-start(), calls=%async_computation.9 | async-start | bytes 3133440 | tf_op jit(solution)/shard_map/all_gather | solution.py:150
  10.0 1.3 copy-start.21
  10.0 3.2 copy-start.32
  10.0 4.0 copy-start.22
  10.0 4.2 copy-start.23
  10.0 4.4 copy-start.24
  10.0 4.7 copy-start.25
  10.1 4.9 copy-start.26
  10.1 5.2 copy-start.27
  10.1 5.4 copy-start.28
  10.1 5.7 copy-start.20
  10.1 21.9 %copy-start = (bf16[512,1088]{0,1:T(8,128)(2,1)S(1)}, bf16[512,1088]{0,1:T(8,128)(2,1)}, u32[]{:S(2)}) copy-start(bf16[512,1088]{0,1:T(8,128)(2,1)} %param.18) | copy-start | bytes 3342340
  10.1 173.2 %all-gather.15.cloned.1.call-start = ((), (), s32[]{:S(2)}) async-start(), calls=%async_computation.10 | async-start | bytes 11837440 | tf_op jit(solution)/shard_map/all_gather | solution.py:181
  10.7 241.6 %all-gather.17.cloned.1.call-start = ((), (), s32[]{:S(2)}) async-start(), calls=%async_computation.11 | async-start | bytes 12533760 | tf_op jit(solution)/shard_map/all_gather | solution.py:182
  11.3 430.4 %reduce-scatter.13.cloned.1.call-start = ((), (), s32[]{:S(2)}) async-start(), calls=%async_computation.15 | async-start | bytes 3133440 | tf_op jit(solution)/shard_map/reduce_scatter | solution.py:284
  31.1 59.9 %copy-start.17 = (f32[1088]{0:T(1024)}, f32[1088]{0:T(1024)S(1)}, u32[]{:S(2)}) copy-start(f32[1088]{0:T(1024)S(1)} %convert_element_type.218) | copy-start | bytes 13060
  31.2 152.1 %copy-start.15 = (f32[1088]{0:T(1024)}, f32[1088]{0:T(1024)S(1)}, u32[]{:S(2)}) copy-start(f32[1088]{0:T(1024)S(1)} %convert_element_type.232) | copy-start | bytes 13060
  32.6 9.1 copy-start.13
  41.6 54.1 %copy-start.6 = (bf16[512,1088]{0,1:T(8,128)(2,1)}, bf16[512,1088]{0,1:T(8,128)(2,1)S(1)}, u32[]{:S(2)}) copy-start(bf16[512,1088]{0,1:T(8,128)(2,1)S(1)} %convolution_convert_fusion.7) | copy-start | bytes 3342340
  68.2 27.6 %copy-start.9 = (bf16[512,1088]{0,1:T(8,128)(2,1)}, bf16[512,1088]{0,1:T(8,128)(2,1)S(1)}, u32[]{:S(2)}) copy-start(bf16[512,1088]{0,1:T(8,128)(2,1)S(1)} %fusion.31) | copy-start | bytes 3342340
  91.0 4.7 copy-start.12
  103.8 9.0 copy-start.10
  125.7 141.8 %copy-start.1 = (f32[512,1088]{0,1:T(8,128)}, f32[512,1088]{0,1:T(8,128)S(1)}, u32[]{:S(2)}) copy-start(f32[512,1088]{0,1:T(8,128)S(1)} %get-tuple-element.120) | copy-start | bytes 6684676
  278.1 2.3 copy-start.5
  280.5 1.7 copy-start.34
  281.2 1.0 copy-start.11
  285.3 156.4 %reduce-scatter.11.cloned.1.call-start = ((), (), s32[]{:S(2)}) async-start(), calls=%async_computation.14 | async-start | bytes 3133440 | tf_op jit(solution)/shard_map/reduce_scatter | solution.py:281
  289.4 10.7 copy-start.4
  289.4 11.7 copy-start.18
  300.1 1.0 copy-start.7
  304.3 137.4 %reduce-scatter.9.cloned.1.call-start = ((), (), s32[]{:S(2)}) async-start(), calls=%async_computation.13 | async-start | bytes 3133440 | tf_op jit(solution)/shard_map/reduce_scatter | solution.py:278
  345.8 95.9 %reduce-scatter.7.cloned.1.call-start = ((), (), s32[]{:S(2)}) async-start(), calls=%async_computation.12 | async-start | bytes 3133440 | tf_op jit(solution)/shard_map/reduce_scatter | solution.py:275
  377.0 0.7 copy-start.16
  377.1 134.3 %reduce-scatter.15.cloned.1.call-start = ((), (), s32[]{:S(2)}) async-start(), calls=%async_computation.16 | async-start | bytes 11837440 | tf_op jit(solution)/shard_map/reduce_scatter | solution.py:215
  388.1 208.1 %reduce-scatter.17.cloned.1.call-start = ((), (), s32[]{:S(2)}) async-start(), calls=%async_computation.17 | async-start | bytes 12533760 | tf_op jit(solution)/shard_map/reduce_scatter | solution.py:218
  398.9 1.3 copy-start.29
  400.6 3.8 copy-start.30
  400.6 3.8 copy-start.33
  404.5 1.6 copy-start.8
  404.5 2.2 copy-start.31
  406.6 2.0 copy-start.14
  408.6 1.4 copy-start.3
  408.6 2.4 copy-start.19
  424.3 4.1 copy-start.2
Sparse Core Ops, SparseCore 0:
  9.6 28.3 all-gather.10
  39.6 24.8 all-gather.8
  66.1 24.8 all-gather.6
  92.4 24.8 all-gather.12
  118.8 64.4 all-gather.14
  184.7 67.5 all-gather.16
  285.4 33.9 reduce-scatter.12
  322.2 33.9 reduce-scatter.10
  358.8 33.9 reduce-scatter.8
  395.4 34.7 reduce-scatter.6
  432.8 78.5 reduce-scatter.14
  513.8 82.3 reduce-scatter.16
where the time goes:
time: 1180 us; the launch traced here: 1170 us
  blocking collectives  597 us (51%)
  waiting for transfers between devices  302 us (26%)
  matrix products  225 us (19%)
  other arithmetic  21 us (2%)
  between operations  17.6 us (1%)
    psum x1, blocking collectives, shards(): lax.psum((attention_owned[0], attention_owned[1], attention_owned[2], att...  569 us
    reduce_scatter x1, waiting for transfers between devices, shards(): lax.psum_scatter(grad_down_term.astype(jnp.bfloat16), 'shard', scatter_di...  84.8 us
    reduce_scatter x1, waiting for transfers between devices, shards(): lax.psum_scatter(grad_up_term.astype(jnp.bfloat16), 'shard', scatter_dime...  69.6 us
    all_gather x1, waiting for transfers between devices, shards(): lax.all_gather(up_weight, 'shard', axis=0, tiled=True)  57.2 us
    all_gather x1, waiting for transfers between devices, shards(): lax.all_gather(down_weight, 'shard', axis=0, tiled=True)  37 us
    dot_general x6, matrix products, inner(): lax.dot_general(left, right, (((1,), (1,)), ((), ())), preferred_element_...  36.8 us
    dot_general x6, matrix products, outer(): lax.dot_general(left, right, (((0,), (0,)), ((), ())), preferred_element_...  36.2 us
    dot_general x1, matrix products, shards(): jnp.dot(normed_two, full_up, preferred_element_type=jnp.float32) + up_shift  32 us
  transfers between devices with their start and end apart: 12, of which 7 were waited for; matrix products, arithmetic and copies ran while one was open for 19% of the time, Pallas kernels for 0%

commit v1 on v0

--- a/solution.py
+++ b/solution.py
@@ -120,6 +120,76 @@
 
 def column_sum(values):
     return jnp.sum(values.astype(jnp.float32), axis=0)
+
+
+def swap(value, axis, bit):
+    size = lax.axis_size(axis)
+    return lax.ppermute(value, axis, [(i, i ^ bit) for i in range(size)])
+
+
+def has_bit(axis, bit):
+    return (lax.axis_index(axis) // bit) % 2
+
+
+def halve(value, axis, bit, dim):
+    mine = has_bit(axis, bit)
+    half = value.shape[dim] // 2
+    keep = lax.dynamic_slice_in_dim(value, mine * half, half, dim)
+    give = lax.dynamic_slice_in_dim(value, (1 - mine) * half, half, dim)
+    got = swap(give, axis, bit)
+    return (keep.astype(jnp.float32) + got.astype(jnp.float32)).astype(value.dtype)
+
+
+def double(value, axis, bit, dim):
+    got = swap(value, axis, bit)
+    mine = has_bit(axis, bit)
+    first = jnp.where(mine == 0, value, got)
+    second = jnp.where(mine == 0, got, value)
+    return jnp.concatenate([first, second], axis=dim)
+
+
+def exchange_sum(value, axis, bit):
+    return (value.astype(jnp.float32) + swap(value, axis, bit).astype(jnp.float32)).astype(
+        value.dtype
+    )
+
+
+def reduce_owned(term, first_dim, second_dim):
+    shards_count = lax.axis_size("shard")
+    rep_count = lax.axis_size("rep")
+    trailing = term.shape[1:]
+    bits = []
+    bit = 1
+    while bit < shards_count:
+        bits.append(bit)
+        bit *= 2
+    term = term.reshape((2,) * len(bits) + trailing)
+    for place, bit in enumerate(bits):
+        dim = len(bits) - 1 - place
+        term = halve(term, "shard", bit, dim)
+    term = term.reshape(trailing)
+    split = []
+    bit = 1
+    while bit < rep_count:
+        if len(split) < 2:
+            dim = (first_dim, second_dim)[len(split)]
+            term = halve(term, "rep", bit, dim)
+            split.append((bit, dim))
+        else:
+            term = exchange_sum(term, "rep", bit)
+        bit *= 2
+    for bit, dim in reversed(split):
+        term = double(term, "rep", bit, dim)
+    return term.astype(jnp.float32)
+
+
+def reduce_small(term):
+    for axis in ("shard", "rep"):
+        bit = 1
+        while bit < lax.axis_size(axis):
+            term = exchange_sum(term, axis, bit)
+            bit *= 2
+    return lax.dynamic_index_in_dim(term, lax.axis_index("shard"), 0, keepdims=False)
 
 
 def shards(
@@ -211,36 +281,12 @@
     _, second_pull = jax.vjp(normalize, middle, second_gain, second_shift)
     grad_middle_norm, grad_second_gain, grad_second_shift = second_pull(grad_normed_two)
     grad_middle = upstream + grad_middle_norm
-    network_owned = (
-        lax.psum_scatter(
-            grad_up_term.astype(jnp.bfloat16), "shard", scatter_dimension=0, tiled=True
-        ).astype(jnp.float32),
-        lax.psum_scatter(
-            grad_down_term.astype(jnp.bfloat16), "shard", scatter_dimension=0, tiled=True
-        ).astype(jnp.float32),
-        lax.psum_scatter(
-            column_sum(grad_pre).astype(jnp.bfloat16), "shard", scatter_dimension=0, tiled=True
-        ).astype(jnp.float32),
-        lax.psum_scatter(
-            column_sum(upstream_low).astype(jnp.bfloat16), "shard", scatter_dimension=0, tiled=True
-        ).astype(jnp.float32),
-        lax.psum_scatter(
-            grad_second_gain.astype(jnp.bfloat16), "shard", scatter_dimension=0, tiled=True
-        ).astype(jnp.float32),
-        lax.psum_scatter(
-            grad_second_shift.astype(jnp.bfloat16), "shard", scatter_dimension=0, tiled=True
-        ).astype(jnp.float32),
-    )
-    network_total = lax.psum(
-        (
-            network_owned[0],
-            network_owned[1],
-            network_owned[2],
-            network_owned[3],
-            network_owned[4],
-            network_owned[5],
-        ),
-        "rep",
+    count = lax.axis_size("shard")
+    down_total = reduce_owned(
+        grad_down_term.astype(jnp.bfloat16).reshape(count, -1, grad_down_term.shape[1]), 0, 0
+    )
+    up_total = reduce_owned(
+        grad_up_term.astype(jnp.bfloat16).reshape(count, -1, grad_up_term.shape[1]), 0, 1
     )
     attention_back = (
         lax.all_gather(query_weight, "shard", axis=0, tiled=True),
@@ -271,67 +317,51 @@
     _, first_pull = jax.vjp(normalize, residual, first_gain, first_shift)
     grad_residual_norm, grad_first_gain, grad_first_shift = first_pull(grad_normed_one)
     grad_inputs = (grad_middle + grad_residual_norm).astype(jnp.bfloat16)
-    attention_owned = (
-        lax.psum_scatter(
-            grad_query_term.astype(jnp.bfloat16), "shard", scatter_dimension=0, tiled=True
-        ).astype(jnp.float32),
-        lax.psum_scatter(
-            grad_key_term.astype(jnp.bfloat16), "shard", scatter_dimension=0, tiled=True
-        ).astype(jnp.float32),
-        lax.psum_scatter(
-            grad_value_term.astype(jnp.bfloat16), "shard", scatter_dimension=0, tiled=True
-        ).astype(jnp.float32),
-        lax.psum_scatter(
-            grad_out_term.astype(jnp.bfloat16), "shard", scatter_dimension=0, tiled=True
-        ).astype(jnp.float32),
-        lax.psum_scatter(
-            column_sum(grad_queries).astype(jnp.bfloat16), "shard", scatter_dimension=0, tiled=True
-        ).astype(jnp.float32),
-        lax.psum_scatter(
-            column_sum(grad_values).astype(jnp.bfloat16), "shard", scatter_dimension=0, tiled=True
-        ).astype(jnp.float32),
-        lax.psum_scatter(
-            column_sum(grad_branch).astype(jnp.bfloat16), "shard", scatter_dimension=0, tiled=True
-        ).astype(jnp.float32),
-        lax.psum_scatter(
-            grad_first_gain.astype(jnp.bfloat16), "shard", scatter_dimension=0, tiled=True
-        ).astype(jnp.float32),
-        lax.psum_scatter(
-            grad_first_shift.astype(jnp.bfloat16), "shard", scatter_dimension=0, tiled=True
-        ).astype(jnp.float32),
-    )
-    attention_total = lax.psum(
-        (
-            attention_owned[0],
-            attention_owned[1],
-            attention_owned[2],
-            attention_owned[3],
-            attention_owned[4],
-            attention_owned[5],
-            attention_owned[6],
-            attention_owned[7],
-            attention_owned[8],
-        ),
-        "rep",
-    )
+
+    def paired(one, two):
+        width = one.shape[1]
+        return jnp.stack(
+            [
+                one.astype(jnp.bfloat16).reshape(count, -1, width),
+                two.astype(jnp.bfloat16).reshape(count, -1, width),
+            ],
+            axis=1,
+        )
+
+    first_pair = reduce_owned(paired(grad_out_term, grad_value_term), 1, 0)
+    second_pair = reduce_owned(paired(grad_query_term, grad_key_term), 1, 0)
+    small = [
+        column_sum(grad_queries),
+        column_sum(grad_values),
+        column_sum(grad_branch),
+        column_sum(grad_pre),
+        column_sum(upstream_low),
+        grad_first_gain,
+        grad_first_shift,
+        grad_second_gain,
+        grad_second_shift,
+    ]
+    widths = [item.shape[0] // count for item in small]
+    packed = jnp.concatenate(
+        [item.astype(jnp.bfloat16).astype(jnp.float32).reshape(count, -1) for item in small],
+        axis=1,
+    )
+    owned = reduce_small(packed)
+    pieces = []
+    start = 0
+    for width in widths:
+        pieces.append(owned[start : start + width])
+        start += width
     return (
         outputs,
         grad_inputs,
-        attention_total[0],
-        attention_total[1],
-        attention_total[2],
-        attention_total[3],
-        network_total[0],
-        network_total[1],
-        attention_total[4],
-        attention_total[5],
-        attention_total[6],
-        network_total[2],
-        network_total[3],
-        attention_total[7],
-        attention_total[8],
-        network_total[4],
-        network_total[5],
+        second_pair[0],
+        second_pair[1],
+        first_pair[1],
+        first_pair[0],
+        up_total,
+        down_total,
+        *pieces,
     )
 
 

time: 1180 us -> 781 us (0.66)
  blocking collectives: 597 us -> 15.1 us
  waiting for transfers between devices: 302 us -> 406 us
  other arithmetic: 21 us -> 54 us
  starting transfers between devices: 1.26 us -> 34.2 us
  local copies, waits for them, and re-layouts: 8.19 us -> 38.7 us
  matrix products: 225 us -> 213 us
    psum x1 -> x0, blocking collectives: 569 us -> none  [shards(): lax.psum((attention_owned[0], attention_owned[1], attention_owned[2], att...]
    ppermute x0 -> x33, waiting for transfers between devices: none -> 260 us  [swap(): return lax.ppermute(value, axis, [(i, i ^ bit) for i in range(size)])]
    reduce_scatter x6 -> x0, waiting for transfers between devices: 154 us -> none  [the longest x1 84.8 us: shards(): lax.psum_scatter(grad_down_term.astype(jnp.bfloat16), 'shard', scatter_di...]
    ppermute x0 -> x33, starting transfers between devices: none -> 34 us  [swap(): return lax.ppermute(value, axis, [(i, i ^ bit) for i in range(size)])]
    convert_element_type x5 -> x24, other arithmetic: 0.41 us -> 24 us  [the longest x16 17.1 us: halve(): (keep.astype(jnp.float32) + got.astype(jnp.float32)).astype(value.dtype)]
    another operation x0 -> x1, local copies, waits for them, and re-layouts: none -> 13.9 us  [reduce_owned(): term = term.reshape((2,) * len(bits) + trailing)]
    dynamic_slice x0 -> x14, local copies, waits for them, and re-layouts: none -> 12.8 us  [halve(): give = lax.dynamic_slice_in_dim(value, (1 - mine) * half, half, dim)]
    unnamed x2 -> x1, blocking collectives: 27.8 us -> 15.1 us
  transfers between devices with their start and end apart: 12 -> 39, of which waited for: 7 -> 25; matrix products, arithmetic and copies ran while one was open for 19% -> 23% of each run, Pallas kernels for 0% -> 0%
where the time goes in v1:
time: 781 us; the launch traced here: 778 us
  waiting for transfers between devices  406 us (52%)
  matrix products  213 us (27%)
  other arithmetic  54 us (7%)
  local copies, waits for them, and re-layouts  38.7 us (5%)
  starting transfers between devices  34.2 us (4%)
  between operations  16.9 us (2%)
  blocking collectives  15.1 us (2%)
    ppermute x33, waiting for transfers between devices, swap(): return lax.ppermute(value, axis, [(i, i ^ bit) for i in range(size)])  260 us
    all_gather x1, waiting for transfers between devices, shards(): lax.all_gather(up_weight, 'shard', axis=0, tiled=True)  57.2 us
    all_gather x1, waiting for transfers between devices, shards(): lax.all_gather(down_weight, 'shard', axis=0, tiled=True)  36.9 us
    ppermute x33, starting transfers between devices, swap(): return lax.ppermute(value, axis, [(i, i ^ bit) for i in range(size)])  34 us
    dot_general x6, matrix products, inner(): lax.dot_general(left, right, (((1,), (1,)), ((), ())), preferred_element_...  32.9 us
    dot_general x1, matrix products, shards(): jnp.dot(normed_two, full_up, preferred_element_type=jnp.float32) + up_shift  32.1 us
    dot_general x6, matrix products, outer(): lax.dot_general(left, right, (((0,), (0,)), ((), ())), preferred_element_...  31.8 us
    dot_general x1, matrix products, block(): jnp.einsum('hqk,khd->qhd', grad_scores, key_heads, preferred_element_type...  25.3 us
  transfers between devices with their start and end apart: 39, of which 25 were waited for; matrix products, arithmetic and copies ran while one was open for 23% of the time, Pallas kernels for 0%

profile of v1, /device:TPU:0, one launch (start us, length us, event | category | flops | bytes accessed | tf_op | source)
XLA Modules:
  0.0 777.5 jit_solution(8448892967417105160)
XLA Ops:
  16.4 15.1 %all-reduce.9 = (bf16[1088]{0:T(1024)(128)(2,1)S(1)}, bf16[1088]{0:T(1024)(128)(2,1)S(1)}, bf16[1088]{0:T(1024)(128)(2,1)S(1)}, bf16[1088]{0:T(1024)(128)(2,1)S(...) all-reduce(bf16[1088]{0:T(1024)(128)(2,1)S(1)} %dynamic-update-slic, ...), channel_id=1, replica_groups=mesh['shard'=4,'rep'=8] {'shard'}, use_global_device_ids=true, to_apply=%add.2 | all-reduce | flops 13056 | bytes 52224
  38.1 3.6 convolution_convert_fusion.7
  41.7 22.9 %all-gather.9.cloned.1.call-done = bf16[1088,1088]{1,0:T(8,128)(2,1)} async-done(((bf16[272,1088]{1,0:T(8,128)(2,1)}), bf16[1088,1088]{1,0:T(8,128)(2,1)}) %all-gather.9.cloned.1.call-update) | async-done | bytes 2367504 | tf_op jit(solution)/shard_map/all_gather | solution.py:217
  64.6 3.6 fusion.31
  68.2 22.8 %all-gather.7.cloned.1.call-done = bf16[1088,1088]{1,0:T(8,128)(2,1)} async-done(((bf16[272,1088]{1,0:T(8,128)(2,1)}), bf16[1088,1088]{1,0:T(8,128)(2,1)}) %all-gather.7.cloned.1.call-update) | async-done | bytes 2367504 | tf_op jit(solution)/shard_map/all_gather | solution.py:219
  91.1 4.7 fusion.30
  95.8 8.1 %fusion.87 = (f32[17,512]{1,0:T(8,128)S(1)}, f32[17,512,512]{1,2,0:T(8,128)}) fusion(bf16[512,17,64]{0,2,1:T(8,128)(2,1)S(1)} %bitcast.117, bf16[512,17,64]{0,2,1:T(8,128)(2,1)S(1)} %bitcast.115, pred[512,512]{0,1:T(8,128)(4,1)S(1)} %copy-done.19), kind=kOutput, calls=%fused_computation.199 | convolution fusion | flops 583785984 | bytes 20350976 | tf_op jit(solution)/shard_map/while/body/eval_jaxpr/qhd,khd->hqk/dot_general | solution.py:49
  103.9 9.0 %fusion.2 = f32[17,512]{1,0:T(8,128)S(1)} fusion(f32[17,512,512]{1,2,0:T(8,128)} %get-tuple-element.120, f32[17,512]{1,0:T(8,128)S(1)} %get-tuple-element.119), kind=kLoop, calls=%fused_computation.10 | loop fusion | flops 8904192 | bytes 17895424 | tf_op jit(solution)/shard_map/while/body/eval_jaxpr/reduce_sum | solution.py:67
  112.9 9.1 %fusion.47 = bf16[17,64,512]{2,1,0:T(8,128)(2,1)} fusion(bf16[512,17,64]{0,2,1:T(8,128)(2,1)S(1)} %bitcast.119, f32[17,512,512]{1,2,0:T(8,128)} %get-tuple-element.120, f32[17,512]{1,0:T(8,128)S(1)} %fusion.2, f32[17,512]{1,0:T(8,128)S(1)} %get-tuple-element.119), kind=kOutput, calls=%fused_computation.102 | convolution fusion | flops 584351744 | bytes 20123648 | tf_op jit(solution)/shard_map/while/body/eval_jaxpr/hqk,khd->qhd/dot_general | solution.py:69
  122.0 3.8 fusion.88
  126.1 57.2 %all-gather.15.cloned.1.call-done = bf16[1088,4352]{1,0:T(8,128)(2,1)} async-done(((bf16[272,4352]{1,0:T(8,128)(2,1)}), bf16[1088,4352]{1,0:T(8,128)(2,1)}) %all-gather.15.cloned.1.call-update) | async-done | bytes 9469968 | tf_op jit(solution)/shard_map/all_gather | solution.py:251
  183.3 32.1 %multiply_convert_fusion.1 = (bf16[512,4352]{1,0:T(8,128)(2,1)}, f32[512,4352]{1,0:T(8,128)}, f32[512,4352]{1,0:T(8,128)}) fusion(f32[4352]{0:T(1024)S(1)} %convert_element_type.446, bf16[1088,4352]{1,0:T(8,128)(2,1)} %all-gather.15.cloned.1.call-done, f32[512,1088]{0,1:T(8,128)S(1)} %get-tuple-element.122, f32[1088]{0:T(1024)S(1)} %convert_element_type.444, ...), kind=kOutput, calls=%fused_computation.20 | convolution fusion | flops 4998463488 | bytes 34010624 | tf_op jit(solution)/shard_map/dot_general | solution.py:264
  215.4 36.9 %all-gather.17.cloned.1.call-done = bf16[4352,1088]{1,0:T(8,128)(2,1)} async-done(((bf16[1088,1088]{1,0:T(8,128)(2,1)}), bf16[4352,1088]{1,0:T(8,128)(2,1)}) %all-gather.17.cloned.1.call-update) | async-done | bytes 9469968 | tf_op jit(solution)/shard_map/all_gather | solution.py:252
  252.3 15.2 %fusion.93 = (bf16[4352]{0:T(1024)(128)(2,1)S(1)}, bf16[512,4352]{1,0:T(8,128)(2,1)}) fusion(f32[512,4352]{1,0:T(8,128)} %get-tuple-element.97, bf16[4352,1088]{1,0:T(8,128)(2,1)} %all-gather.17.cloned.1.call-done, bf16[512,1088]{0,1:T(8,128)(2,1)} %param.35, f32[512]{0:T(512)S(1)} %fusion.68, f32[512,4352]{1,0:T(8,128)} %get-tuple-element.123, ...), kind=kOutput, calls=%fused_computation.203 | convolution fusion | flops 4885934080 | bytes 32894464 | tf_op jit(solution)/shard_map/dot_general | solution.py:37
  267.5 10.3 %convolution_convert_fusion.1 = bf16[1088,4352]{1,0:T(8,128)(2,1)} fusion(bf16[512,4352]{1,0:T(8,128)(2,1)} %get-tuple-element.131, f32[512,1088]{0,1:T(8,128)S(1)} %get-tuple-element.122, f32[1088]{0:T(1024)S(1)} %convert_element_type.444, f32[1088]{0:T(1024)S(1)} %convert_element_type.443, f32[512]{0:T(512)S(1)} %fusion.70, f32[512]{0:T(512)S(1)} %broadcast_multiply_fusion), kind=kOutput, calls=%fused_computation.2 | convolution fusion | flops 4856135680 | bytes 16167424 | tf_op jit(solution)/shard_map/dot_general | solution.py:31
  277.8 9.7 %multiply_reduce_fusion.1 = (bf16[1088]{0:T(1024)(128)(2,1)S(1)}, f32[512]{0:T(512)S(1)}, bf16[1088]{0:T(1024)(128)(2,1)S(1)}, f32[512,1088]{0,1:T(8,128)S(1)}) fusion(f32[512,1088]{0,1:T(8,128)S(1)} %get-tuple-element.122, f32[512]{0:T(512)S(1)} %fusion.70, f32[512]{0:T(512)S(1)} %broadcast_multiply_fusion, f32[1088]{0:T(1024)S(1)} %convert_element_type.443, ...), kind=kOutput, calls=%fused_computation.94 | convolution fusion | flops 4853069312 | bytes 18397696 | tf_op jit(solution)/shard_map/dot_general | solution.py:37
  295.8 8.6 %fusion.94 = f32[17,512,512]{1,2,0:T(8,128)} fusion(bf16[512,17,64]{0,2,1:T(8,128)(2,1)S(1)} %bitcast.113, bf16[512,17,64]{0,2,1:T(8,128)(2,1)S(1)} %bitcast.120), kind=kOutput, calls=%fused_computation.204 | convolution fusion | flops 570425344 | bytes 20054016 | tf_op jit(solution)/shard_map/while/body/eval_jaxpr/qhd,khd->hqk/dot_general | solution.py:97
  304.4 9.9 %fusion.92 = (bf16[17,64]{1,0:T(8,128)(2,1)S(1)}, bf16[17,64,512]{2,1,0:T(8,128)(2,1)}) fusion(bf16[512,17,64]{0,2,1:T(8,128)(2,1)S(1)} %bitcast.114, f32[17,512,512]{1,2,0:T(8,128)} %get-tuple-element.120, f32[17,512]{1,0:T(8,128)S(1)} %log_add_fusion), kind=kOutput, calls=%fused_computation.202 | convolution fusion | flops 580451264 | bytes 20091008 | tf_op jit(solution)/shard_map/while/body/eval_jaxpr/hqk,qhd->khd/dot_general | solution.py:91
  314.3 25.3 %fusion.54 = bf16[17,64,512]{2,1,0:T(8,128)(2,1)} fusion(bf16[512,17,64]{0,2,1:T(8,128)(2,1)} %bitcast.118, f32[17,512,512]{1,2,0:T(8,128)} %fusion.94, f32[17,512,512]{1,2,0:T(8,128)} %get-tuple-element.120, f32[17,512]{1,0:T(8,128)S(1)} %log_add_fusion), kind=kOutput, calls=%fused_computation.105 | convolution fusion | flops 602186752 | bytes 37914624 | tf_op jit(solution)/shard_map/while/body/eval_jaxpr/hqk,qhd->khd/dot_general | solution.py:105
  339.7 25.3 %fusion.89 = (bf16[17,64]{1,0:T(8,128)(2,1)S(1)}, bf16[17,64,512]{2,1,0:T(8,128)(2,1)}) fusion(bf16[512,17,64]{0,2,1:T(8,128)(2,1)} %bitcast.116, f32[17,512,512]{1,2,0:T(8,128)} %fusion.94, f32[17,512,512]{1,2,0:T(8,128)} %get-tuple-element.120, f32[17,512]{1,0:T(8,128)S(1)} %log_add_fusion), kind=kOutput, calls=%fused_computation.201 | convolution fusion | flops 602742720 | bytes 37916800 | tf_op jit(solution)/shard_map/while/body/eval_jaxpr/hqk,khd->qhd/dot_general | solution.py:102
  371.6 5.1 constant_dynamic-slice_fusion.5
  377.0 7.4 convolution_convert_fusion
  384.4 13.9 %copy.59 = bf16[4352,1088]{1,0:T(8,128)(2,1)} copy(bf16[4352,1088]{0,1:T(8,128)(2,1)} %convolution_convert_fusion) | data formatting | bytes 18939904 | tf_op jit(solution)/shard_map/reshape;reshape | solution.py:166
  398.3 5.1 constant_dynamic-slice_fusion.2
  403.7 4.6 convolution_convert_fusion.4
  422.2 3.5 fusion.37
  426.4 13.6 %fusion.32 = bf16[512,1088]{0,1:T(8,128)(2,1)} fusion(f32[512,1088]{0,1:T(8,128)S(1)} %copy-done.9, bf16[512,4352]{1,0:T(8,128)(2,1)} %get-tuple-element.96, bf16[4352,1088]{1,0:T(8,128)(2,1)} %all-gather.17.cloned.1.call-done, f32[512]{0:T(512)S(1)} %fusion.68, f32[1088]{0:T(1024)S(1)} %copy-done.28), kind=kOutput, calls=%fused_computation.74 | convolution fusion | flops 4850843648 | bytes 17275136 | tf_op jit(solution)/shard_map/dot_general | solution.py:266
  459.1 25.5 %collective-permute-done.8 = bf16[1,1,2,272,1088]{4,3,2,1,0:T(8,128)(2,1)S(1)} collective-permute-done((bf16[1,1,2,272,1088]{4,3,2,1,0:T(8,128)(2,1)S(1)}, bf16[1,1,2,272,1088]{4,3,2,1,0:T(8,128)(2,1)S(1)}, u32[]{:S(2)}, u32[]{:S(2)}) %collective-permute-start.8) | collective-permute-done | bytes 1183776 | tf_op jit(solution)/shard_map/ppermute | solution.py:127
  486.6 21.3 %collective-permute-done.1 = bf16[1,1,2,272,1088]{4,3,2,1,0:T(8,128)(2,1)S(1)} collective-permute-done((bf16[1,1,2,272,1088]{4,3,2,1,0:T(8,128)(2,1)S(1)}, bf16[1,1,2,272,1088]{4,3,2,1,0:T(8,128)(2,1)S(1)}, u32[]{:S(2)}, u32[]{:S(2)}) %collective-permute-start.1) | collective-permute-done | bytes 1183776 | tf_op jit(solution)/shard_map/ppermute | solution.py:127
  511.4 9.6 %collective-permute-done.2 = bf16[2,136,1088]{2,1,0:T(8,128)(2,1)S(1)} collective-permute-done((bf16[2,136,1088]{2,1,0:T(8,128)(2,1)S(1)}, bf16[2,136,1088]{2,1,0:T(8,128)(2,1)S(1)}, u32[]{:S(2)}, u32[]{:S(2)}) %collective-permute-start.2) | collective-permute-done | bytes 591904 | tf_op jit(solution)/shard_map/ppermute | solution.py:127
  522.9 10.0 %collective-permute-done.3 = bf16[1,136,1088]{2,1,0:T(8,128)(2,1)S(1)} collective-permute-done((bf16[1,136,1088]{2,1,0:T(8,128)(2,1)S(1)}, bf16[1,136,1088]{2,1,0:T(8,128)(2,1)S(1)}, u32[]{:S(2)}, u32[]{:S(2)}) %collective-permute-start.3) | collective-permute-done | bytes 295968 | tf_op jit(solution)/shard_map/ppermute | solution.py:127
  533.1 7.7 collective-permute-done.11
  541.4 5.2 add_convert_fusion.1
  549.5 4.2 collective-permute-start.15
  556.4 3.7 add_convert_fusion
  565.2 9.5 %collective-permute-done.13 = bf16[2,136,1088]{2,1,0:T(8,128)(2,1)S(1)} collective-permute-done((bf16[2,136,1088]{2,1,0:T(8,128)(2,1)S(1)}, bf16[2,136,1088]{2,1,0:T(8,128)(2,1)S(1)}, u32[]{:S(2)}, u32[]{:S(2)}) %collective-permute-start.13) | collective-permute-done | bytes 591904 | tf_op jit(solution)/shard_map/ppermute | solution.py:127
  574.9 7.2 collective-permute-done.6
  582.2 24.1 %collective-permute-done.15 = bf16[1,1,272,4352]{3,2,1,0:T(8,128)(2,1)} collective-permute-done((bf16[1,1,272,4352]{3,2,1,0:T(8,128)(2,1)}, bf16[1,1,272,4352]{3,2,1,0:T(8,128)(2,1)}, u32[]{:S(2)}, u32[]{:S(2)}) %collective-permute-start.15) | collective-permute-done | bytes 2367520 | tf_op jit(solution)/shard_map/ppermute | solution.py:127
  610.6 34.0 %collective-permute-done.22 = bf16[1,1,1088,1088]{3,2,1,0:T(8,128)(2,1)S(1)} collective-permute-done((bf16[1,1,1088,1088]{3,2,1,0:T(8,128)(2,1)S(1)}, bf16[1,1,1088,1088]{3,2,1,0:T(8,128)(2,1)S(1)}, u32[]{:S(2)}, u32[]{:S(2)}) %collective-permute-start.22) | collective-permute-done | bytes 2367520 | tf_op jit(solution)/shard_map/ppermute | solution.py:127
  648.9 13.5 %collective-permute-done.23 = bf16[544,1088]{1,0:T(8,128)(2,1)S(1)} collective-permute-done((bf16[544,1088]{1,0:T(8,128)(2,1)S(1)}, bf16[544,1088]{1,0:T(8,128)(2,1)S(1)}, u32[]{:S(2)}, u32[]{:S(2)}) %collective-permute-start.23) | collective-permute-done | bytes 1183776 | tf_op jit(solution)/shard_map/ppermute | solution.py:127
  664.2 4.3 collective-permute-done.17
  669.4 13.4 %collective-permute-done.24 = bf16[272,1088]{1,0:T(8,128)(2,1)S(1)} collective-permute-done((bf16[272,1088]{1,0:T(8,128)(2,1)S(1)}, bf16[272,1088]{1,0:T(8,128)(2,1)S(1)}, u32[]{:S(2)}, u32[]{:S(2)}) %collective-permute-start.24) | collective-permute-done | bytes 591904 | tf_op jit(solution)/shard_map/ppermute | solution.py:127
  683.0 21.7 %collective-permute-done.18 = bf16[136,2176]{1,0:T(8,128)(2,1)S(1)} collective-permute-done((bf16[136,2176]{1,0:T(8,128)(2,1)S(1)}, bf16[136,2176]{1,0:T(8,128)(2,1)S(1)}, u32[]{:S(2)}, u32[]{:S(2)}) %collective-permute-start.18) | collective-permute-done | bytes 591904 | tf_op jit(solution)/shard_map/ppermute | solution.py:127
  705.1 6.4 collective-permute-done.25
  711.8 12.4 %collective-permute-done.19 = bf16[136,2176]{1,0:T(8,128)(2,1)S(1)} collective-permute-done((bf16[136,2176]{1,0:T(8,128)(2,1)S(1)}, bf16[136,2176]{1,0:T(8,128)(2,1)S(1)}, u32[]{:S(2)}, u32[]{:S(2)}) %collective-permute-start.19) | collective-permute-done | bytes 591904 | tf_op jit(solution)/shard_map/ppermute | solution.py:127
  727.2 4.0 collective-permute-done.26
  731.9 21.5 %collective-permute-done.20 = bf16[136,4352]{1,0:T(8,128)(2,1)S(1)} collective-permute-done((bf16[136,4352]{1,0:T(8,128)(2,1)S(1)}, bf16[136,4352]{1,0:T(8,128)(2,1)S(1)}, u32[]{:S(2)}, u32[]{:S(2)}) %collective-permute-start.20) | collective-permute-done | bytes 1183776 | tf_op jit(solution)/shard_map/ppermute | solution.py:127
  756.3 11.0 %collective-permute-done.27 = bf16[544,1088]{1,0:T(8,128)(2,1)S(1)} collective-permute-done((bf16[544,1088]{1,0:T(8,128)(2,1)S(1)}, bf16[544,1088]{1,0:T(8,128)(2,1)S(1)}, u32[]{:S(2)}, u32[]{:S(2)}) %collective-permute-start.27) | collective-permute-done | bytes 1183776 | tf_op jit(solution)/shard_map/ppermute | solution.py:127
  (301 shorter events, 103.9 us)
Async XLA Ops:
  7.2 30.9 %all-gather.11.cloned.1.call-start = ((), (), s32[]{:S(2)}) async-start(), calls=%async_computation.2 | async-start | bytes 3133440 | tf_op jit(solution)/shard_map/all_gather | solution.py:218
  7.9 56.6 %all-gather.9.cloned.1.call-start = ((), (), s32[]{:S(2)}) async-start(), calls=%async_computation.1 | async-start | bytes 3133440 | tf_op jit(solution)/shard_map/all_gather | solution.py:217
  8.7 82.4 %all-gather.7.cloned.1.call-start = ((), (), s32[]{:S(2)}) async-start(), calls=%async_computation | async-start | bytes 3133440 | tf_op jit(solution)/shard_map/all_gather | solution.py:219
  9.4 112.6 %all-gather.13.cloned.1.call-start = ((), (), s32[]{:S(2)}) async-start(), calls=%async_computation.3 | async-start | bytes 3133440 | tf_op jit(solution)/shard_map/all_gather | solution.py:220
  10.1 173.2 %all-gather.15.cloned.1.call-start = ((), (), s32[]{:S(2)}) async-start(), calls=%async_computation.4 | async-start | bytes 11837440 | tf_op jit(solution)/shard_map/all_gather | solution.py:251
  10.7 241.6 %all-gather.17.cloned.1.call-start = ((), (), s32[]{:S(2)}) async-start(), calls=%async_computation.5 | async-start | bytes 12533760 | tf_op jit(solution)/shard_map/all_gather | solution.py:252
  31.5 59.6 %copy-start.20 = (f32[1088]{0:T(1024)}, f32[1088]{0:T(1024)S(1)}, u32[]{:S(2)}) copy-start(f32[1088]{0:T(1024)S(1)} %convert_element_type.429) | copy-start | bytes 13060
  31.5 59.6 %copy-start.29 = (f32[1088]{0:T(1024)}, f32[1088]{0:T(1024)S(1)}, u32[]{:S(2)}) copy-start(f32[1088]{0:T(1024)S(1)} %convert_element_type.430) | copy-start | bytes 13060
  33.2 57.9 %copy-start.22 = (f32[512]{0:T(512)}, f32[512]{0:T(512)S(1)}, u32[]{:S(2)}) copy-start(f32[512]{0:T(512)S(1)} %broadcast_multiply_fusion.1) | copy-start | bytes 6148
  34.2 56.9 %copy-start.24 = (f32[512]{0:T(512)}, f32[512]{0:T(512)S(1)}, u32[]{:S(2)}) copy-start(f32[512]{0:T(512)S(1)} %fusion.69) | copy-start | bytes 6148
  41.7 54.1 %copy-start.14 = (bf16[512,1088]{0,1:T(8,128)(2,1)}, bf16[512,1088]{0,1:T(8,128)(2,1)S(1)}, u32[]{:S(2)}) copy-start(bf16[512,1088]{0,1:T(8,128)(2,1)S(1)} %convolution_convert_fusion.7) | copy-start | bytes 3342340
  68.2 27.6 %copy-start.15 = (bf16[512,1088]{0,1:T(8,128)(2,1)}, bf16[512,1088]{0,1:T(8,128)(2,1)S(1)}, u32[]{:S(2)}) copy-start(bf16[512,1088]{0,1:T(8,128)(2,1)S(1)} %fusion.31) | copy-start | bytes 3342340
  125.8 152.0 %copy-start.8 = (f32[512,1088]{0,1:T(8,128)}, f32[512,1088]{0,1:T(8,128)S(1)}, u32[]{:S(2)}) copy-start(f32[512,1088]{0,1:T(8,128)S(1)} %get-tuple-element.122) | copy-start | bytes 6684676
  371.3 80.0 %collective-permute-start.7 = (bf16[2,1,2,272,1088]{4,3,2,1,0:T(8,128)(2,1)}, bf16[2,1,2,272,1088]{4,3,2,1,0:T(8,128)(2,1)}, u32[]{:S(2)}, u32[]{:S(2)}) collective-permute-start(bf16[2,1,2,272,1088]{4,3,2,1,0:T(8,128)(2,1)} %fusion.35), channel_id=1, source_target_pairs={{0,8},{8,0},{16,24},{24,16},{1,9},{9,1},{17,25},{25,17},{2,10},{10... | collective-permute-start | bytes 7102472 | tf_op jit(solution)/shard_map/ppermute | solution.py:127
  376.7 164.7 %collective-permute-start.14 = (bf16[2,1,272,4352]{3,2,1,0:T(8,128)(2,1)}, bf16[2,1,272,4352]{3,2,1,0:T(8,128)(2,1)}, u32[]{:S(2)}, u32[]{:S(2)}) collective-permute-start(bf16[2,1,272,4352]{3,2,1,0:T(8,128)(2,1)} %constant_dynamic-slice_fusion.5), channel_id=1, source_target_pairs={{0,8},{8,0},{16,24},{24,16},{1,9},{9,1},{17,25},{25,17},{2,10},{10... | collective-permute-start | bytes 14204936 | tf_op jit(solution)/shard_map/ppermute | solution.py:127
  403.4 153.0 %collective-permute-start.21 = (bf16[2,1,1088,1088]{3,2,1,0:T(8,128)(2,1)}, bf16[2,1,1088,1088]{3,2,1,0:T(8,128)(2,1)}, u32[]{:S(2)}, u32[]{:S(2)}) collective-permute-start(bf16[2,1,1088,1088]{3,2,1,0:T(8,128)(2,1)} %constant_dynamic-slice_fusion.2), channel_id=1, source_target_pairs={{0,8},{8,0},{16,24},{24,16},{1,9},{9,1},{17,25},{25,17},{2,10},{10... | collective-permute-start | bytes 14204936 | tf_op jit(solution)/shard_map/ppermute | solution.py:127
  421.8 4.1 collective-permute-start.28
  425.7 29.6 %collective-permute-start = (bf16[2,1,2,272,1088]{4,3,2,1,0:T(8,128)(2,1)}, bf16[2,1,2,272,1088]{4,3,2,1,0:T(8,128)(2,1)S(1)}, u32[]{:S(2)}, u32[]{:S(2)}) collective-permute-start(bf16[2,1,2,272,1088]{4,3,2,1,0:T(8,128)(2,1)} %fusion.37), channel_id=1, source_target_pairs={{0,8},{8,0},{16,24},{24,16},{1,9},{9,1},{17,25},{25,17},{2,10},{10... | collective-permute-start | bytes 7102472 | tf_op jit(solution)/shard_map/ppermute | solution.py:127
  426.0 14.0 %collective-permute-start.29 = (f32[4,3264]{1,0:T(4,128)S(1)}, f32[4,3264]{1,0:T(4,128)S(1)}, u32[]{:S(2)}, u32[]{:S(2)}) collective-permute-start(f32[4,3264]{1,0:T(4,128)S(1)} %convert_add_fusion.4), channel_id=1, source_target_pairs={{0,16},{8,24},{16,0},{24,8},{1,17},{9,25},{17,1},{25,9},{2,18},{10... | collective-permute-start | bytes 156680 | tf_op jit(solution)/shard_map/ppermute | solution.py:127
  440.1 4.2 collective-permute-start.30
  444.3 4.2 collective-permute-start.31
  448.5 9.2 %collective-permute-start.32 = (f32[4,3264]{1,0:T(4,128)S(1)}, f32[4,3264]{1,0:T(4,128)S(1)}, u32[]{:S(2)}, u32[]{:S(2)}) collective-permute-start(f32[4,3264]{1,0:T(4,128)S(1)} %add.384), channel_id=1, source_target_pairs={{0,4},{1,5},{2,6},{3,7},{4,0},{5,1},{6,2},{7,3},{8,12},{9,13},{10,... | collective-permute-start | bytes 156680 | tf_op jit(solution)/shard_map/ppermute | solution.py:127
  454.1 30.6 %collective-permute-start.8 = (bf16[1,1,2,272,1088]{4,3,2,1,0:T(8,128)(2,1)S(1)}, bf16[1,1,2,272,1088]{4,3,2,1,0:T(8,128)(2,1)S(1)}, u32[]{:S(2)}, u32[]{:S(2)}) collective-permute-start(bf16[1,1,2,272,1088]{4,3,2,1,0:T(8,128)(2,1)S(1)} %constant_dynamic-slice_fusion.7), channel_id=1, source_target_pairs={{0,16},{8,24},{16,0},{24,8},{1,17},{9,25},{17,1},{25,9},{2,18},{10... | collective-permute-start | bytes 3551240 | tf_op jit(solution)/shard_map/ppermute | solution.py:127
  456.5 51.4 %collective-permute-start.1 = (bf16[1,1,2,272,1088]{4,3,2,1,0:T(8,128)(2,1)S(1)}, bf16[1,1,2,272,1088]{4,3,2,1,0:T(8,128)(2,1)S(1)}, u32[]{:S(2)}, u32[]{:S(2)}) collective-permute-start(bf16[1,1,2,272,1088]{4,3,2,1,0:T(8,128)(2,1)S(1)} %constant_dynamic-slice_fusion.9), channel_id=1, source_target_pairs={{0,16},{8,24},{16,0},{24,8},{1,17},{9,25},{17,1},{25,9},{2,18},{10... | collective-permute-start | bytes 3551240 | tf_op jit(solution)/shard_map/ppermute | solution.py:127
  485.0 24.8 %collective-permute-start.9 = (bf16[2,136,1088]{2,1,0:T(8,128)(2,1)S(1)}, bf16[2,136,1088]{2,1,0:T(8,128)(2,1)S(1)}, u32[]{:S(2)}, u32[]{:S(2)}) collective-permute-start(bf16[2,136,1088]{2,1,0:T(8,128)(2,1)S(1)} %dynamic-slice_bitcast_fusion.2), channel_id=1, source_target_pairs={{0,1},{1,0},{2,3},{3,2},{4,5},{5,4},{6,7},{7,6},{8,9},{9,8},{10,11... | collective-permute-start | bytes 1775624 | tf_op jit(solution)/shard_map/ppermute | solution.py:127
  508.3 12.6 %collective-permute-start.2 = (bf16[2,136,1088]{2,1,0:T(8,128)(2,1)S(1)}, bf16[2,136,1088]{2,1,0:T(8,128)(2,1)S(1)}, u32[]{:S(2)}, u32[]{:S(2)}) collective-permute-start(bf16[2,136,1088]{2,1,0:T(8,128)(2,1)S(1)} %dynamic-slice_bitcast_fusion.3), channel_id=1, source_target_pairs={{0,1},{1,0},{2,3},{3,2},{4,5},{5,4},{6,7},{7,6},{8,9},{9,8},{10,11... | collective-permute-start | bytes 1775624 | tf_op jit(solution)/shard_map/ppermute | solution.py:127
  510.0 12.2 %collective-permute-start.10 = (bf16[1,136,1088]{2,1,0:T(8,128)(2,1)S(1)}, bf16[1,136,1088]{2,1,0:T(8,128)(2,1)S(1)}, u32[]{:S(2)}, u32[]{:S(2)}) collective-permute-start(bf16[1,136,1088]{2,1,0:T(8,128)(2,1)S(1)} %constant_dynamic-slice_fusion.6), channel_id=1, source_target_pairs={{0,2},{1,3},{2,0},{3,1},{4,6},{5,7},{6,4},{7,5},{8,10},{9,11},{10,... | collective-permute-start | bytes 887816 | tf_op jit(solution)/shard_map/ppermute | solution.py:127
  521.1 11.8 %collective-permute-start.3 = (bf16[1,136,1088]{2,1,0:T(8,128)(2,1)S(1)}, bf16[1,136,1088]{2,1,0:T(8,128)(2,1)S(1)}, u32[]{:S(2)}, u32[]{:S(2)}) collective-permute-start(bf16[1,136,1088]{2,1,0:T(8,128)(2,1)S(1)} %constant_dynamic-slice_fusion.8), channel_id=1, source_target_pairs={{0,2},{1,3},{2,0},{3,1},{4,6},{5,7},{6,4},{7,5},{8,10},{9,11},{10,... | collective-permute-start | bytes 887816 | tf_op jit(solution)/shard_map/ppermute | solution.py:127
  522.3 18.4 %collective-permute-start.11 = (bf16[1,136,1088]{2,1,0:T(8,128)(2,1)S(1)}, bf16[1,136,1088]{2,1,0:T(8,128)(2,1)S(1)}, u32[]{:S(2)}, u32[]{:S(2)}) collective-permute-start(bf16[1,136,1088]{2,1,0:T(8,128)(2,1)S(1)} %add_convert_fusion.16), channel_id=1, source_target_pairs={{0,4},{1,5},{2,6},{3,7},{4,0},{5,1},{6,2},{7,3},{8,12},{9,13},{10,... | collective-permute-start | bytes 887816 | tf_op jit(solution)/shard_map/ppermute | solution.py:127
  533.0 20.7 %collective-permute-start.4 = (bf16[1,136,1088]{2,1,0:T(8,128)(2,1)S(1)}, bf16[1,136,1088]{2,1,0:T(8,128)(2,1)S(1)}, u32[]{:S(2)}, u32[]{:S(2)}) collective-permute-start(bf16[1,136,1088]{2,1,0:T(8,128)(2,1)S(1)} %add_convert_fusion.18), channel_id=1, source_target_pairs={{0,4},{1,5},{2,6},{3,7},{4,0},{5,1},{6,2},{7,3},{8,12},{9,13},{10,... | collective-permute-start | bytes 887816 | tf_op jit(solution)/shard_map/ppermute | solution.py:127
  540.8 19.3 %collective-permute-start.12 = (bf16[1,136,1088]{2,1,0:T(8,128)(2,1)S(1)}, bf16[1,136,1088]{2,1,0:T(8,128)(2,1)}, u32[]{:S(2)}, u32[]{:S(2)}) collective-permute-start(bf16[1,136,1088]{2,1,0:T(8,128)(2,1)S(1)} %add_convert_fusion.15), channel_id=1, source_target_pairs={{0,2},{1,3},{2,0},{3,1},{4,6},{5,7},{6,4},{7,5},{8,10},{9,11},{10,... | collective-permute-start | bytes 887816 | tf_op jit(solution)/shard_map/ppermute | solution.py:127
  549.5 56.9 %collective-permute-start.15 = (bf16[1,1,272,4352]{3,2,1,0:T(8,128)(2,1)}, bf16[1,1,272,4352]{3,2,1,0:T(8,128)(2,1)}, u32[]{:S(2)}, u32[]{:S(2)}) collective-permute-start(bf16[1,1,272,4352]{3,2,1,0:T(8,128)(2,1)} %constant_dynamic-slice_fusion.4), channel_id=1, source_target_pairs={{0,16},{8,24},{16,0},{24,8},{1,17},{9,25},{17,1},{25,9},{2,18},{10... | collective-permute-start | bytes 7102472 | tf_op jit(solution)/shard_map/ppermute | solution.py:127
  554.5 8.3 %collective-permute-start.5 = (bf16[1,136,1088]{2,1,0:T(8,128)(2,1)}, bf16[1,136,1088]{2,1,0:T(8,128)(2,1)}, u32[]{:S(2)}, u32[]{:S(2)}) collective-permute-start(bf16[1,136,1088]{2,1,0:T(8,128)(2,1)} %add_convert_fusion.17), channel_id=1, source_target_pairs={{0,2},{1,3},{2,0},{3,1},{4,6},{5,7},{6,4},{7,5},{8,10},{9,11},{10,... | collective-permute-start | bytes 887816 | tf_op jit(solution)/shard_map/ppermute | solution.py:127
  561.3 13.4 %collective-permute-start.13 = (bf16[2,136,1088]{2,1,0:T(8,128)(2,1)S(1)}, bf16[2,136,1088]{2,1,0:T(8,128)(2,1)S(1)}, u32[]{:S(2)}, u32[]{:S(2)}) collective-permute-start(bf16[2,136,1088]{2,1,0:T(8,128)(2,1)S(1)} %pad_maximum_fusion.3), channel_id=1, source_target_pairs={{0,1},{1,0},{2,3},{3,2},{4,5},{5,4},{6,7},{7,6},{8,9},{9,8},{10,11... | collective-permute-start | bytes 1775624 | tf_op jit(solution)/shard_map/ppermute | solution.py:127
  564.0 42.4 %slice-start.3 = ((s8[4734976]{0:T(1024)(128)(4,1)}), s8[4194304]{0:T(1024)(128)(4,1)S(1)}, s32[]{:S(2)}) async-start(s8[4734976]{0:T(1024)(128)(4,1)} %bitcast.101), calls=%async_computation.9 | async-start | bytes 8388608
  564.1 42.3 %slice-start.4 = ((s8[4734976]{0:T(1024)(128)(4,1)}), s8[540672]{0:T(1024)(128)(4,1)S(1)}, s32[]{:S(2)}) async-start(s8[4734976]{0:T(1024)(128)(4,1)} %bitcast.101), calls=%async_computation.10 | async-start | bytes 1081344
  564.1 18.0 %collective-permute-start.6 = (bf16[2,136,1088]{2,1,0:T(8,128)(2,1)S(1)}, bf16[2,136,1088]{2,1,0:T(8,128)(2,1)S(1)}, u32[]{:S(2)}, u32[]{:S(2)}) collective-permute-start(bf16[2,136,1088]{2,1,0:T(8,128)(2,1)S(1)} %pad_maximum_fusion.2), channel_id=1, source_target_pairs={{0,1},{1,0},{2,3},{3,2},{4,5},{5,4},{6,7},{7,6},{8,9},{9,8},{10,11... | collective-permute-start | bytes 1775624 | tf_op jit(solution)/shard_map/ppermute | solution.py:127
  564.8 79.7 %collective-permute-start.22 = (bf16[1,1,1088,1088]{3,2,1,0:T(8,128)(2,1)S(1)}, bf16[1,1,1088,1088]{3,2,1,0:T(8,128)(2,1)S(1)}, u32[]{:S(2)}, u32[]{:S(2)}) collective-permute-start(bf16[1,1,1088,1088]{3,2,1,0:T(8,128)(2,1)S(1)} %constant_dynamic-slice_fusion.1), channel_id=1, source_target_pairs={{0,16},{8,24},{16,0},{24,8},{1,17},{9,25},{17,1},{25,9},{2,18},{10... | collective-permute-start | bytes 7102472 | tf_op jit(solution)/shard_map/ppermute | solution.py:127
  608.7 37.4 %collective-permute-start.16 = (bf16[136,4352]{1,0:T(8,128)(2,1)S(1)}, bf16[136,4352]{1,0:T(8,128)(2,1)S(1)}, u32[]{:S(2)}, u32[]{:S(2)}) collective-permute-start(bf16[136,4352]{1,0:T(8,128)(2,1)S(1)} %dynamic-slice_bitcast_fusion.1), channel_id=1, source_target_pairs={{0,1},{1,0},{2,3},{3,2},{4,5},{5,4},{6,7},{7,6},{8,9},{9,8},{10,11... | collective-permute-start | bytes 3551240 | tf_op jit(solution)/shard_map/ppermute | solution.py:127
  645.4 17.1 %collective-permute-start.23 = (bf16[544,1088]{1,0:T(8,128)(2,1)S(1)}, bf16[544,1088]{1,0:T(8,128)(2,1)S(1)}, u32[]{:S(2)}, u32[]{:S(2)}) collective-permute-start(bf16[544,1088]{1,0:T(8,128)(2,1)S(1)} %dynamic-slice_bitcast_fusion), channel_id=1, source_target_pairs={{0,1},{1,0},{2,3},{3,2},{4,5},{5,4},{6,7},{7,6},{8,9},{9,8},{10,11... | collective-permute-start | bytes 3551240 | tf_op jit(solution)/shard_map/ppermute | solution.py:127
  646.5 22.0 %collective-permute-start.17 = (bf16[136,2176]{1,0:T(8,128)(2,1)S(1)}, bf16[136,2176]{1,0:T(8,128)(2,1)S(1)}, u32[]{:S(2)}, u32[]{:S(2)}) collective-permute-start(bf16[136,2176]{1,0:T(8,128)(2,1)S(1)} %constant_dynamic-slice_fusion.3), channel_id=1, source_target_pairs={{0,2},{1,3},{2,0},{3,1},{4,6},{5,7},{6,4},{7,5},{8,10},{9,11},{10,... | collective-permute-start | bytes 1775624 | tf_op jit(solution)/shard_map/ppermute | solution.py:127
  662.8 19.9 %collective-permute-start.24 = (bf16[272,1088]{1,0:T(8,128)(2,1)S(1)}, bf16[272,1088]{1,0:T(8,128)(2,1)S(1)}, u32[]{:S(2)}, u32[]{:S(2)}) collective-permute-start(bf16[272,1088]{1,0:T(8,128)(2,1)S(1)} %constant_dynamic-slice_fusion), channel_id=1, source_target_pairs={{0,2},{1,3},{2,0},{3,1},{4,6},{5,7},{6,4},{7,5},{8,10},{9,11},{10,... | collective-permute-start | bytes 1775624 | tf_op jit(solution)/shard_map/ppermute | solution.py:127
  668.6 36.2 %collective-permute-start.18 = (bf16[136,2176]{1,0:T(8,128)(2,1)S(1)}, bf16[136,2176]{1,0:T(8,128)(2,1)S(1)}, u32[]{:S(2)}, u32[]{:S(2)}) collective-permute-start(bf16[136,2176]{1,0:T(8,128)(2,1)S(1)} %add_convert_fusion.14), channel_id=1, source_target_pairs={{0,4},{1,5},{2,6},{3,7},{4,0},{5,1},{6,2},{7,3},{8,12},{9,13},{10,... | collective-permute-start | bytes 1775624 | tf_op jit(solution)/shard_map/ppermute | solution.py:127
  682.9 28.6 %collective-permute-start.25 = (bf16[272,1088]{1,0:T(8,128)(2,1)S(1)}, bf16[272,1088]{1,0:T(8,128)(2,1)S(1)}, u32[]{:S(2)}, u32[]{:S(2)}) collective-permute-start(bf16[272,1088]{1,0:T(8,128)(2,1)S(1)} %add_convert_fusion.12), channel_id=1, source_target_pairs={{0,4},{1,5},{2,6},{3,7},{4,0},{5,1},{6,2},{7,3},{8,12},{9,13},{10,... | collective-permute-start | bytes 1775624 | tf_op jit(solution)/shard_map/ppermute | solution.py:127
  704.9 19.4 %collective-permute-start.19 = (bf16[136,2176]{1,0:T(8,128)(2,1)S(1)}, bf16[136,2176]{1,0:T(8,128)(2,1)S(1)}, u32[]{:S(2)}, u32[]{:S(2)}) collective-permute-start(bf16[136,2176]{1,0:T(8,128)(2,1)S(1)} %add_convert_fusion.13), channel_id=1, source_target_pairs={{0,2},{1,3},{2,0},{3,1},{4,6},{5,7},{6,4},{7,5},{8,10},{9,11},{10,... | collective-permute-start | bytes 1775624 | tf_op jit(solution)/shard_map/ppermute | solution.py:127
  711.7 19.5 %collective-permute-start.26 = (bf16[272,1088]{1,0:T(8,128)(2,1)S(1)}, bf16[272,1088]{1,0:T(8,128)(2,1)S(1)}, u32[]{:S(2)}, u32[]{:S(2)}) collective-permute-start(bf16[272,1088]{1,0:T(8,128)(2,1)S(1)} %add_convert_fusion.11), channel_id=1, source_target_pairs={{0,2},{1,3},{2,0},{3,1},{4,6},{5,7},{6,4},{7,5},{8,10},{9,11},{10,... | collective-permute-start | bytes 1775624 | tf_op jit(solution)/shard_map/ppermute | solution.py:127
  724.4 29.0 %collective-permute-start.20 = (bf16[136,4352]{1,0:T(8,128)(2,1)S(1)}, bf16[136,4352]{1,0:T(8,128)(2,1)S(1)}, u32[]{:S(2)}, u32[]{:S(2)}) collective-permute-start(bf16[136,4352]{1,0:T(8,128)(2,1)S(1)} %pad_maximum_fusion.1), channel_id=1, source_target_pairs={{0,1},{1,0},{2,3},{3,2},{4,5},{5,4},{6,7},{7,6},{8,9},{9,8},{10,11... | collective-permute-start | bytes 3551240 | tf_op jit(solution)/shard_map/ppermute | solution.py:127
  731.5 35.9 %collective-permute-start.27 = (bf16[544,1088]{1,0:T(8,128)(2,1)S(1)}, bf16[544,1088]{1,0:T(8,128)(2,1)S(1)}, u32[]{:S(2)}, u32[]{:S(2)}) collective-permute-start(bf16[544,1088]{1,0:T(8,128)(2,1)S(1)} %pad_maximum_fusion), channel_id=1, source_target_pairs={{0,1},{1,0},{2,3},{3,2},{4,5},{5,4},{6,7},{7,6},{8,9},{9,8},{10,11... | collective-permute-start | bytes 3551240 | tf_op jit(solution)/shard_map/ppermute | solution.py:127
  (48 other events, 378.6 us)
Sparse Core Ops, SparseCore 0:
  9.6 28.4 all-gather.10
  39.6 24.9 all-gather.8
  66.1 24.8 all-gather.6
  92.5 24.8 all-gather.12
  118.8 64.4 all-gather.14
  184.7 67.5 all-gather.16

commit v2 on v1

v2 whole, which is shorter than its diff:
```python
from functools import partial

import jax
import jax.numpy as jnp
from jax import lax
from jax.sharding import PartitionSpec as P

H = 17
HD = 64


epsilon = 1e-05


def normalize(values, gain, shift):
    center = values - jnp.mean(values, axis=-1, keepdims=True)
    spread = jnp.mean(center * center, axis=-1, keepdims=True)
    return center * lax.rsqrt(spread + epsilon) * gain + shift


def arrange(lengths, count):
    ends = jnp.cumsum(lengths)
    rowids = jnp.arange(count, dtype=jnp.int32)
    segment = jnp.sum((rowids[:, None] >= ends[None, :]).astype(jnp.int32), axis=1)
    inside = rowids < ends[-1]
    segment = jnp.where(inside, segment, lengths.shape[0] + rowids)
    return (segment, inside.astype(jnp.float32))


def outer(left, right):
    return lax.dot_general(
        left, right, (((0,), (0,)), ((), ())), preferred_element_type=jnp.float32
    )


def inner(left, right):
    return lax.dot_general(
        left, right, (((1,), (1,)), ((), ())), preferred_element_type=jnp.float32
    )


def block_scores(query_block, key_heads, query_segment, segment, start, width):
    key_rows = jnp.arange(segment.shape[0], dtype=jnp.int32)
    query_rows = start + jnp.arange(width, dtype=jnp.int32)
    allowed = (query_segment[:, None] == segment[None, :]) & (
        query_rows[:, None] >= key_rows[None, :]
    )
    scores = (
        jnp.einsum("qhd,khd->hqk", query_block, key_heads, preferred_element_type=jnp.float32)
        * 0.125
    )
    return jnp.where(allowed[None], scores, -1e30)


def attend_forward(queries, keys, values, segment):
    count = queries.shape[0]
    width = min(512, count)
    query_heads = queries.reshape(count, H, HD)
    key_heads = keys.reshape(count, H, HD)
    value_heads = values.reshape(count, H, HD)

    def block(index):
        start = index * width
        scores = block_scores(query_heads, key_heads, segment, segment, start, width)
        highest = jnp.max(scores, axis=-1, keepdims=True)
        expo = jnp.exp(scores - highest)
        total = jnp.sum(expo, axis=-1, keepdims=True)
        weights = (expo / total).astype(jnp.bfloat16)
        result = jnp.einsum(
            "hqk,khd->qhd", weights, value_heads, preferred_element_type=jnp.float32
        )
        return (result, (highest + jnp.log(total))[..., 0])

    results, logsums = lax.map(block, jnp.arange(count // width, dtype=jnp.int32))
    return (results.reshape(count, H * HD), logsums)


def column_sum(values):
    return jnp.sum(values.astype(jnp.float32), axis=0)


def swap(value, axis, bit):
    size = lax.axis_size(axis)
    return lax.ppermute(value, axis, [(i, i ^ bit) for i in range(size)])


def has_bit(axis, bit):
    return (lax.axis_index(axis) // bit) % 2


def tie(*values):
    return lax.optimization_barrier(values)


def halve(value, axis, bit, dim):
    mine = has_bit(axis, bit)
    half = value.shape[dim] // 2
    keep = lax.dynamic_slice_in_dim(value, mine * half, half, dim)
    give = lax.dynamic_slice_in_dim(value, (1 - mine) * half, half, dim)
    got = swap(give, axis, bit)
    return (keep.astype(jnp.float32) + got.astype(jnp.float32)).astype(value.dtype)


def double(value, axis, bit, dim):
    got = swap(value, axis, bit)
    mine = has_bit(axis, bit)
    first = jnp.where(mine == 0, value, got)
    second = jnp.where(mine == 0, got, value)
    return jnp.concatenate([first, second], axis=dim)


def exchange_sum(value, axis, bit):
    return (value.astype(jnp.float32) + swap(value, axis, bit).astype(jnp.float32)).astype(
        value.dtype
    )


def core_stage(term):
    return halve(term.astype(jnp.bfloat16), "shard", 1, 1)


def y_stage(term):
    return halve(term, "shard", 2, 0)


def x_stage(term, dim):
    return halve(term, "rep", 1, dim)


def rest_stage(term, x_dim, z_dim):
    term = halve(term, "rep", 2, z_dim)
    bit = 4
    while bit < lax.axis_size("rep"):
        term = exchange_sum(term, "rep", bit)
        bit *= 2
    term = double(term, "rep", 2, z_dim)
    term = double(term, "rep", 1, x_dim)
    return term.reshape(term.shape[2:]).astype(jnp.float32)


def reduce_small(term):
    for axis in ("shard", "rep"):
        bit = 1
        while bit < lax.axis_size(axis):
            term = exchange_sum(term, axis, bit)
            bit *= 2
    return lax.dynamic_index_in_dim(term, lax.axis_index("shard"), 0, keepdims=False)


def place(blocks):
    me = lax.axis_index("shard")
    rows = blocks[0].shape[0]
    full = jnp.zeros((rows * len(blocks),) + blocks[0].shape[1:], blocks[0].dtype)
    for offset, block in enumerate(blocks):
        full = lax.dynamic_update_slice_in_dim(full, block, (me ^ offset) * rows, 0)
    return full


def fetch_half(own):
    half = own.shape[0] // 2
    give = lax.dynamic_slice_in_dim(own, has_bit("rep", 1) * half, half, 0)
    return swap(give, "shard", 2)


def spread(own, got):
    sibling = swap(own, "shard", 1)
    remote = double(got, "rep", 1, 0)
    remote_sibling = swap(remote, "shard", 1)
    return place([own, sibling, remote, remote_sibling])


def shards(
    inputs,
    lengths,
    query_weight,
    key_weight,
    value_weight,
    out_weight,
    up_weight,
    down_weight,
    query_bias,
    value_bias,
    out_bias,
    up_bias,
    down_bias,
    gain_one,
    bias_one,
    gain_two,
    bias_two,
    cotangent,
):
    segment, inside = arrange(lengths[0], inputs.shape[0])
    count = lax.axis_size("shard")
    vectors = [
        query_bias,
        value_bias,
        out_bias,
        gain_one,
        bias_one,
        up_bias,
        down_bias,
        gain_two,
        bias_two,
    ]
    pack = jnp.concatenate(vectors)[None]
    pack_far = swap(pack, "shard", 2)
    pack_near = swap(jnp.concatenate([pack, pack_far]), "shard", 1)
    pack_all = place([pack, pack_near[:1], pack_far, pack_near[1:]]).astype(jnp.float32)
    shifts = []
    start = 0
    for item in vectors:
        shifts.append(pack_all[:, start : start + item.shape[0]].reshape(-1))
        start += item.shape[0]
    query_shift, value_shift, out_shift, first_gain, first_shift = shifts[:5]
    up_shift, down_shift, second_gain, second_shift = shifts[5:]
    got_query, got_key, got_value = (fetch_half(w) for w in (query_weight, key_weight, value_weight))
    full_query = spread(query_weight, got_query)
    full_key = spread(key_weight, got_key)
    full_value = spread(value_weight, got_value)
    got_query, got_key, got_value, out_later, up_later = tie(
        got_query, got_key, got_value, out_weight, up_weight
    )
    got_out, got_up = fetch_half(out_later), fetch_half(up_later)
    full_out = spread(out_later, got_out)
    full_up = spread(up_later, got_up)
    got_up, down_later = tie(got_up, down_weight)
    full_down = spread(down_later, fetch_half(down_later))
    residual = inputs.astype(jnp.float32)
    normed_one = normalize(residual, first_gain, first_shift).astype(jnp.bfloat16)
    queries = (
        jnp.dot(normed_one, full_query, preferred_element_type=jnp.float32) + query_shift
    ).astype(jnp.bfloat16)
    keys = jnp.dot(normed_one, full_key, preferred_element_type=jnp.float32).astype(jnp.bfloat16)
    values = (
        jnp.dot(normed_one, full_value, preferred_element_type=jnp.float32) + value_shift
    ).astype(jnp.bfloat16)
    mixed_float, logsums = attend_forward(queries, keys, values, segment)
    mixed = mixed_float.astype(jnp.bfloat16)
    middle = residual + jnp.dot(mixed, full_out, preferred_element_type=jnp.float32) + out_shift
    normed_two = normalize(middle, second_gain, second_shift).astype(jnp.bfloat16)
    pre_hidden = jnp.dot(normed_two, full_up, preferred_element_type=jnp.float32) + up_shift
    hidden = jax.nn.gelu(pre_hidden, approximate=False).astype(jnp.bfloat16)
    upstream = cotangent.astype(jnp.float32) * inside[:, None]
    upstream_low = upstream.astype(jnp.bfloat16)

    def split(term):
        return term.astype(jnp.bfloat16).reshape(2, 2, -1, term.shape[1])

    def paired(one, two):
        return jnp.stack([split(one), split(two)], axis=2)

    down_sum = split(outer(hidden, upstream_low))
    down_sum, full_down = tie(down_sum, full_down)
    down_sum = core_stage(down_sum)
    result = middle + jnp.dot(hidden, full_down, preferred_element_type=jnp.float32) + down_shift
    outputs = (result * inside[:, None]).astype(jnp.bfloat16)
    grad_hidden = inner(upstream_low, full_down)
    _, gelu_pull = jax.vjp(partial(jax.nn.gelu, approximate=False), pre_hidden)
    grad_pre = gelu_pull(grad_hidden)[0].astype(jnp.bfloat16)
    down_sum, grad_pre, outputs = tie(down_sum, grad_pre, outputs)
    down_sum = y_stage(down_sum)
    up_sum = split(outer(normed_two, grad_pre))
    up_sum, grad_pre = tie(up_sum, grad_pre)
    up_sum = core_stage(up_sum)
    grad_normed_two = inner(grad_pre, full_up)
    _, second_pull = jax.vjp(normalize, middle, second_gain, second_shift)
    grad_middle_norm, grad_second_gain, grad_second_shift = second_pull(grad_normed_two)
    grad_middle = upstream + grad_middle_norm
    grad_branch = grad_middle.astype(jnp.bfloat16)
    grad_out_term = outer(mixed, grad_branch)
    up_sum, grad_branch = tie(up_sum, grad_branch)
    up_sum = x_stage(up_sum, 2)
    grad_mixed = inner(grad_branch, full_out).astype(jnp.bfloat16)

    width = queries.shape[0]
    query_heads = queries.reshape(width, H, HD)
    key_heads = keys.reshape(width, H, HD)
    value_heads = values.reshape(width, H, HD)
    grad_heads = grad_mixed.reshape(width, H, HD)
    scores = block_scores(query_heads, key_heads, segment, segment, 0, width)
    probs = jnp.exp(scores - logsums[0][:, :, None])
    grad_values = jnp.einsum(
        "hqk,qhd->khd",
        probs.astype(jnp.bfloat16),
        grad_heads,
        preferred_element_type=jnp.float32,
    ).reshape(width, H * HD).astype(jnp.bfloat16)
    pair_one = paired(grad_out_term, outer(normed_one, grad_values))
    pair_one, grad_heads = tie(pair_one, grad_heads)
    pair_one = core_stage(pair_one)
    grad_probs = jnp.einsum(
        "qhd,khd->hqk", grad_heads, value_heads, preferred_element_type=jnp.float32
    )
    grad_scores = probs * (grad_probs - jnp.sum(probs * grad_probs, axis=-1, keepdims=True))
    grad_scores = (grad_scores * 0.125).astype(jnp.bfloat16)
    down_sum, up_sum, pair_one, grad_scores = tie(down_sum, up_sum, pair_one, grad_scores)
    down_sum = x_stage(down_sum, 2)
    up_sum = y_stage(up_sum)
    grad_queries = jnp.einsum(
        "hqk,khd->qhd", grad_scores, key_heads, preferred_element_type=jnp.float32
    ).reshape(width, H * HD).astype(jnp.bfloat16)
    grad_keys = jnp.einsum(
        "hqk,qhd->khd", grad_scores, query_heads, preferred_element_type=jnp.float32
    ).reshape(width, H * HD).astype(jnp.bfloat16)
    pair_two = paired(outer(normed_one, grad_queries), outer(normed_one, grad_keys))
    pair_two, down_sum, grad_queries, grad_keys = tie(
        pair_two, down_sum, grad_queries, grad_keys
    )
    pair_two = core_stage(pair_two)
    grad_normed_one = (
        inner(grad_queries, full_query)
        + inner(grad_keys, full_key)
        + inner(grad_values, full_value)
    )
    _, first_pull = jax.vjp(normalize, residual, first_gain, first_shift)
    grad_residual_norm, grad_first_gain, grad_first_shift = first_pull(grad_normed_one)
    grad_inputs = (grad_middle + grad_residual_norm).astype(jnp.bfloat16)
    down_total = rest_stage(down_sum, 2, 2)
    up_total = rest_stage(up_sum, 2, 3)
    pair_one = rest_stage(x_stage(y_stage(pair_one), 3), 3, 2)
    pair_two = rest_stage(y_stage(x_stage(pair_two, 3)), 3, 2)
    small = [
        column_sum(grad_queries),
        column_sum(grad_values),
        column_sum(grad_branch),
        column_sum(grad_pre),
        column_sum(upstream_low),
        grad_first_gain,
        grad_first_shift,
        grad_second_gain,
        grad_second_shift,
    ]
    packed = jnp.concatenate(
        [item.astype(jnp.bfloat16).astype(jnp.float32).reshape(count, -1) for item in small],
        axis=1,
    )
    owned = reduce_small(packed)
    pieces = []
    start = 0
    for item in small:
        size = item.shape[0] // count
        pieces.append(owned[start : start + size])
        start += size
    return (
        outputs,
        grad_inputs,
        pair_two[0],
        pair_two[1],
        pair_one[1],
        pair_one[0],
        up_total,
        down_total,
        *pieces,
    )


def solution(mesh):
    return jax.shard_map(
        shards,
        mesh=mesh,
        in_specs=(
            P(("shard", "rep"), None),
            P(("shard", "rep"), None),
            P("shard", None),
            P("shard", None),
            P("shard", None),
            P("shard", None),
            P("shard", None),
            P("shard", None),
            P("shard"),
            P("shard"),
            P("shard"),
            P("shard"),
            P("shard"),
            P("shard"),
            P("shard"),
            P("shard"),
            P("shard"),
            P(("shard", "rep"), None),
        ),
        out_specs=(
            P(("shard", "rep"), None),
            P(("shard", "rep"), None),
            P("shard", None),
            P("shard", None),
            P("shard", None),
            P("shard", None),
            P("shard", None),
            P("shard", None),
            P("shard"),
            P("shard"),
            P("shard"),
            P("shard"),
            P("shard"),
            P("shard"),
            P("shard"),
            P("shard"),
            P("shard"),
        ),
        check_vma=False,
    )
```

time: 781 us -> 802 us (1.027)
  local copies, waits for them, and re-layouts: 38.7 us -> 124 us
  waiting for transfers between devices: 406 us -> 353 us
  matrix products: 213 us -> 187 us
  starting transfers between devices: 34.2 us -> 56.5 us
  other arithmetic: 54 us -> 75.2 us
  blocking collectives: 15.1 us -> 0 us
  between operations: 16.9 us -> 2.42 us
    all_gather x6 -> x0, waiting for transfers between devices: 143 us -> none  [the longest x1 57.2 us: shards(): lax.all_gather(up_weight, 'shard', axis=0, tiled=True)]
    ppermute x33 -> x59, waiting for transfers between devices: 260 us -> 353 us  [swap(): return lax.ppermute(value, axis, [(i, i ^ bit) for i in range(size)])]
    dot_general x4 -> x3, matrix products: 69.1 us -> 17.3 us  [the longest x1 10.7 us: shards(): jnp.einsum('hqk,qhd->khd', probs.astype(jnp.bfloat16), grad_heads, prefer...]
    optimization_barrier x0 -> x1, local copies, waits for them, and re-layouts: none -> 28.9 us  [tie(): return lax.optimization_barrier(values)]
    sub x0 -> x1, matrix products: none -> 23.6 us  [shards(): grad_probs - jnp.sum(probs * grad_probs, axis=-1, keepdims=True)]
    ppermute x33 -> x59, starting transfers between devices: 34 us -> 56.5 us  [swap(): return lax.ppermute(value, axis, [(i, i ^ bit) for i in range(size)])]
    dynamic_update_slice x0 -> x22, local copies, waits for them, and re-layouts: none -> 20.9 us  [place(): full = lax.dynamic_update_slice_in_dim(full, block, (me ^ offset) * rows, 0)]
    reshape x0 -> x1, local copies, waits for them, and re-layouts: none -> 16.9 us  [split(): return term.astype(jnp.bfloat16).reshape(2, 2, -1, term.shape[1])]
  transfers between devices with their start and end apart: 39 -> 59, of which waited for: 25 -> 27; matrix products, arithmetic and copies ran while one was open for 23% -> 34% of each run, Pallas kernels for 0% -> 0%
where the time goes in v2:
time: 802 us; the launch traced here: 797 us
  waiting for transfers between devices  353 us (44%)
  matrix products  187 us (23%)
  local copies, waits for them, and re-layouts  124 us (15%)
  other arithmetic  75.2 us (9%)
  starting transfers between devices  56.5 us (7%)
    ppermute x59, waiting for transfers between devices, swap(): return lax.ppermute(value, axis, [(i, i ^ bit) for i in range(size)])  353 us
    ppermute x59, starting transfers between devices, swap(): return lax.ppermute(value, axis, [(i, i ^ bit) for i in range(size)])  56.5 us
    dot_general x6, matrix products, inner(): lax.dot_general(left, right, (((1,), (1,)), ((), ())), preferred_element_...  40.8 us
    dot_general x1, matrix products, shards(): jnp.dot(normed_two, full_up, preferred_element_type=jnp.float32) + up_shift  35.2 us
    dot_general x6, matrix products, outer(): lax.dot_general(left, right, (((0,), (0,)), ((), ())), preferred_element_...  30 us
    optimization_barrier x1, local copies, waits for them, and re-layouts, tie(): return lax.optimization_barrier(values)  28.9 us
    convert_element_type x16, other arithmetic, halve(): (keep.astype(jnp.float32) + got.astype(jnp.float32)).astype(value.dtype)  27.3 us
    sub x1, matrix products, shards(): grad_probs - jnp.sum(probs * grad_probs, axis=-1, keepdims=True)  23.6 us
  transfers between devices with their start and end apart: 59, of which 27 were waited for; matrix products, arithmetic and copies ran while one was open for 34% of the time, Pallas kernels for 0%

profile of v2, /device:TPU:0, one launch (start us, length us, event | category | flops | bytes accessed | tf_op | source)
XLA Modules:
  0.0 797.2 jit_solution(1321015869093532760)
XLA Ops:
  0.7 6.4 concatenate.54
  30.9 5.4 collective-permute-done.7
  37.1 4.1 broadcast_in_dim.88
  45.7 6.9 collective-permute-done.4
  54.2 7.5 collective-permute-done.12
  63.2 6.6 collective-permute-done.8
  74.7 5.5 collective-permute-done.15
  81.9 8.1 %collective-permute-done.16 = bf16[136,1088]{1,0:T(8,128)(2,1)S(1)} collective-permute-done((bf16[136,1088]{1,0:T(8,128)(2,1)S(1)}, bf16[136,1088]{1,0:T(8,128)(2,1)S(1)}, u32[]{:S(2)}, u32[]{:S(2)}) %collective-permute-start.16) | collective-permute-done | bytes 295968 | tf_op jit(solution)/shard_map/ppermute | solution.py:84
  100.3 8.4 %fusion.69 = (f32[17,512]{1,0:T(8,128)S(1)}, f32[17,512,512]{1,2,0:T(8,128)}) fusion(bf16[512,17,64]{0,2,1:T(8,128)(2,1)S(1)} %bitcast.103, bf16[512,17,64]{0,2,1:T(8,128)(2,1)S(1)} %bitcast.98, pred[512,512]{0,1:T(8,128)(4,1)S(1)} %copy-done.49), kind=kOutput, calls=%fused_computation.236 | convolution fusion | flops 583785984 | bytes 20350976 | tf_op jit(solution)/shard_map/while/body/eval_jaxpr/qhd,khd->hqk/dot_general | solution.py:49
  108.8 9.4 %fusion.2 = f32[17,512]{1,0:T(8,128)} fusion(f32[17,512,512]{1,2,0:T(8,128)} %get-tuple-element.156, f32[17,512]{1,0:T(8,128)S(1)} %get-tuple-element.155), kind=kLoop, calls=%fused_computation.10 | loop fusion | flops 8904192 | bytes 17895424 | tf_op jit(solution)/shard_map/while/body/eval_jaxpr/reduce_sum | solution.py:67
  118.2 9.5 %fusion.40 = bf16[17,64,512]{2,1,0:T(8,128)(2,1)S(1)} fusion(bf16[512,17,64]{0,2,1:T(8,128)(2,1)} %bitcast.117, f32[17,512,512]{1,2,0:T(8,128)} %get-tuple-element.156, f32[17,512]{1,0:T(8,128)} %fusion.2, f32[17,512]{1,0:T(8,128)S(1)} %get-tuple-element.155), kind=kOutput, calls=%fused_computation.93 | convolution fusion | flops 584351744 | bytes 20123648 | tf_op jit(solution)/shard_map/while/body/eval_jaxpr/hqk,khd->qhd/dot_general | solution.py:69
  138.8 22.3 %collective-permute-done.23 = bf16[544,1088]{1,0:T(8,128)(2,1)} collective-permute-done((bf16[544,1088]{1,0:T(8,128)(2,1)}, bf16[544,1088]{1,0:T(8,128)(2,1)}, u32[]{:S(2)}, u32[]{:S(2)}) %collective-permute-start.23) | collective-permute-done | bytes 1183776 | tf_op jit(solution)/shard_map/ppermute | solution.py:84
  171.5 19.2 %collective-permute-done.24 = bf16[544,1088]{1,0:T(8,128)(2,1)S(1)} collective-permute-done((bf16[544,1088]{1,0:T(8,128)(2,1)}, bf16[544,1088]{1,0:T(8,128)(2,1)S(1)}, u32[]{:S(2)}, u32[]{:S(2)}) %collective-permute-start.24) | collective-permute-done | bytes 1183776 | tf_op jit(solution)/shard_map/ppermute | solution.py:84
  195.9 35.2 %multiply_convert_fusion.1 = (bf16[512,4352]{1,0:T(8,128)(2,1)}, f32[512,4352]{1,0:T(8,128)}, f32[512,4352]{1,0:T(8,128)}) fusion(f32[4352]{0:T(1024)S(1)} %copy-done.62, bf16[1088,4352]{1,0:T(8,128)(2,1)} %constant_dynamic-update-slice_fusion.4, f32[512,1088]{0,1:T(8,128)S(1)} %get-tuple-element.158, f32[1088]{0:T(1024)S(1)} %copy-done.71, ...), kind=kOutput, calls=%fused_computation.20 | convolution fusion | flops 4998463488 | bytes 34010624 | tf_op jit(solution)/shard_map/dot_general | solution.py:241
  231.1 9.8 %convolution_convert_fusion = bf16[4352,1088]{0,1:T(8,128)(2,1)} fusion(bf16[512,4352]{1,0:T(8,128)(2,1)} %get-tuple-element.99, bf16[512,1088]{0,1:T(8,128)(2,1)S(1)} %copy-done.6, f32[512]{0:T(512)S(1)} %fusion.54), kind=kOutput, calls=%fused_computation.1 | convolution fusion | flops 4855021568 | bytes 15042560 | tf_op jit(solution)/shard_map/dot_general | solution.py:31
  240.9 16.9 %reshape.335 = bf16[2,2,1088,1088]{2,1,0,3:T(2,128)(2,1)} reshape(bf16[4352,1088]{0,1:T(8,128)(2,1)} %convolution_convert_fusion) | data formatting | bytes 18939904 | tf_op jit(solution)/shard_map/reshape | solution.py:247
  261.1 28.9 %copy.46 = bf16[2,2,1088,1088]{3,2,1,0:T(8,128)(2,1)} copy(bf16[2,2,1088,1088]{2,1,0,3:T(2,128)(2,1)} %reshape.335) | data formatting | bytes 18939904 | tf_op jit(solution)/shard_map/optimization_barrier | solution.py:92
  290.0 5.2 constant_dynamic-slice_fusion.17
  296.4 13.4 %fusion.27 = bf16[512,1088]{0,1:T(8,128)(2,1)} fusion(f32[512,1088]{0,1:T(8,128)S(1)} %copy-done.13, bf16[512,4352]{1,0:T(8,128)(2,1)} %get-tuple-element.99, bf16[4352,1088]{1,0:T(8,128)(2,1)} %constant_dynamic-update-slice_fusion, f32[1088]{0:T(1024)} %add.431, f32[512]{0:T(512)S(1)} %fusion.54), kind=kOutput, calls=%fused_computation.66 | convolution fusion | flops 4850843648 | bytes 17275136 | tf_op jit(solution)/shard_map/dot_general | solution.py:255
  309.7 14.8 %add_convert_fusion.2 = bf16[512,4352]{1,0:T(8,128)(2,1)} fusion(f32[512,4352]{1,0:T(8,128)} %get-tuple-element.100, f32[512,4352]{1,0:T(8,128)} %get-tuple-element.159, f32[4352]{0:T(1024)S(1)} %copy-done.62, bf16[4352,1088]{1,0:T(8,128)(2,1)} %constant_dynamic-update-slice_fusion, bf16[512,1088]{0,1:T(8,128)(2,1)S(1)} %copy-done.6, f32[512]{0:T(512)S(1)} %fusion.54), kind=kOutput, calls=%fused_computation.19 | convolution fusion | flops 4883709952 | bytes 32885760 | tf_op jit(solution)/shard_map/dot_general | solution.py:37
  324.5 5.1 add_convert_fusion
  329.7 10.2 %convolution_convert_fusion.1 = bf16[1088,4352]{1,0:T(8,128)(2,1)S(1)} fusion(bf16[512,4352]{1,0:T(8,128)(2,1)} %add_convert_fusion.2, f32[512,1088]{0,1:T(8,128)} %copy-done.12, f32[1088]{0:T(1024)S(1)} %copy-done.71, f32[1088]{0:T(1024)S(1)} %mul.271, f32[512]{0:T(512)S(1)} %fusion.56, f32[512]{0:T(512)S(1)} %broadcast_multiply_fusion), kind=kOutput, calls=%fused_computation.2 | convolution fusion | flops 4856135680 | bytes 16167424 | tf_op jit(solution)/shard_map/dot_general | solution.py:31
  348.8 10.7 %multiply_reduce_fusion.1 = (bf16[1088]{0:T(1024)(128)(2,1)S(1)}, f32[512]{0:T(512)S(1)}, bf16[1088]{0:T(1024)(128)(2,1)S(1)}, f32[512,1088]{0,1:T(8,128)}) fusion(f32[512,1088]{0,1:T(8,128)S(1)} %copy-done.14, f32[512]{0:T(512)S(1)} %fusion.56, f32[512]{0:T(512)S(1)} %broadcast_multiply_fusion, f32[1088]{0:T(1024)S(1)} %mul.271, ...), kind=kOutput, calls=%fused_computation.84 | convolution fusion | flops 4853069312 | bytes 18397696 | tf_op jit(solution)/shard_map/dot_general | solution.py:37
  370.3 34.6 %collective-permute-done.27 = bf16[1,1,1088,1088]{3,2,1,0:T(8,128)(2,1)} collective-permute-done((bf16[1,1,1088,1088]{3,2,1,0:T(8,128)(2,1)}, bf16[1,1,1088,1088]{3,2,1,0:T(8,128)(2,1)}, u32[]{:S(2)}, u32[]{:S(2)}) %collective-permute-start.27) | collective-permute-done | bytes 2367520 | tf_op jit(solution)/shard_map/ppermute | solution.py:84
  404.9 3.8 add_convert_fusion.5
  408.8 5.8 add_convert_fusion.1
  418.8 10.7 %fusion.71 = (bf16[17,64]{1,0:T(8,128)(2,1)S(1)}, bf16[17,64,512]{2,1,0:T(8,128)(2,1)}) fusion(bf16[512,17,64]{0,2,1:T(8,128)(2,1)} %bitcast.109, f32[17,512,512]{1,2,0:T(8,128)} %get-tuple-element.156, f32[17,512]{1,0:T(8,128)S(1)} %log_add_fusion), kind=kOutput, calls=%fused_computation.238 | convolution fusion | flops 580451264 | bytes 20091008 | tf_op jit(solution)/shard_map/hqk,qhd->khd/dot_general | solution.py:282
  433.5 5.1 constant_dynamic-slice_fusion.14
  444.9 23.6 %multiply_convert_fusion = bf16[17,512,512]{1,2,0:T(8,128)(2,1)} fusion(f32[17,512,512]{1,2,0:T(8,128)} %get-tuple-element.156, f32[17,512]{1,0:T(8,128)S(1)} %log_add_fusion, bf16[512,17,64]{0,2,1:T(8,128)(2,1)} %bitcast.110, bf16[512,17,64]{0,2,1:T(8,128)(2,1)} %bitcast.118), kind=kOutput, calls=%fused_computation.3 | convolution fusion | flops 1172055040 | bytes 29001728 | tf_op jit(solution)/shard_map/sub | solution.py:294
  468.5 22.9 %collective-permute-done.29 = bf16[2,1,136,4352]{3,2,1,0:T(8,128)(2,1)} collective-permute-done((bf16[2,1,136,4352]{3,2,1,0:T(8,128)(2,1)}, bf16[2,1,136,4352]{3,2,1,0:T(8,128)(2,1)}, u32[]{:S(2)}, u32[]{:S(2)}) %collective-permute-start.29) | collective-permute-done | bytes 2367520 | tf_op jit(solution)/shard_map/ppermute | solution.py:84
  497.4 5.0 convolution_convert_fusion.8
  515.4 17.7 %collective-permute-done.45 = bf16[1,1,136,4352]{3,2,1,0:T(8,128)(2,1)S(1)} collective-permute-done((bf16[1,1,136,4352]{3,2,1,0:T(8,128)(2,1)S(1)}, bf16[1,1,136,4352]{3,2,1,0:T(8,128)(2,1)S(1)}, u32[]{:S(2)}, u32[]{:S(2)}) %collective-permute-start.45) | collective-permute-done | bytes 1183776 | tf_op jit(solution)/shard_map/ppermute | solution.py:84
  541.8 6.7 fusion.64
  551.6 5.6 collective-permute-done.39
  567.9 6.1 collective-permute-done.56
  581.8 6.0 collective-permute-done.58
  598.4 16.1 %collective-permute-done.41 = bf16[1,1,1,136,1088]{4,3,2,1,0:T(8,128)(2,1)S(1)} collective-permute-done((bf16[1,1,1,136,1088]{4,3,2,1,0:T(8,128)(2,1)S(1)}, bf16[1,1,1,136,1088]{4,3,2,1,0:T(8,128)(2,1)S(1)}, u32[]{:S(2)}, u32[]{:S(2)}) %collective-permute-start.41) | collective-permute-done | bytes 295968 | tf_op jit(solution)/shard_map/ppermute | solution.py:84
  614.5 4.5 collective-permute-start.42
  619.0 20.0 %collective-permute-done.47 = bf16[1,1,136,2176]{3,2,1,0:T(8,128)(2,1)S(1)} collective-permute-done((bf16[1,1,136,2176]{3,2,1,0:T(8,128)(2,1)S(1)}, bf16[1,1,136,2176]{3,2,1,0:T(8,128)(2,1)S(1)}, u32[]{:S(2)}, u32[]{:S(2)}) %collective-permute-start.47) | collective-permute-done | bytes 591904 | tf_op jit(solution)/shard_map/ppermute | solution.py:84
  639.2 17.1 %collective-permute-done.42 = bf16[1,1,1,136,1088]{4,3,2,1,0:T(8,128)(2,1)S(1)} collective-permute-done((bf16[1,1,1,136,1088]{4,3,2,1,0:T(8,128)(2,1)S(1)}, bf16[1,1,1,136,1088]{4,3,2,1,0:T(8,128)(2,1)S(1)}, u32[]{:S(2)}, u32[]{:S(2)}) %collective-permute-start.42) | collective-permute-done | bytes 295968 | tf_op jit(solution)/shard_map/ppermute | solution.py:84
  658.7 17.0 %collective-permute-done.43 = bf16[1,1,1,136,1088]{4,3,2,1,0:T(8,128)(2,1)S(1)} collective-permute-done((bf16[1,1,1,136,1088]{4,3,2,1,0:T(8,128)(2,1)S(1)}, bf16[1,1,1,136,1088]{4,3,2,1,0:T(8,128)(2,1)S(1)}, u32[]{:S(2)}, u32[]{:S(2)}) %collective-permute-start.43) | collective-permute-done | bytes 295968 | tf_op jit(solution)/shard_map/ppermute | solution.py:84
  680.5 8.5 %collective-permute-done.52 = bf16[1,1,272,1088]{3,2,1,0:T(8,128)(2,1)S(1)} collective-permute-done((bf16[1,1,272,1088]{3,2,1,0:T(8,128)(2,1)S(1)}, bf16[1,1,272,1088]{3,2,1,0:T(8,128)(2,1)S(1)}, u32[]{:S(2)}, u32[]{:S(2)}) %collective-permute-start.52) | collective-permute-done | bytes 591904 | tf_op jit(solution)/shard_map/ppermute | solution.py:84
  690.8 28.9 %collective-permute-done.33 = bf16[2,1,2,136,1088]{4,3,2,1,0:T(8,128)(2,1)S(1)} collective-permute-done((bf16[2,1,2,136,1088]{4,3,2,1,0:T(8,128)(2,1)S(1)}, bf16[2,1,2,136,1088]{4,3,2,1,0:T(8,128)(2,1)S(1)}, u32[]{:S(2)}, u32[]{:S(2)}) %collective-permute-start.33) | collective-permute-done | bytes 1183776 | tf_op jit(solution)/shard_map/ppermute | solution.py:84
  721.0 13.3 %collective-permute-done.34 = bf16[1,1,2,136,1088]{4,3,2,1,0:T(8,128)(2,1)S(1)} collective-permute-done((bf16[1,1,2,136,1088]{4,3,2,1,0:T(8,128)(2,1)S(1)}, bf16[1,1,2,136,1088]{4,3,2,1,0:T(8,128)(2,1)S(1)}, u32[]{:S(2)}, u32[]{:S(2)}) %collective-permute-start.34) | collective-permute-done | bytes 591904 | tf_op jit(solution)/shard_map/ppermute | solution.py:84
  734.5 10.6 %collective-permute-done.49 = bf16[1,1,136,4352]{3,2,1,0:T(8,128)(2,1)S(1)} collective-permute-done((bf16[1,1,136,4352]{3,2,1,0:T(8,128)(2,1)S(1)}, bf16[1,1,136,4352]{3,2,1,0:T(8,128)(2,1)S(1)}, u32[]{:S(2)}, u32[]{:S(2)}) %collective-permute-start.49) | collective-permute-done | bytes 1183776 | tf_op jit(solution)/shard_map/ppermute | solution.py:84
  746.7 24.2 %collective-permute-done.53 = bf16[1,1,544,1088]{3,2,1,0:T(8,128)(2,1)S(1)} collective-permute-done((bf16[1,1,544,1088]{3,2,1,0:T(8,128)(2,1)S(1)}, bf16[1,1,544,1088]{3,2,1,0:T(8,128)(2,1)S(1)}, u32[]{:S(2)}, u32[]{:S(2)}) %collective-permute-start.53) | collective-permute-done | bytes 1183776 | tf_op jit(solution)/shard_map/ppermute | solution.py:84
  774.2 5.7 collective-permute-done.37
  784.2 10.2 %collective-permute-done.38 = bf16[1,1,2,136,1088]{4,3,2,1,0:T(8,128)(2,1)S(1)} collective-permute-done((bf16[1,1,2,136,1088]{4,3,2,1,0:T(8,128)(2,1)S(1)}, bf16[1,1,2,136,1088]{4,3,2,1,0:T(8,128)(2,1)S(1)}, u32[]{:S(2)}, u32[]{:S(2)}) %collective-permute-start.38) | collective-permute-done | bytes 591904 | tf_op jit(solution)/shard_map/ppermute | solution.py:84
  (425 shorter events, 195.6 us)
Async XLA Ops:
  7.1 18.1 %collective-permute-start = (bf16[1,3264]{1,0:T(2,128)(2,1)S(1)}, bf16[1,3264]{1,0:T(2,128)(2,1)S(1)}, u32[]{:S(2)}, u32[]{:S(2)}) collective-permute-start(bf16[1,3264]{1,0:T(2,128)(2,1)S(1)} %broadcast_in_dim.85), channel_id=1, source_target_pairs={{0,16},{8,24},{16,0},{24,8},{1,17},{9,25},{17,1},{25,9},{2,18},{10... | collective-permute-start | bytes 19592 | tf_op jit(solution)/shard_map/ppermute | solution.py:84
  11.1 19.6 %collective-permute-start.3 = (bf16[136,1088]{1,0:T(8,128)(2,1)S(1)}, bf16[136,1088]{1,0:T(8,128)(2,1)S(1)}, u32[]{:S(2)}, u32[]{:S(2)}) collective-permute-start(bf16[136,1088]{1,0:T(8,128)(2,1)S(1)} %constant_dynamic-slice_fusion.23), channel_id=1, source_target_pairs={{0,16},{8,24},{16,0},{24,8},{1,17},{9,25},{17,1},{25,9},{2,18},{10... | collective-permute-start | bytes 887816 | tf_op jit(solution)/shard_map/ppermute | solution.py:84
  11.2 58.7 %collective-permute-start.10 = (bf16[272,1088]{1,0:T(8,128)(2,1)}, bf16[272,1088]{1,0:T(8,128)(2,1)}, u32[]{:S(2)}, u32[]{:S(2)}) collective-permute-start(bf16[272,1088]{1,0:T(8,128)(2,1)} %param.21), channel_id=1, source_target_pairs={{0,8},{8,0},{16,24},{24,16},{1,9},{9,1},{17,25},{25,17},{2,10},{10... | collective-permute-start | bytes 1775624 | tf_op jit(solution)/shard_map/ppermute | solution.py:84
  12.3 18.6 %collective-permute-start.11 = (bf16[136,1088]{1,0:T(8,128)(2,1)S(1)}, bf16[136,1088]{1,0:T(8,128)(2,1)S(1)}, u32[]{:S(2)}, u32[]{:S(2)}) collective-permute-start(bf16[136,1088]{1,0:T(8,128)(2,1)S(1)} %constant_dynamic-slice_fusion.21), channel_id=1, source_target_pairs={{0,16},{8,24},{16,0},{24,8},{1,17},{9,25},{17,1},{25,9},{2,18},{10... | collective-permute-start | bytes 887816 | tf_op jit(solution)/shard_map/ppermute | solution.py:84
  14.3 57.3 %collective-permute-start.6 = (bf16[272,1088]{1,0:T(8,128)(2,1)}, bf16[272,1088]{1,0:T(8,128)(2,1)}, u32[]{:S(2)}, u32[]{:S(2)}) collective-permute-start(bf16[272,1088]{1,0:T(8,128)(2,1)} %param.20), channel_id=1, source_target_pairs={{0,8},{8,0},{16,24},{24,16},{1,9},{9,1},{17,25},{25,17},{2,10},{10... | collective-permute-start | bytes 1775624 | tf_op jit(solution)/shard_map/ppermute | solution.py:84
  26.5 9.8 %collective-permute-start.7 = (bf16[136,1088]{1,0:T(8,128)(2,1)}, bf16[136,1088]{1,0:T(8,128)(2,1)S(1)}, u32[]{:S(2)}, u32[]{:S(2)}) collective-permute-start(bf16[136,1088]{1,0:T(8,128)(2,1)} %constant_dynamic-slice_fusion.22), channel_id=1, source_target_pairs={{0,16},{8,24},{16,0},{24,8},{1,17},{9,25},{17,1},{25,9},{2,18},{10... | collective-permute-start | bytes 887816 | tf_op jit(solution)/shard_map/ppermute | solution.py:84
  30.8 49.4 %collective-permute-start.2 = (bf16[272,1088]{1,0:T(8,128)(2,1)}, bf16[272,1088]{1,0:T(8,128)(2,1)S(1)}, u32[]{:S(2)}, u32[]{:S(2)}) collective-permute-start(bf16[272,1088]{1,0:T(8,128)(2,1)} %param.22), channel_id=1, source_target_pairs={{0,8},{8,0},{16,24},{24,16},{1,9},{9,1},{17,25},{25,17},{2,10},{10... | collective-permute-start | bytes 1775624 | tf_op jit(solution)/shard_map/ppermute | solution.py:84
  37.0 53.0 %collective-permute-start.14 = (bf16[272,1088]{1,0:T(8,128)(2,1)}, bf16[272,1088]{1,0:T(8,128)(2,1)S(1)}, u32[]{:S(2)}, u32[]{:S(2)}) collective-permute-start(bf16[272,1088]{1,0:T(8,128)(2,1)} %param.23), channel_id=1, source_target_pairs={{0,8},{8,0},{16,24},{24,16},{1,9},{9,1},{17,25},{25,17},{2,10},{10... | collective-permute-start | bytes 1775624 | tf_op jit(solution)/shard_map/ppermute | solution.py:84
  42.8 9.8 %collective-permute-start.4 = (bf16[136,1088]{1,0:T(8,128)(2,1)S(1)}, bf16[136,1088]{1,0:T(8,128)(2,1)S(1)}, u32[]{:S(2)}, u32[]{:S(2)}) collective-permute-start(bf16[136,1088]{1,0:T(8,128)(2,1)S(1)} %copy-done.53), channel_id=1, source_target_pairs={{0,1},{1,0},{2,3},{3,2},{4,5},{5,4},{6,7},{7,6},{8,9},{9,8},{10,11... | collective-permute-start | bytes 887816 | tf_op jit(solution)/shard_map/ppermute | solution.py:84
  69.8 92.8 %collective-permute-start.18 = (bf16[272,4352]{1,0:T(8,128)(2,1)S(1)}, bf16[272,4352]{1,0:T(8,128)(2,1)}, u32[]{:S(2)}, u32[]{:S(2)}) collective-permute-start(bf16[272,4352]{1,0:T(8,128)(2,1)S(1)} %copy-done.19), channel_id=1, source_target_pairs={{0,8},{8,0},{16,24},{24,16},{1,9},{9,1},{17,25},{25,17},{2,10},{10... | collective-permute-start | bytes 7102472 | tf_op jit(solution)/shard_map/ppermute | solution.py:84
  69.9 10.3 %collective-permute-start.15 = (bf16[136,1088]{1,0:T(8,128)(2,1)S(1)}, bf16[136,1088]{1,0:T(8,128)(2,1)S(1)}, u32[]{:S(2)}, u32[]{:S(2)}) collective-permute-start(bf16[136,1088]{1,0:T(8,128)(2,1)S(1)} %constant_dynamic-slice_fusion.20), channel_id=1, source_target_pairs={{0,16},{8,24},{16,0},{24,8},{1,17},{9,25},{17,1},{25,9},{2,18},{10... | collective-permute-start | bytes 887816 | tf_op jit(solution)/shard_map/ppermute | solution.py:84
  71.6 56.1 %collective-permute-start.19 = (bf16[136,4352]{1,0:T(8,128)(2,1)}, bf16[136,4352]{1,0:T(8,128)(2,1)}, u32[]{:S(2)}, u32[]{:S(2)}) collective-permute-start(bf16[136,4352]{1,0:T(8,128)(2,1)} %constant_dynamic-slice_fusion.19), channel_id=1, source_target_pairs={{0,16},{8,24},{16,0},{24,8},{1,17},{9,25},{17,1},{25,9},{2,18},{10... | collective-permute-start | bytes 3551240 | tf_op jit(solution)/shard_map/ppermute | solution.py:84
  80.2 11.5 %collective-permute-start.13 = (bf16[272,1088]{1,0:T(8,128)(2,1)S(1)}, bf16[272,1088]{1,0:T(8,128)(2,1)S(1)}, u32[]{:S(2)}, u32[]{:S(2)}) collective-permute-start(bf16[272,1088]{1,0:T(8,128)(2,1)S(1)} %get-tuple-element.133), channel_id=1, source_target_pairs={{0,8},{8,0},{16,24},{24,16},{1,9},{9,1},{17,25},{25,17},{2,10},{10... | collective-permute-start | bytes 1775624 | tf_op jit(solution)/shard_map/ppermute | solution.py:84
  80.2 9.8 %collective-permute-start.16 = (bf16[136,1088]{1,0:T(8,128)(2,1)S(1)}, bf16[136,1088]{1,0:T(8,128)(2,1)S(1)}, u32[]{:S(2)}, u32[]{:S(2)}) collective-permute-start(bf16[136,1088]{1,0:T(8,128)(2,1)S(1)} %collective-permute-done.15), channel_id=1, source_target_pairs={{0,1},{1,0},{2,3},{3,2},{4,5},{5,4},{6,7},{7,6},{8,9},{9,8},{10,11... | collective-permute-start | bytes 887816 | tf_op jit(solution)/shard_map/ppermute | solution.py:84
  91.7 39.4 %collective-permute-start.17 = (bf16[272,1088]{1,0:T(8,128)(2,1)}, bf16[272,1088]{1,0:T(8,128)(2,1)}, u32[]{:S(2)}, u32[]{:S(2)}) collective-permute-start(bf16[272,1088]{1,0:T(8,128)(2,1)} %get-tuple-element.129), channel_id=1, source_target_pairs={{0,8},{8,0},{16,24},{24,16},{1,9},{9,1},{17,25},{25,17},{2,10},{10... | collective-permute-start | bytes 1775624 | tf_op jit(solution)/shard_map/ppermute | solution.py:84
  127.7 41.6 %collective-permute-start.22 = (bf16[1088,1088]{1,0:T(8,128)(2,1)}, bf16[1088,1088]{1,0:T(8,128)(2,1)}, u32[]{:S(2)}, u32[]{:S(2)}) collective-permute-start(bf16[1088,1088]{1,0:T(8,128)(2,1)} %param.25), channel_id=1, source_target_pairs={{0,8},{8,0},{16,24},{24,16},{1,9},{9,1},{17,25},{25,17},{2,10},{10... | collective-permute-start | bytes 7102472 | tf_op jit(solution)/shard_map/ppermute | solution.py:84
  130.7 30.4 %collective-permute-start.23 = (bf16[544,1088]{1,0:T(8,128)(2,1)}, bf16[544,1088]{1,0:T(8,128)(2,1)}, u32[]{:S(2)}, u32[]{:S(2)}) collective-permute-start(bf16[544,1088]{1,0:T(8,128)(2,1)} %constant_dynamic-slice_fusion.18), channel_id=1, source_target_pairs={{0,16},{8,24},{16,0},{24,8},{1,17},{9,25},{17,1},{25,9},{2,18},{10... | collective-permute-start | bytes 3551240 | tf_op jit(solution)/shard_map/ppermute | solution.py:84
  134.0 31.9 %collective-permute-start.20 = (bf16[136,4352]{1,0:T(8,128)(2,1)}, bf16[136,4352]{1,0:T(8,128)(2,1)}, u32[]{:S(2)}, u32[]{:S(2)}) collective-permute-start(bf16[136,4352]{1,0:T(8,128)(2,1)} %collective-permute-done.19), channel_id=1, source_target_pairs={{0,1},{1,0},{2,3},{3,2},{4,5},{5,4},{6,7},{7,6},{8,9},{9,8},{10,11... | collective-permute-start | bytes 3551240 | tf_op jit(solution)/shard_map/ppermute | solution.py:84
  161.1 29.5 %collective-permute-start.24 = (bf16[544,1088]{1,0:T(8,128)(2,1)}, bf16[544,1088]{1,0:T(8,128)(2,1)S(1)}, u32[]{:S(2)}, u32[]{:S(2)}) collective-permute-start(bf16[544,1088]{1,0:T(8,128)(2,1)} %collective-permute-done.23), channel_id=1, source_target_pairs={{0,1},{1,0},{2,3},{3,2},{4,5},{5,4},{6,7},{7,6},{8,9},{9,8},{10,11... | collective-permute-start | bytes 3551240 | tf_op jit(solution)/shard_map/ppermute | solution.py:84
  169.3 24.8 %collective-permute-start.21 = (bf16[272,4352]{1,0:T(8,128)(2,1)S(1)}, bf16[272,4352]{1,0:T(8,128)(2,1)S(1)}, u32[]{:S(2)}, u32[]{:S(2)}) collective-permute-start(bf16[272,4352]{1,0:T(8,128)(2,1)S(1)} %get-tuple-element.113), channel_id=1, source_target_pairs={{0,8},{8,0},{16,24},{24,16},{1,9},{9,1},{17,25},{25,17},{2,10},{10... | collective-permute-start | bytes 7102472 | tf_op jit(solution)/shard_map/ppermute | solution.py:84
  194.1 63.6 %collective-permute-start.25 = (bf16[1088,1088]{1,0:T(8,128)(2,1)}, bf16[1088,1088]{1,0:T(8,128)(2,1)}, u32[]{:S(2)}, u32[]{:S(2)}) collective-permute-start(bf16[1088,1088]{1,0:T(8,128)(2,1)} %get-tuple-element.107), channel_id=1, source_target_pairs={{0,8},{8,0},{16,24},{24,16},{1,9},{9,1},{17,25},{25,17},{2,10},{10... | collective-permute-start | bytes 7102472 | tf_op jit(solution)/shard_map/ppermute | solution.py:84
  295.2 29.3 %collective-permute-start.26 = (bf16[2,1,1088,1088]{3,2,1,0:T(8,128)(2,1)}, bf16[2,1,1088,1088]{3,2,1,0:T(8,128)(2,1)}, u32[]{:S(2)}, u32[]{:S(2)}) collective-permute-start(bf16[2,1,1088,1088]{3,2,1,0:T(8,128)(2,1)} %constant_dynamic-slice_fusion.17), channel_id=1, source_target_pairs={{0,8},{8,0},{16,24},{24,16},{1,9},{9,1},{17,25},{25,17},{2,10},{10... | collective-permute-start | bytes 14204936 | tf_op jit(solution)/shard_map/ppermute | solution.py:84
  346.1 62.6 %collective-permute-start.28 = (bf16[2,1,272,4352]{3,2,1,0:T(8,128)(2,1)}, bf16[2,1,272,4352]{3,2,1,0:T(8,128)(2,1)}, u32[]{:S(2)}, u32[]{:S(2)}) collective-permute-start(bf16[2,1,272,4352]{3,2,1,0:T(8,128)(2,1)} %constant_dynamic-slice_fusion.15), channel_id=1, source_target_pairs={{0,8},{8,0},{16,24},{24,16},{1,9},{9,1},{17,25},{25,17},{2,10},{10... | collective-permute-start | bytes 14204936 | tf_op jit(solution)/shard_map/ppermute | solution.py:84
  348.2 56.6 %collective-permute-start.27 = (bf16[1,1,1088,1088]{3,2,1,0:T(8,128)(2,1)}, bf16[1,1,1088,1088]{3,2,1,0:T(8,128)(2,1)}, u32[]{:S(2)}, u32[]{:S(2)}) collective-permute-start(bf16[1,1,1088,1088]{3,2,1,0:T(8,128)(2,1)} %constant_dynamic-slice_fusion.16), channel_id=1, source_target_pairs={{0,16},{8,24},{16,0},{24,8},{1,17},{9,25},{17,1},{25,9},{2,18},{10... | collective-permute-start | bytes 7102472 | tf_op jit(solution)/shard_map/ppermute | solution.py:84
  438.6 52.8 %collective-permute-start.29 = (bf16[2,1,136,4352]{3,2,1,0:T(8,128)(2,1)}, bf16[2,1,136,4352]{3,2,1,0:T(8,128)(2,1)}, u32[]{:S(2)}, u32[]{:S(2)}) collective-permute-start(bf16[2,1,136,4352]{3,2,1,0:T(8,128)(2,1)} %constant_dynamic-slice_fusion.14), channel_id=1, source_target_pairs={{0,1},{1,0},{2,3},{3,2},{4,5},{5,4},{6,7},{7,6},{8,9},{9,8},{10,11... | collective-permute-start | bytes 7102472 | tf_op jit(solution)/shard_map/ppermute | solution.py:84
  441.9 52.6 %collective-permute-start.30 = (bf16[2,1,2,272,1088]{4,3,2,1,0:T(8,128)(2,1)}, bf16[2,1,2,272,1088]{4,3,2,1,0:T(8,128)(2,1)}, u32[]{:S(2)}, u32[]{:S(2)}) collective-permute-start(bf16[2,1,2,272,1088]{4,3,2,1,0:T(8,128)(2,1)} %constant_dynamic-slice_fusion.13), channel_id=1, source_target_pairs={{0,8},{8,0},{16,24},{24,16},{1,9},{9,1},{17,25},{25,17},{2,10},{10... | collective-permute-start | bytes 7102472 | tf_op jit(solution)/shard_map/ppermute | solution.py:84
  504.0 29.1 %collective-permute-start.45 = (bf16[1,1,136,4352]{3,2,1,0:T(8,128)(2,1)S(1)}, bf16[1,1,136,4352]{3,2,1,0:T(8,128)(2,1)S(1)}, u32[]{:S(2)}, u32[]{:S(2)}) collective-permute-start(bf16[1,1,136,4352]{3,2,1,0:T(8,128)(2,1)S(1)} %constant_dynamic-slice_fusion.4), channel_id=1, source_target_pairs={{0,16},{8,24},{16,0},{24,8},{1,17},{9,25},{17,1},{25,9},{2,18},{10... | collective-permute-start | bytes 3551240 | tf_op jit(solution)/shard_map/ppermute | solution.py:84
  505.7 51.5 %collective-permute-start.39 = (bf16[1,1,2,272,1088]{4,3,2,1,0:T(8,128)(2,1)}, bf16[1,1,2,272,1088]{4,3,2,1,0:T(8,128)(2,1)}, u32[]{:S(2)}, u32[]{:S(2)}) collective-permute-start(bf16[1,1,2,272,1088]{4,3,2,1,0:T(8,128)(2,1)} %constant_dynamic-slice_fusion.7), channel_id=1, source_target_pairs={{0,16},{8,24},{16,0},{24,8},{1,17},{9,25},{17,1},{25,9},{2,18},{10... | collective-permute-start | bytes 3551240 | tf_op jit(solution)/shard_map/ppermute | solution.py:84
  507.4 28.5 %collective-permute-start.31 = (bf16[1,1,544,1088]{3,2,1,0:T(8,128)(2,1)S(1)}, bf16[1,1,544,1088]{3,2,1,0:T(8,128)(2,1)S(1)}, u32[]{:S(2)}, u32[]{:S(2)}) collective-permute-start(bf16[1,1,544,1088]{3,2,1,0:T(8,128)(2,1)S(1)} %constant_dynamic-slice_fusion.12), channel_id=1, source_target_pairs={{0,1},{1,0},{2,3},{3,2},{4,5},{5,4},{6,7},{7,6},{8,9},{9,8},{10,11... | collective-permute-start | bytes 3551240 | tf_op jit(solution)/shard_map/ppermute | solution.py:84
  534.3 54.9 %collective-permute-start.46 = (bf16[1,1,136,2176]{3,2,1,0:T(8,128)(2,1)}, bf16[1,1,136,2176]{3,2,1,0:T(8,128)(2,1)}, u32[]{:S(2)}, u32[]{:S(2)}) collective-permute-start(bf16[1,1,136,2176]{3,2,1,0:T(8,128)(2,1)} %constant_dynamic-slice_fusion.3), channel_id=1, source_target_pairs={{0,2},{1,3},{2,0},{3,1},{4,6},{5,7},{6,4},{7,5},{8,10},{9,11},{10,... | collective-permute-start | bytes 1775624 | tf_op jit(solution)/shard_map/ppermute | solution.py:84
  559.4 34.5 %collective-permute-start.40 = (bf16[1,1,2,136,1088]{4,3,2,1,0:T(8,128)(2,1)S(1)}, bf16[1,1,2,136,1088]{4,3,2,1,0:T(8,128)(2,1)S(1)}, u32[]{:S(2)}, u32[]{:S(2)}) collective-permute-start(bf16[1,1,2,136,1088]{4,3,2,1,0:T(8,128)(2,1)S(1)} %constant_dynamic-slice_fusion.6), channel_id=1, source_target_pairs={{0,1},{1,0},{2,3},{3,2},{4,5},{5,4},{6,7},{7,6},{8,9},{9,8},{10,11... | collective-permute-start | bytes 1775624 | tf_op jit(solution)/shard_map/ppermute | solution.py:84
  575.7 19.6 %collective-permute-start.50 = (bf16[1,1,272,1088]{3,2,1,0:T(8,128)(2,1)S(1)}, bf16[1,1,272,1088]{3,2,1,0:T(8,128)(2,1)S(1)}, u32[]{:S(2)}, u32[]{:S(2)}) collective-permute-start(bf16[1,1,272,1088]{3,2,1,0:T(8,128)(2,1)S(1)} %constant_dynamic-slice_fusion.2), channel_id=1, source_target_pairs={{0,2},{1,3},{2,0},{3,1},{4,6},{5,7},{6,4},{7,5},{8,10},{9,11},{10,... | collective-permute-start | bytes 1775624 | tf_op jit(solution)/shard_map/ppermute | solution.py:84
  581.7 95.8 %collective-permute-start.32 = (bf16[2,1,2,272,1088]{4,3,2,1,0:T(8,128)(2,1)S(1)}, bf16[2,1,2,272,1088]{4,3,2,1,0:T(8,128)(2,1)S(1)}, u32[]{:S(2)}, u32[]{:S(2)}) collective-permute-start(bf16[2,1,2,272,1088]{4,3,2,1,0:T(8,128)(2,1)S(1)} %constant_dynamic-slice_fusion.11), channel_id=1, source_target_pairs={{0,8},{8,0},{16,24},{24,16},{1,9},{9,1},{17,25},{25,17},{2,10},{10... | collective-permute-start | bytes 7102472 | tf_op jit(solution)/shard_map/ppermute | solution.py:84
  590.5 48.6 %collective-permute-start.47 = (bf16[1,1,136,2176]{3,2,1,0:T(8,128)(2,1)S(1)}, bf16[1,1,136,2176]{3,2,1,0:T(8,128)(2,1)S(1)}, u32[]{:S(2)}, u32[]{:S(2)}) collective-permute-start(bf16[1,1,136,2176]{3,2,1,0:T(8,128)(2,1)S(1)} %add_convert_fusion.18), channel_id=1, source_target_pairs={{0,4},{1,5},{2,6},{3,7},{4,0},{5,1},{6,2},{7,3},{8,12},{9,13},{10,... | collective-permute-start | bytes 1775624 | tf_op jit(solution)/shard_map/ppermute | solution.py:84
  594.1 20.3 %collective-permute-start.41 = (bf16[1,1,1,136,1088]{4,3,2,1,0:T(8,128)(2,1)S(1)}, bf16[1,1,1,136,1088]{4,3,2,1,0:T(8,128)(2,1)S(1)}, u32[]{:S(2)}, u32[]{:S(2)}) collective-permute-start(bf16[1,1,1,136,1088]{4,3,2,1,0:T(8,128)(2,1)S(1)} %constant_dynamic-slice_fusion.5), channel_id=1, source_target_pairs={{0,2},{1,3},{2,0},{3,1},{4,6},{5,7},{6,4},{7,5},{8,10},{9,11},{10,... | collective-permute-start | bytes 887816 | tf_op jit(solution)/shard_map/ppermute | solution.py:84
  595.4 61.1 %collective-permute-start.51 = (bf16[1,1,272,1088]{3,2,1,0:T(8,128)(2,1)S(1)}, bf16[1,1,272,1088]{3,2,1,0:T(8,128)(2,1)S(1)}, u32[]{:S(2)}, u32[]{:S(2)}) collective-permute-start(bf16[1,1,272,1088]{3,2,1,0:T(8,128)(2,1)S(1)} %add_convert_fusion.14), channel_id=1, source_target_pairs={{0,4},{1,5},{2,6},{3,7},{4,0},{5,1},{6,2},{7,3},{8,12},{9,13},{10,... | collective-permute-start | bytes 1775624 | tf_op jit(solution)/shard_map/ppermute | solution.py:84
  614.5 41.8 %collective-permute-start.42 = (bf16[1,1,1,136,1088]{4,3,2,1,0:T(8,128)(2,1)S(1)}, bf16[1,1,1,136,1088]{4,3,2,1,0:T(8,128)(2,1)S(1)}, u32[]{:S(2)}, u32[]{:S(2)}) collective-permute-start(bf16[1,1,1,136,1088]{4,3,2,1,0:T(8,128)(2,1)S(1)} %add_convert_fusion.20), channel_id=1, source_target_pairs={{0,4},{1,5},{2,6},{3,7},{4,0},{5,1},{6,2},{7,3},{8,12},{9,13},{10,... | collective-permute-start | bytes 887816 | tf_op jit(solution)/shard_map/ppermute | solution.py:84
  639.2 38.2 %collective-permute-start.48 = (bf16[1,1,136,2176]{3,2,1,0:T(8,128)(2,1)S(1)}, bf16[1,1,136,2176]{3,2,1,0:T(8,128)(2,1)S(1)}, u32[]{:S(2)}, u32[]{:S(2)}) collective-permute-start(bf16[1,1,136,2176]{3,2,1,0:T(8,128)(2,1)S(1)} %add_convert_fusion.17), channel_id=1, source_target_pairs={{0,2},{1,3},{2,0},{3,1},{4,6},{5,7},{6,4},{7,5},{8,10},{9,11},{10,... | collective-permute-start | bytes 1775624 | tf_op jit(solution)/shard_map/ppermute | solution.py:84
  656.4 19.3 %collective-permute-start.43 = (bf16[1,1,1,136,1088]{4,3,2,1,0:T(8,128)(2,1)S(1)}, bf16[1,1,1,136,1088]{4,3,2,1,0:T(8,128)(2,1)S(1)}, u32[]{:S(2)}, u32[]{:S(2)}) collective-permute-start(bf16[1,1,1,136,1088]{4,3,2,1,0:T(8,128)(2,1)S(1)} %add_convert_fusion.19), channel_id=1, source_target_pairs={{0,2},{1,3},{2,0},{3,1},{4,6},{5,7},{6,4},{7,5},{8,10},{9,11},{10,... | collective-permute-start | bytes 887816 | tf_op jit(solution)/shard_map/ppermute | solution.py:84
  656.6 32.4 %collective-permute-start.52 = (bf16[1,1,272,1088]{3,2,1,0:T(8,128)(2,1)S(1)}, bf16[1,1,272,1088]{3,2,1,0:T(8,128)(2,1)S(1)}, u32[]{:S(2)}, u32[]{:S(2)}) collective-permute-start(bf16[1,1,272,1088]{3,2,1,0:T(8,128)(2,1)S(1)} %add_convert_fusion.13), channel_id=1, source_target_pairs={{0,2},{1,3},{2,0},{3,1},{4,6},{5,7},{6,4},{7,5},{8,10},{9,11},{10,... | collective-permute-start | bytes 1775624 | tf_op jit(solution)/shard_map/ppermute | solution.py:84
  675.8 44.8 %collective-permute-start.44 = (bf16[1,1,2,136,1088]{4,3,2,1,0:T(8,128)(2,1)S(1)}, bf16[1,1,2,136,1088]{4,3,2,1,0:T(8,128)(2,1)S(1)}, u32[]{:S(2)}, u32[]{:S(2)}) collective-permute-start(bf16[1,1,2,136,1088]{4,3,2,1,0:T(8,128)(2,1)S(1)} %pad_maximum_fusion.11), channel_id=1, source_target_pairs={{0,1},{1,0},{2,3},{3,2},{4,5},{5,4},{6,7},{7,6},{8,9},{9,8},{10,11... | collective-permute-start | bytes 1775624 | tf_op jit(solution)/shard_map/ppermute | solution.py:84
  678.3 41.5 %collective-permute-start.33 = (bf16[2,1,2,136,1088]{4,3,2,1,0:T(8,128)(2,1)S(1)}, bf16[2,1,2,136,1088]{4,3,2,1,0:T(8,128)(2,1)S(1)}, u32[]{:S(2)}, u32[]{:S(2)}) collective-permute-start(bf16[2,1,2,136,1088]{4,3,2,1,0:T(8,128)(2,1)S(1)} %constant_dynamic-slice_fusion.10), channel_id=1, source_target_pairs={{0,1},{1,0},{2,3},{3,2},{4,5},{5,4},{6,7},{7,6},{8,9},{9,8},{10,11... | collective-permute-start | bytes 3551240 | tf_op jit(solution)/shard_map/ppermute | solution.py:84
  678.9 66.2 %collective-permute-start.49 = (bf16[1,1,136,4352]{3,2,1,0:T(8,128)(2,1)S(1)}, bf16[1,1,136,4352]{3,2,1,0:T(8,128)(2,1)S(1)}, u32[]{:S(2)}, u32[]{:S(2)}) collective-permute-start(bf16[1,1,136,4352]{3,2,1,0:T(8,128)(2,1)S(1)} %pad_maximum_fusion.5), channel_id=1, source_target_pairs={{0,1},{1,0},{2,3},{3,2},{4,5},{5,4},{6,7},{7,6},{8,9},{9,8},{10,11... | collective-permute-start | bytes 3551240 | tf_op jit(solution)/shard_map/ppermute | solution.py:84
  689.3 81.7 %collective-permute-start.53 = (bf16[1,1,544,1088]{3,2,1,0:T(8,128)(2,1)S(1)}, bf16[1,1,544,1088]{3,2,1,0:T(8,128)(2,1)S(1)}, u32[]{:S(2)}, u32[]{:S(2)}) collective-permute-start(bf16[1,1,544,1088]{3,2,1,0:T(8,128)(2,1)S(1)} %pad_maximum_fusion.4), channel_id=1, source_target_pairs={{0,1},{1,0},{2,3},{3,2},{4,5},{5,4},{6,7},{7,6},{8,9},{9,8},{10,11... | collective-permute-start | bytes 3551240 | tf_op jit(solution)/shard_map/ppermute | solution.py:84
  720.1 14.1 %collective-permute-start.34 = (bf16[1,1,2,136,1088]{4,3,2,1,0:T(8,128)(2,1)S(1)}, bf16[1,1,2,136,1088]{4,3,2,1,0:T(8,128)(2,1)S(1)}, u32[]{:S(2)}, u32[]{:S(2)}) collective-permute-start(bf16[1,1,2,136,1088]{4,3,2,1,0:T(8,128)(2,1)S(1)} %constant_dynamic-slice_fusion.9), channel_id=1, source_target_pairs={{0,16},{8,24},{16,0},{24,8},{1,17},{9,25},{17,1},{25,9},{2,18},{10... | collective-permute-start | bytes 1775624 | tf_op jit(solution)/shard_map/ppermute | solution.py:84
  734.4 11.1 %collective-permute-start.35 = (bf16[1,1,1,136,1088]{4,3,2,1,0:T(8,128)(2,1)S(1)}, bf16[1,1,1,136,1088]{4,3,2,1,0:T(8,128)(2,1)S(1)}, u32[]{:S(2)}, u32[]{:S(2)}) collective-permute-start(bf16[1,1,1,136,1088]{4,3,2,1,0:T(8,128)(2,1)S(1)} %constant_dynamic-slice_fusion.8), channel_id=1, source_target_pairs={{0,2},{1,3},{2,0},{3,1},{4,6},{5,7},{6,4},{7,5},{8,10},{9,11},{10,... | collective-permute-start | bytes 887816 | tf_op jit(solution)/shard_map/ppermute | solution.py:84
  745.6 25.8 %collective-permute-start.36 = (bf16[1,1,1,136,1088]{4,3,2,1,0:T(8,128)(2,1)S(1)}, bf16[1,1,1,136,1088]{4,3,2,1,0:T(8,128)(2,1)S(1)}, u32[]{:S(2)}, u32[]{:S(2)}) collective-permute-start(bf16[1,1,1,136,1088]{4,3,2,1,0:T(8,128)(2,1)S(1)} %add_convert_fusion.22), channel_id=1, source_target_pairs={{0,4},{1,5},{2,6},{3,7},{4,0},{5,1},{6,2},{7,3},{8,12},{9,13},{10,... | collective-permute-start | bytes 887816 | tf_op jit(solution)/shard_map/ppermute | solution.py:84
  780.1 14.2 %collective-permute-start.38 = (bf16[1,1,2,136,1088]{4,3,2,1,0:T(8,128)(2,1)S(1)}, bf16[1,1,2,136,1088]{4,3,2,1,0:T(8,128)(2,1)S(1)}, u32[]{:S(2)}, u32[]{:S(2)}) collective-permute-start(bf16[1,1,2,136,1088]{4,3,2,1,0:T(8,128)(2,1)S(1)} %pad_maximum_fusion.10), channel_id=1, source_target_pairs={{0,1},{1,0},{2,3},{3,2},{4,5},{5,4},{6,7},{7,6},{8,9},{9,8},{10,11... | collective-permute-start | bytes 1775624 | tf_op jit(solution)/shard_map/ppermute | solution.py:84
  (93 other events, 1252.7 us)

commit v3 on v2

--- a/solution.py
+++ b/solution.py
@@ -3,6 +3,7 @@
 import jax
 import jax.numpy as jnp
 from jax import lax
+from jax.experimental.layout import Layout, with_layout_constraint
 from jax.sharding import PartitionSpec as P
 
 H = 17
@@ -116,7 +117,7 @@
 
 
 def core_stage(term):
-    return halve(term.astype(jnp.bfloat16), "shard", 1, 1)
+    return halve(term, "shard", 1, 1)
 
 
 def y_stage(term):
@@ -127,24 +128,35 @@
     return halve(term, "rep", 1, dim)
 
 
-def rest_stage(term, x_dim, z_dim):
-    term = halve(term, "rep", 2, z_dim)
+def z_stage(term, dim):
+    return halve(term, "rep", 2, dim)
+
+
+def far_stage(term):
     bit = 4
     while bit < lax.axis_size("rep"):
         term = exchange_sum(term, "rep", bit)
         bit *= 2
-    term = double(term, "rep", 2, z_dim)
-    term = double(term, "rep", 1, x_dim)
+    return term
+
+
+def z_back(term, dim):
+    return double(term, "rep", 2, dim)
+
+
+def x_back(term, dim):
+    return double(term, "rep", 1, dim)
+
+
+def finish(term):
     return term.reshape(term.shape[2:]).astype(jnp.float32)
 
 
-def reduce_small(term):
-    for axis in ("shard", "rep"):
-        bit = 1
-        while bit < lax.axis_size(axis):
+def small_stage(term, axis, bits):
+    for bit in bits:
+        if bit < lax.axis_size(axis):
             term = exchange_sum(term, axis, bit)
-            bit *= 2
-    return lax.dynamic_index_in_dim(term, lax.axis_index("shard"), 0, keepdims=False)
+    return term
 
 
 def place(blocks):
@@ -244,14 +256,13 @@
     upstream_low = upstream.astype(jnp.bfloat16)
 
     def split(term):
-        return term.astype(jnp.bfloat16).reshape(2, 2, -1, term.shape[1])
+        low = with_layout_constraint(term.astype(jnp.bfloat16), Layout(major_to_minor=(0, 1)))
+        return low.reshape(2, 2, -1, term.shape[1])
 
     def paired(one, two):
         return jnp.stack([split(one), split(two)], axis=2)
 
-    down_sum = split(outer(hidden, upstream_low))
-    down_sum, full_down = tie(down_sum, full_down)
-    down_sum = core_stage(down_sum)
+    down_sum = core_stage(split(outer(hidden, upstream_low)))
     result = middle + jnp.dot(hidden, full_down, preferred_element_type=jnp.float32) + down_shift
     outputs = (result * inside[:, None]).astype(jnp.bfloat16)
     grad_hidden = inner(upstream_low, full_down)
@@ -259,19 +270,17 @@
     grad_pre = gelu_pull(grad_hidden)[0].astype(jnp.bfloat16)
     down_sum, grad_pre, outputs = tie(down_sum, grad_pre, outputs)
     down_sum = y_stage(down_sum)
-    up_sum = split(outer(normed_two, grad_pre))
-    up_sum, grad_pre = tie(up_sum, grad_pre)
-    up_sum = core_stage(up_sum)
+    up_sum = core_stage(split(outer(normed_two, grad_pre)))
     grad_normed_two = inner(grad_pre, full_up)
     _, second_pull = jax.vjp(normalize, middle, second_gain, second_shift)
     grad_middle_norm, grad_second_gain, grad_second_shift = second_pull(grad_normed_two)
     grad_middle = upstream + grad_middle_norm
     grad_branch = grad_middle.astype(jnp.bfloat16)
+    grad_mixed = inner(grad_branch, full_out).astype(jnp.bfloat16)
+    down_sum, up_sum, grad_mixed, grad_branch = tie(down_sum, up_sum, grad_mixed, grad_branch)
+    up_sum = y_stage(up_sum)
+    down_sum = x_stage(down_sum, 2)
     grad_out_term = outer(mixed, grad_branch)
-    up_sum, grad_branch = tie(up_sum, grad_branch)
-    up_sum = x_stage(up_sum, 2)
-    grad_mixed = inner(grad_branch, full_out).astype(jnp.bfloat16)
-
     width = queries.shape[0]
     query_heads = queries.reshape(width, H, HD)
     key_heads = keys.reshape(width, H, HD)
@@ -286,16 +295,19 @@
         preferred_element_type=jnp.float32,
     ).reshape(width, H * HD).astype(jnp.bfloat16)
     pair_one = paired(grad_out_term, outer(normed_one, grad_values))
-    pair_one, grad_heads = tie(pair_one, grad_heads)
+    down_sum, up_sum, pair_one, grad_heads = tie(down_sum, up_sum, pair_one, grad_heads)
     pair_one = core_stage(pair_one)
+    up_sum = x_stage(up_sum, 2)
+    down_sum = z_stage(down_sum, 2)
     grad_probs = jnp.einsum(
         "qhd,khd->hqk", grad_heads, value_heads, preferred_element_type=jnp.float32
     )
     grad_scores = probs * (grad_probs - jnp.sum(probs * grad_probs, axis=-1, keepdims=True))
     grad_scores = (grad_scores * 0.125).astype(jnp.bfloat16)
     down_sum, up_sum, pair_one, grad_scores = tie(down_sum, up_sum, pair_one, grad_scores)
-    down_sum = x_stage(down_sum, 2)
-    up_sum = y_stage(up_sum)
+    pair_one = y_stage(pair_one)
+    up_sum = z_stage(up_sum, 3)
+    down_sum = far_stage(down_sum)
     grad_queries = jnp.einsum(
         "hqk,khd->qhd", grad_scores, key_heads, preferred_element_type=jnp.float32
     ).reshape(width, H * HD).astype(jnp.bfloat16)
@@ -303,10 +315,16 @@
         "hqk,qhd->khd", grad_scores, query_heads, preferred_element_type=jnp.float32
     ).reshape(width, H * HD).astype(jnp.bfloat16)
     pair_two = paired(outer(normed_one, grad_queries), outer(normed_one, grad_keys))
-    pair_two, down_sum, grad_queries, grad_keys = tie(
-        pair_two, down_sum, grad_queries, grad_keys
+    pair_two, pair_one, up_sum, down_sum, grad_queries, grad_keys = tie(
+        pair_two, pair_one, up_sum, down_sum, grad_queries, grad_keys
     )
     pair_two = core_stage(pair_two)
+    pair_one = x_stage(pair_one, 3)
+    up_sum = far_stage(up_sum)
+    down_sum = z_back(down_sum, 2)
+    pair_two, pair_one, up_sum, down_sum, grad_queries, grad_keys = tie(
+        pair_two, pair_one, up_sum, down_sum, grad_queries, grad_keys
+    )
     grad_normed_one = (
         inner(grad_queries, full_query)
         + inner(grad_keys, full_key)
@@ -315,10 +333,6 @@
     _, first_pull = jax.vjp(normalize, residual, first_gain, first_shift)
     grad_residual_norm, grad_first_gain, grad_first_shift = first_pull(grad_normed_one)
     grad_inputs = (grad_middle + grad_residual_norm).astype(jnp.bfloat16)
-    down_total = rest_stage(down_sum, 2, 2)
-    up_total = rest_stage(up_sum, 2, 3)
-    pair_one = rest_stage(x_stage(y_stage(pair_one), 3), 3, 2)
-    pair_two = rest_stage(y_stage(x_stage(pair_two, 3)), 3, 2)
     small = [
         column_sum(grad_queries),
         column_sum(grad_values),
@@ -334,7 +348,32 @@
         [item.astype(jnp.bfloat16).astype(jnp.float32).reshape(count, -1) for item in small],
         axis=1,
     )
-    owned = reduce_small(packed)
+    pair_two = y_stage(pair_two)
+    pair_one = z_stage(pair_one, 2)
+    up_sum = z_back(up_sum, 3)
+    down_total = finish(x_back(down_sum, 2))
+    pair_two, pair_one, up_sum, packed, grad_inputs = tie(
+        pair_two, pair_one, up_sum, packed, grad_inputs
+    )
+    pair_two = x_stage(pair_two, 3)
+    pair_one = far_stage(pair_one)
+    up_total = finish(x_back(up_sum, 2))
+    packed = small_stage(packed, "shard", (1,))
+    pair_two, pair_one, packed = tie(pair_two, pair_one, packed)
+    pair_two = z_stage(pair_two, 2)
+    pair_one = z_back(pair_one, 2)
+    packed = small_stage(packed, "shard", (2,))
+    pair_two, pair_one, packed = tie(pair_two, pair_one, packed)
+    pair_two = far_stage(pair_two)
+    pair_one = finish(x_back(pair_one, 3))
+    packed = small_stage(packed, "rep", (1,))
+    pair_two, packed = tie(pair_two, packed)
+    pair_two = z_back(pair_two, 2)
+    packed = small_stage(packed, "rep", (2,))
+    pair_two, packed = tie(pair_two, packed)
+    pair_two = finish(x_back(pair_two, 3))
+    packed = small_stage(packed, "rep", (4, 8, 16, 32, 64, 128))
+    owned = lax.dynamic_index_in_dim(packed, lax.axis_index("shard"), 0, keepdims=False)
     pieces = []
     start = 0
     for item in small:

time: 802 us -> 643 us (0.80)
  waiting for transfers between devices: 353 us -> 261 us
  local copies, waits for them, and re-layouts: 124 us -> 82.5 us
  matrix products: 187 us -> 164 us
  starting transfers between devices: 56.5 us -> 47.1 us
    ppermute x59, waiting for transfers between devices: 353 us -> 261 us  [swap(): return lax.ppermute(value, axis, [(i, i ^ bit) for i in range(size)])]
    optimization_barrier x1 -> x0, local copies, waits for them, and re-layouts: 28.9 us -> none  [tie(): return lax.optimization_barrier(values)]
    reshape x1 -> x0, local copies, waits for them, and re-layouts: 16.9 us -> none  [split(): return term.astype(jnp.bfloat16).reshape(2, 2, -1, term.shape[1])]
    ppermute x59, starting transfers between devices: 56.5 us -> 47.1 us  [swap(): return lax.ppermute(value, axis, [(i, i ^ bit) for i in range(size)])]
    dot_general x6, matrix products: 40.8 us -> 32.3 us  [inner(): lax.dot_general(left, right, (((1,), (1,)), ((), ())), preferred_element_...]
  transfers between devices with their start and end apart: 59 -> 59, of which waited for: 27 -> 32; matrix products, arithmetic and copies ran while one was open for 34% -> 42% of each run, Pallas kernels for 0% -> 0%
where the time goes in v3:
time: 643 us; the launch traced here: 638 us
  waiting for transfers between devices  261 us (41%)
  matrix products  164 us (26%)
  local copies, waits for them, and re-layouts  82.5 us (13%)
  other arithmetic  81 us (13%)
  starting transfers between devices  47.1 us (7%)
    ppermute x59, waiting for transfers between devices, swap(): return lax.ppermute(value, axis, [(i, i ^ bit) for i in range(size)])  261 us
    ppermute x59, starting transfers between devices, swap(): return lax.ppermute(value, axis, [(i, i ^ bit) for i in range(size)])  47.1 us
    dot_general x1, matrix products, shards(): jnp.dot(normed_two, full_up, preferred_element_type=jnp.float32) + up_shift  35 us
    convert_element_type x16, other arithmetic, halve(): (keep.astype(jnp.float32) + got.astype(jnp.float32)).astype(value.dtype)  32.6 us
    dot_general x6, matrix products, inner(): lax.dot_general(left, right, (((1,), (1,)), ((), ())), preferred_element_...  32.3 us
    sub x1, matrix products, shards(): grad_probs - jnp.sum(probs * grad_probs, axis=-1, keepdims=True)  23.7 us
    dot_general x6, matrix products, outer(): lax.dot_general(left, right, (((0,), (0,)), ((), ())), preferred_element_...  23.2 us
    dynamic_update_slice x22, local copies, waits for them, and re-layouts, place(): full = lax.dynamic_update_slice_in_dim(full, block, (me ^ offset) * rows, 0)  18.1 us
  transfers between devices with their start and end apart: 59, of which 32 were waited for; matrix products, arithmetic and copies ran while one was open for 42% of the time, Pallas kernels for 0%

profile of v3, /device:TPU:0, one launch (start us, length us, event | category | flops | bytes accessed | tf_op | source)
XLA Modules:
  0.0 638.5 jit_solution(5874511793703061512)
XLA Ops:
  0.7 6.4 %concatenate.54 = bf16[3264]{0:T(1024)(128)(2,1)S(1)} concatenate(bf16[272]{0:T(512)(128)(2,1)} %param.26, bf16[272]{0:T(512)(128)(2,1)} %param.27, bf16[272]{0:T(512)(128)(2,1)} %param.28, bf16[272]{0:T(512)(128)(2,1)} %param.31, bf16[272]{0:T(512)(128)(2,1)} %param.32, bf16[1088]{0:T(1024)(128)(2,1)} %param.29, bf16[272]{0:T(512)(128)(2,1)} %param.30, bf16[272]{0:T(512)(128)(2,1)} %param.33, ...), dimensions={0} | concatenate | bytes 13056 | tf_op jit(solution)/shard_map/concatenate | solution.py:217
  7.1 3.0 collective-permute-start
  36.2 4.2 broadcast_in_dim.88
  40.4 3.2 constant_dynamic-update-slice_fusion.7
  46.8 6.9 %collective-permute-done.4 = bf16[136,1088]{1,0:T(8,128)(2,1)S(1)} collective-permute-done((bf16[136,1088]{1,0:T(8,128)(2,1)}, bf16[136,1088]{1,0:T(8,128)(2,1)S(1)}, u32[]{:S(2)}, u32[]{:S(2)}) %collective-permute-start.4) | collective-permute-done | bytes 295968 | tf_op jit(solution)/shard_map/ppermute | solution.py:85
  56.2 6.6 %collective-permute-done.12 = bf16[136,1088]{1,0:T(8,128)(2,1)S(1)} collective-permute-done((bf16[136,1088]{1,0:T(8,128)(2,1)S(1)}, bf16[136,1088]{1,0:T(8,128)(2,1)S(1)}, u32[]{:S(2)}, u32[]{:S(2)}) %collective-permute-start.12) | collective-permute-done | bytes 295968 | tf_op jit(solution)/shard_map/ppermute | solution.py:85
  64.4 6.7 %collective-permute-done.8 = bf16[136,1088]{1,0:T(8,128)(2,1)S(1)} collective-permute-done((bf16[136,1088]{1,0:T(8,128)(2,1)S(1)}, bf16[136,1088]{1,0:T(8,128)(2,1)S(1)}, u32[]{:S(2)}, u32[]{:S(2)}) %collective-permute-start.8) | collective-permute-done | bytes 295968 | tf_op jit(solution)/shard_map/ppermute | solution.py:85
  75.9 5.5 collective-permute-done.15
  83.1 8.1 %collective-permute-done.16 = bf16[136,1088]{1,0:T(8,128)(2,1)S(1)} collective-permute-done((bf16[136,1088]{1,0:T(8,128)(2,1)S(1)}, bf16[136,1088]{1,0:T(8,128)(2,1)S(1)}, u32[]{:S(2)}, u32[]{:S(2)}) %collective-permute-start.16) | collective-permute-done | bytes 295968 | tf_op jit(solution)/shard_map/ppermute | solution.py:85
  101.7 8.4 %fusion.68 = (f32[17,512]{1,0:T(8,128)S(1)}, f32[17,512,512]{1,2,0:T(8,128)}) fusion(bf16[512,17,64]{0,2,1:T(8,128)(2,1)S(1)} %bitcast.100, bf16[512,17,64]{0,2,1:T(8,128)(2,1)S(1)} %bitcast.95, pred[512,512]{0,1:T(8,128)(4,1)S(1)} %copy-done.59), kind=kOutput, calls=%fused_computation.234 | convolution fusion | flops 583785984 | bytes 20350976 | tf_op jit(solution)/shard_map/while/body/eval_jaxpr/qhd,khd->hqk/dot_general | solution.py:50
  110.1 8.8 %fusion.2 = f32[17,512]{1,0:T(8,128)S(1)} fusion(f32[17,512,512]{1,2,0:T(8,128)} %get-tuple-element.201, f32[17,512]{1,0:T(8,128)S(1)} %get-tuple-element.200), kind=kLoop, calls=%fused_computation.10 | loop fusion | flops 8904192 | bytes 17895424 | tf_op jit(solution)/shard_map/while/body/eval_jaxpr/reduce_sum | solution.py:68
  119.0 9.7 %fusion.40 = bf16[17,64,512]{2,1,0:T(8,128)(2,1)S(1)} fusion(bf16[512,17,64]{0,2,1:T(8,128)(2,1)} %bitcast.114, f32[17,512,512]{1,2,0:T(8,128)} %get-tuple-element.201, f32[17,512]{1,0:T(8,128)S(1)} %fusion.2, f32[17,512]{1,0:T(8,128)S(1)} %get-tuple-element.200), kind=kOutput, calls=%fused_computation.93 | convolution fusion | flops 584351744 | bytes 20123648 | tf_op jit(solution)/shard_map/while/body/eval_jaxpr/hqk,khd->qhd/dot_general | solution.py:70
  136.1 24.1 %collective-permute-done.24 = bf16[544,1088]{1,0:T(8,128)(2,1)} collective-permute-done((bf16[544,1088]{1,0:T(8,128)(2,1)}, bf16[544,1088]{1,0:T(8,128)(2,1)}, u32[]{:S(2)}, u32[]{:S(2)}) %collective-permute-start.24) | collective-permute-done | bytes 1183776 | tf_op jit(solution)/shard_map/ppermute | solution.py:85
  161.7 3.3 constant_dynamic-update-slice_fusion.6
  170.6 19.0 %collective-permute-done.25 = bf16[544,1088]{1,0:T(8,128)(2,1)S(1)} collective-permute-done((bf16[544,1088]{1,0:T(8,128)(2,1)}, bf16[544,1088]{1,0:T(8,128)(2,1)S(1)}, u32[]{:S(2)}, u32[]{:S(2)}) %collective-permute-start.25) | collective-permute-done | bytes 1183776 | tf_op jit(solution)/shard_map/ppermute | solution.py:85
  194.9 35.0 %multiply_convert_fusion.1 = (bf16[512,4352]{1,0:T(8,128)(2,1)}, f32[512,4352]{1,0:T(8,128)}, f32[512,4352]{1,0:T(8,128)}) fusion(f32[4352]{0:T(1024)S(1)} %copy-done.75, bf16[1088,4352]{1,0:T(8,128)(2,1)} %constant_dynamic-update-slice_fusion.4, f32[512,1088]{0,1:T(8,128)S(1)} %get-tuple-element.203, f32[1088]{0:T(1024)S(1)} %copy-done.83, ...), kind=kOutput, calls=%fused_computation.20 | convolution fusion | flops 4998463488 | bytes 34010624 | tf_op jit(solution)/shard_map/dot_general | solution.py:253
  229.9 9.9 %convolution_convert_fusion.1 = bf16[4352,1088]{1,0:T(8,128)(2,1)S(1)} fusion(bf16[512,4352]{1,0:T(8,128)(2,1)} %get-tuple-element.144, bf16[512,1088]{0,1:T(8,128)(2,1)S(1)} %copy-done.7, f32[512]{0:T(512)S(1)} %fusion.54), kind=kOutput, calls=%fused_computation.2 | convolution fusion | flops 4855021568 | bytes 15042560 | tf_op jit(solution)/shard_map/dot_general | solution.py:32
  239.9 3.0 constant_dynamic-slice_fusion.18
  246.2 3.5 constant_dynamic-update-slice_fusion
  249.7 10.1 %fusion.27 = bf16[512,1088]{0,1:T(8,128)(2,1)} fusion(f32[512,1088]{0,1:T(8,128)S(1)} %get-tuple-element.203, bf16[512,4352]{1,0:T(8,128)(2,1)S(1)} %copy-done.90, bf16[4352,1088]{1,0:T(8,128)(2,1)} %constant_dynamic-update-slice_fusion, f32[1088]{0:T(1024)S(1)} %add.431, f32[512]{0:T(512)S(1)} %fusion.54), kind=kOutput, calls=%fused_computation.66 | convolution fusion | flops 4850843648 | bytes 17275136 | tf_op jit(solution)/shard_map/dot_general | solution.py:266
  259.8 13.4 %add_convert_fusion.2 = bf16[512,4352]{1,0:T(8,128)(2,1)S(1)} fusion(f32[512,4352]{1,0:T(8,128)} %get-tuple-element.145, f32[512,4352]{1,0:T(8,128)} %get-tuple-element.204, f32[4352]{0:T(1024)S(1)} %copy-done.75, bf16[4352,1088]{1,0:T(8,128)(2,1)} %constant_dynamic-update-slice_fusion, bf16[512,1088]{0,1:T(8,128)(2,1)S(1)} %copy-done.7, f32[512]{0:T(512)S(1)} %fusion.54), kind=kOutput, calls=%fused_computation.19 | convolution fusion | flops 4883709952 | bytes 32885760 | tf_op jit(solution)/shard_map/dot_general | solution.py:38
  273.3 6.7 %add_convert_fusion = bf16[2,1,1088,1088]{3,2,1,0:T(8,128)(2,1)S(1)} fusion(bf16[2,1,1088,1088]{3,2,1,0:T(8,128)(2,1)} %collective-permute-done.22, bf16[2,2,1088,1088]{3,2,1,0:T(8,128)(2,1)} %bitcast.92, s32[]{:T(128)S(6)} %select_n.435), kind=kLoop, calls=%fused_computation.13 | loop fusion | flops 9469952 | bytes 14204932 | tf_op jit(solution)/shard_map/convert_element_type | solution.py:102
  283.5 5.8 convolution_convert_fusion
  294.7 10.6 %multiply_reduce_fusion.1 = (bf16[1088]{0:T(1024)(128)(2,1)S(1)}, f32[512]{0:T(512)S(1)}, bf16[1088]{0:T(1024)(128)(2,1)S(1)}, f32[512,1088]{0,1:T(8,128)}) fusion(f32[512,1088]{0,1:T(8,128)S(1)} %get-tuple-element.203, f32[512]{0:T(512)S(1)} %fusion.56, f32[512]{0:T(512)S(1)} %broadcast_multiply_fusion, f32[1088]{0:T(1024)S(1)} %copy-done.73, ...), kind=kOutput, calls=%fused_computation.85 | convolution fusion | flops 4853069312 | bytes 18397696 | tf_op jit(solution)/shard_map/dot_general | solution.py:38
  305.5 3.2 reduce_sum.256
  315.0 25.2 %collective-permute-done.27 = bf16[1,1,1088,1088]{3,2,1,0:T(8,128)(2,1)} collective-permute-done((bf16[1,1,1088,1088]{3,2,1,0:T(8,128)(2,1)}, bf16[1,1,1088,1088]{3,2,1,0:T(8,128)(2,1)}, u32[]{:S(2)}, u32[]{:S(2)}) %collective-permute-start.27) | collective-permute-done | bytes 2367520 | tf_op jit(solution)/shard_map/ppermute | solution.py:85
  342.7 5.8 add_convert_fusion.1
  352.1 9.1 %fusion.70 = (bf16[17,64]{1,0:T(8,128)(2,1)S(1)}, bf16[17,64,512]{2,1,0:T(8,128)(2,1)S(1)}) fusion(bf16[512,17,64]{0,2,1:T(8,128)(2,1)S(1)} %bitcast.108, f32[17,512,512]{1,2,0:T(8,128)} %get-tuple-element.201, f32[17,512]{1,0:T(8,128)S(1)} %log_add_fusion), kind=kOutput, calls=%fused_computation.236 | convolution fusion | flops 580451264 | bytes 20091008 | tf_op jit(solution)/shard_map/hqk,qhd->khd/dot_general | solution.py:291
  365.8 12.2 %collective-permute-done.29 = bf16[1,1,544,1088]{3,2,1,0:T(8,128)(2,1)} collective-permute-done((bf16[1,1,544,1088]{3,2,1,0:T(8,128)(2,1)S(1)}, bf16[1,1,544,1088]{3,2,1,0:T(8,128)(2,1)}, u32[]{:S(2)}, u32[]{:S(2)}) %collective-permute-start.29) | collective-permute-done | bytes 1183776 | tf_op jit(solution)/shard_map/ppermute | solution.py:85
  379.6 25.2 %collective-permute-done.30 = bf16[1,1,272,4352]{3,2,1,0:T(8,128)(2,1)} collective-permute-done((bf16[1,1,272,4352]{3,2,1,0:T(8,128)(2,1)}, bf16[1,1,272,4352]{3,2,1,0:T(8,128)(2,1)}, u32[]{:S(2)}, u32[]{:S(2)}) %collective-permute-start.30) | collective-permute-done | bytes 2367520 | tf_op jit(solution)/shard_map/ppermute | solution.py:85
  412.9 23.7 %multiply_convert_fusion = bf16[17,512,512]{1,2,0:T(8,128)(2,1)} fusion(f32[17,512,512]{1,2,0:T(8,128)} %get-tuple-element.201, f32[17,512]{1,0:T(8,128)S(1)} %log_add_fusion, bf16[512,17,64]{0,2,1:T(8,128)(2,1)} %bitcast.109, bf16[512,17,64]{0,2,1:T(8,128)(2,1)} %bitcast.115), kind=kOutput, calls=%fused_computation.3 | convolution fusion | flops 1172055040 | bytes 29001728 | tf_op jit(solution)/shard_map/sub | solution.py:305
  440.2 3.9 add_convert_fusion.4
  456.6 19.4 %collective-permute-done.36 = bf16[1,1,272,1088]{3,2,1,0:T(8,128)(2,1)S(1)} collective-permute-done((bf16[1,1,272,1088]{3,2,1,0:T(8,128)(2,1)S(1)}, bf16[1,1,272,1088]{3,2,1,0:T(8,128)(2,1)S(1)}, u32[]{:S(2)}, u32[]{:S(2)}) %collective-permute-start.36) | collective-permute-done | bytes 591904 | tf_op jit(solution)/shard_map/ppermute | solution.py:85
  486.0 3.0 fusion.72
  490.6 3.1 collective-permute-start.39
  496.4 7.2 %collective-permute-done.40 = bf16[1,1,272,1088]{3,2,1,0:T(8,128)(2,1)} collective-permute-done((bf16[1,1,272,1088]{3,2,1,0:T(8,128)(2,1)}, bf16[1,1,272,1088]{3,2,1,0:T(8,128)(2,1)}, u32[]{:S(2)}, u32[]{:S(2)}) %collective-permute-start.40) | collective-permute-done | bytes 591904 | tf_op jit(solution)/shard_map/ppermute | solution.py:85
  506.2 5.0 collective-permute-done.38
  511.4 9.3 %collective-permute-done.39 = bf16[1,1,136,2176]{3,2,1,0:T(8,128)(2,1)S(1)} collective-permute-done((bf16[1,1,136,2176]{3,2,1,0:T(8,128)(2,1)}, bf16[1,1,136,2176]{3,2,1,0:T(8,128)(2,1)S(1)}, u32[]{:S(2)}, u32[]{:S(2)}) %collective-permute-start.39) | collective-permute-done | bytes 591904 | tf_op jit(solution)/shard_map/ppermute | solution.py:85
  543.8 10.6 %collective-permute-done.43 = bf16[1,1,136,2176]{3,2,1,0:T(8,128)(2,1)} collective-permute-done((bf16[1,1,136,2176]{3,2,1,0:T(8,128)(2,1)}, bf16[1,1,136,2176]{3,2,1,0:T(8,128)(2,1)}, u32[]{:S(2)}, u32[]{:S(2)}) %collective-permute-start.43) | collective-permute-done | bytes 591904 | tf_op jit(solution)/shard_map/ppermute | solution.py:85
  555.8 11.4 %collective-permute-done.41 = bf16[1,1,2,272,1088]{4,3,2,1,0:T(8,128)(2,1)S(1)} collective-permute-done((bf16[1,1,2,272,1088]{4,3,2,1,0:T(8,128)(2,1)}, bf16[1,1,2,272,1088]{4,3,2,1,0:T(8,128)(2,1)S(1)}, u32[]{:S(2)}, u32[]{:S(2)}) %collective-permute-start.41) | collective-permute-done | bytes 1183776 | tf_op jit(solution)/shard_map/ppermute | solution.py:85
  570.4 12.5 %collective-permute-done.45 = bf16[1,1,1,136,1088]{4,3,2,1,0:T(8,128)(2,1)S(1)} collective-permute-done((bf16[1,1,1,136,1088]{4,3,2,1,0:T(8,128)(2,1)S(1)}, bf16[1,1,1,136,1088]{4,3,2,1,0:T(8,128)(2,1)S(1)}, u32[]{:S(2)}, u32[]{:S(2)}) %collective-permute-start.45) | collective-permute-done | bytes 295968 | tf_op jit(solution)/shard_map/ppermute | solution.py:85
  587.7 3.0 collective-permute-done.49
  590.8 4.5 collective-permute-done.48
  595.4 3.4 collective-permute-done.47
  603.8 7.5 %collective-permute-done.51 = f32[4,3264]{1,0:T(4,128)S(1)} collective-permute-done((f32[4,3264]{1,0:T(4,128)S(1)}, f32[4,3264]{1,0:T(4,128)S(1)}, u32[]{:S(2)}, u32[]{:S(2)}) %collective-permute-start.51) | collective-permute-done | bytes 52256 | tf_op jit(solution)/shard_map/ppermute | solution.py:85
  618.0 3.9 collective-permute-done.52
  623.8 3.4 collective-permute-done.58
  628.6 7.0 %collective-permute-done.54 = bf16[1,1,2,136,1088]{4,3,2,1,0:T(8,128)(2,1)S(1)} collective-permute-done((bf16[1,1,2,136,1088]{4,3,2,1,0:T(8,128)(2,1)S(1)}, bf16[1,1,2,136,1088]{4,3,2,1,0:T(8,128)(2,1)S(1)}, u32[]{:S(2)}, u32[]{:S(2)}) %collective-permute-start.54) | collective-permute-done | bytes 591904 | tf_op jit(solution)/shard_map/ppermute | solution.py:85
  (443 shorter events, 191.5 us)
Async XLA Ops:
  7.1 17.9 %collective-permute-start = (bf16[1,3264]{1,0:T(2,128)(2,1)S(1)}, bf16[1,3264]{1,0:T(2,128)(2,1)S(1)}, u32[]{:S(2)}, u32[]{:S(2)}) collective-permute-start(bf16[1,3264]{1,0:T(2,128)(2,1)S(1)} %broadcast_in_dim.85), channel_id=1, source_target_pairs={{0,16},{8,24},{16,0},{24,8},{1,17},{9,25},{17,1},{25,9},{2,18},{10... | collective-permute-start | bytes 19592 | tf_op jit(solution)/shard_map/ppermute | solution.py:85
  11.1 22.3 %collective-permute-start.3 = (bf16[136,1088]{1,0:T(8,128)(2,1)S(1)}, bf16[136,1088]{1,0:T(8,128)(2,1)}, u32[]{:S(2)}, u32[]{:S(2)}) collective-permute-start(bf16[136,1088]{1,0:T(8,128)(2,1)S(1)} %constant_dynamic-slice_fusion.23), channel_id=1, source_target_pairs={{0,16},{8,24},{16,0},{24,8},{1,17},{9,25},{17,1},{25,9},{2,18},{10... | collective-permute-start | bytes 887816 | tf_op jit(solution)/shard_map/ppermute | solution.py:85
  11.2 59.9 %collective-permute-start.10 = (bf16[272,1088]{1,0:T(8,128)(2,1)}, bf16[272,1088]{1,0:T(8,128)(2,1)}, u32[]{:S(2)}, u32[]{:S(2)}) collective-permute-start(bf16[272,1088]{1,0:T(8,128)(2,1)} %param.21), channel_id=1, source_target_pairs={{0,8},{8,0},{16,24},{24,16},{1,9},{9,1},{17,25},{25,17},{2,10},{10... | collective-permute-start | bytes 1775624 | tf_op jit(solution)/shard_map/ppermute | solution.py:85
  13.0 20.5 %collective-permute-start.11 = (bf16[136,1088]{1,0:T(8,128)(2,1)}, bf16[136,1088]{1,0:T(8,128)(2,1)S(1)}, u32[]{:S(2)}, u32[]{:S(2)}) collective-permute-start(bf16[136,1088]{1,0:T(8,128)(2,1)} %constant_dynamic-slice_fusion.21), channel_id=1, source_target_pairs={{0,16},{8,24},{16,0},{24,8},{1,17},{9,25},{17,1},{25,9},{2,18},{10... | collective-permute-start | bytes 887816 | tf_op jit(solution)/shard_map/ppermute | solution.py:85
  14.9 57.8 %collective-permute-start.6 = (bf16[272,1088]{1,0:T(8,128)(2,1)}, bf16[272,1088]{1,0:T(8,128)(2,1)}, u32[]{:S(2)}, u32[]{:S(2)}) collective-permute-start(bf16[272,1088]{1,0:T(8,128)(2,1)} %param.20), channel_id=1, source_target_pairs={{0,8},{8,0},{16,24},{24,16},{1,9},{9,1},{17,25},{25,17},{2,10},{10... | collective-permute-start | bytes 1775624 | tf_op jit(solution)/shard_map/ppermute | solution.py:85
  33.4 48.0 %collective-permute-start.2 = (bf16[272,1088]{1,0:T(8,128)(2,1)S(1)}, bf16[272,1088]{1,0:T(8,128)(2,1)S(1)}, u32[]{:S(2)}, u32[]{:S(2)}) collective-permute-start(bf16[272,1088]{1,0:T(8,128)(2,1)S(1)} %copy-done.52), channel_id=1, source_target_pairs={{0,8},{8,0},{16,24},{24,16},{1,9},{9,1},{17,25},{25,17},{2,10},{10... | collective-permute-start | bytes 1775624 | tf_op jit(solution)/shard_map/ppermute | solution.py:85
  36.1 55.2 %collective-permute-start.14 = (bf16[272,1088]{1,0:T(8,128)(2,1)S(1)}, bf16[272,1088]{1,0:T(8,128)(2,1)S(1)}, u32[]{:S(2)}, u32[]{:S(2)}) collective-permute-start(bf16[272,1088]{1,0:T(8,128)(2,1)S(1)} %copy-done.53), channel_id=1, source_target_pairs={{0,8},{8,0},{16,24},{24,16},{1,9},{9,1},{17,25},{25,17},{2,10},{10... | collective-permute-start | bytes 1775624 | tf_op jit(solution)/shard_map/ppermute | solution.py:85
  43.6 10.1 %collective-permute-start.4 = (bf16[136,1088]{1,0:T(8,128)(2,1)}, bf16[136,1088]{1,0:T(8,128)(2,1)S(1)}, u32[]{:S(2)}, u32[]{:S(2)}) collective-permute-start(bf16[136,1088]{1,0:T(8,128)(2,1)} %collective-permute-done.3), channel_id=1, source_target_pairs={{0,1},{1,0},{2,3},{3,2},{4,5},{5,4},{6,7},{7,6},{8,9},{9,8},{10,11... | collective-permute-start | bytes 887816 | tf_op jit(solution)/shard_map/ppermute | solution.py:85
  71.1 90.7 %collective-permute-start.18 = (bf16[272,4352]{1,0:T(8,128)(2,1)}, bf16[272,4352]{1,0:T(8,128)(2,1)}, u32[]{:S(2)}, u32[]{:S(2)}) collective-permute-start(bf16[272,4352]{1,0:T(8,128)(2,1)} %param.24), channel_id=1, source_target_pairs={{0,8},{8,0},{16,24},{24,16},{1,9},{9,1},{17,25},{25,17},{2,10},{10... | collective-permute-start | bytes 7102472 | tf_op jit(solution)/shard_map/ppermute | solution.py:85
  71.1 10.3 %collective-permute-start.15 = (bf16[136,1088]{1,0:T(8,128)(2,1)S(1)}, bf16[136,1088]{1,0:T(8,128)(2,1)S(1)}, u32[]{:S(2)}, u32[]{:S(2)}) collective-permute-start(bf16[136,1088]{1,0:T(8,128)(2,1)S(1)} %constant_dynamic-slice_fusion.20), channel_id=1, source_target_pairs={{0,16},{8,24},{16,0},{24,8},{1,17},{9,25},{17,1},{25,9},{2,18},{10... | collective-permute-start | bytes 887816 | tf_op jit(solution)/shard_map/ppermute | solution.py:85
  72.7 56.0 %collective-permute-start.19 = (bf16[136,4352]{1,0:T(8,128)(2,1)S(1)}, bf16[136,4352]{1,0:T(8,128)(2,1)}, u32[]{:S(2)}, u32[]{:S(2)}) collective-permute-start(bf16[136,4352]{1,0:T(8,128)(2,1)S(1)} %constant_dynamic-slice_fusion.19), channel_id=1, source_target_pairs={{0,16},{8,24},{16,0},{24,8},{1,17},{9,25},{17,1},{25,9},{2,18},{10... | collective-permute-start | bytes 3551240 | tf_op jit(solution)/shard_map/ppermute | solution.py:85
  81.4 11.5 %collective-permute-start.13 = (bf16[272,1088]{1,0:T(8,128)(2,1)S(1)}, bf16[272,1088]{1,0:T(8,128)(2,1)S(1)}, u32[]{:S(2)}, u32[]{:S(2)}) collective-permute-start(bf16[272,1088]{1,0:T(8,128)(2,1)S(1)} %get-tuple-element.178), channel_id=1, source_target_pairs={{0,8},{8,0},{16,24},{24,16},{1,9},{9,1},{17,25},{25,17},{2,10},{10... | collective-permute-start | bytes 1775624 | tf_op jit(solution)/shard_map/ppermute | solution.py:85
  81.4 9.8 %collective-permute-start.16 = (bf16[136,1088]{1,0:T(8,128)(2,1)S(1)}, bf16[136,1088]{1,0:T(8,128)(2,1)S(1)}, u32[]{:S(2)}, u32[]{:S(2)}) collective-permute-start(bf16[136,1088]{1,0:T(8,128)(2,1)S(1)} %collective-permute-done.15), channel_id=1, source_target_pairs={{0,1},{1,0},{2,3},{3,2},{4,5},{5,4},{6,7},{7,6},{8,9},{9,8},{10,11... | collective-permute-start | bytes 887816 | tf_op jit(solution)/shard_map/ppermute | solution.py:85
  92.9 37.2 %collective-permute-start.17 = (bf16[272,1088]{1,0:T(8,128)(2,1)}, bf16[272,1088]{1,0:T(8,128)(2,1)S(1)}, u32[]{:S(2)}, u32[]{:S(2)}) collective-permute-start(bf16[272,1088]{1,0:T(8,128)(2,1)} %get-tuple-element.174), channel_id=1, source_target_pairs={{0,8},{8,0},{16,24},{24,16},{1,9},{9,1},{17,25},{25,17},{2,10},{10... | collective-permute-start | bytes 1775624 | tf_op jit(solution)/shard_map/ppermute | solution.py:85
  128.8 39.8 %collective-permute-start.23 = (bf16[1088,1088]{1,0:T(8,128)(2,1)S(1)}, bf16[1088,1088]{1,0:T(8,128)(2,1)}, u32[]{:S(2)}, u32[]{:S(2)}) collective-permute-start(bf16[1088,1088]{1,0:T(8,128)(2,1)S(1)} %copy-done.23), channel_id=1, source_target_pairs={{0,8},{8,0},{16,24},{24,16},{1,9},{9,1},{17,25},{25,17},{2,10},{10... | collective-permute-start | bytes 7102472 | tf_op jit(solution)/shard_map/ppermute | solution.py:85
  130.0 30.3 %collective-permute-start.24 = (bf16[544,1088]{1,0:T(8,128)(2,1)}, bf16[544,1088]{1,0:T(8,128)(2,1)}, u32[]{:S(2)}, u32[]{:S(2)}) collective-permute-start(bf16[544,1088]{1,0:T(8,128)(2,1)} %constant_dynamic-slice_fusion.17), channel_id=1, source_target_pairs={{0,16},{8,24},{16,0},{24,8},{1,17},{9,25},{17,1},{25,9},{2,18},{10... | collective-permute-start | bytes 3551240 | tf_op jit(solution)/shard_map/ppermute | solution.py:85
  133.1 31.9 %collective-permute-start.20 = (bf16[136,4352]{1,0:T(8,128)(2,1)}, bf16[136,4352]{1,0:T(8,128)(2,1)}, u32[]{:S(2)}, u32[]{:S(2)}) collective-permute-start(bf16[136,4352]{1,0:T(8,128)(2,1)} %collective-permute-done.19), channel_id=1, source_target_pairs={{0,1},{1,0},{2,3},{3,2},{4,5},{5,4},{6,7},{7,6},{8,9},{9,8},{10,11... | collective-permute-start | bytes 3551240 | tf_op jit(solution)/shard_map/ppermute | solution.py:85
  160.2 29.4 %collective-permute-start.25 = (bf16[544,1088]{1,0:T(8,128)(2,1)}, bf16[544,1088]{1,0:T(8,128)(2,1)S(1)}, u32[]{:S(2)}, u32[]{:S(2)}) collective-permute-start(bf16[544,1088]{1,0:T(8,128)(2,1)} %collective-permute-done.24), channel_id=1, source_target_pairs={{0,1},{1,0},{2,3},{3,2},{4,5},{5,4},{6,7},{7,6},{8,9},{9,8},{10,11... | collective-permute-start | bytes 3551240 | tf_op jit(solution)/shard_map/ppermute | solution.py:85
  168.5 24.5 %collective-permute-start.21 = (bf16[272,4352]{1,0:T(8,128)(2,1)S(1)}, bf16[272,4352]{1,0:T(8,128)(2,1)S(1)}, u32[]{:S(2)}, u32[]{:S(2)}) collective-permute-start(bf16[272,4352]{1,0:T(8,128)(2,1)S(1)} %get-tuple-element.158), channel_id=1, source_target_pairs={{0,8},{8,0},{16,24},{24,16},{1,9},{9,1},{17,25},{25,17},{2,10},{10... | collective-permute-start | bytes 7102472 | tf_op jit(solution)/shard_map/ppermute | solution.py:85
  193.0 53.2 %collective-permute-start.26 = (bf16[1088,1088]{1,0:T(8,128)(2,1)}, bf16[1088,1088]{1,0:T(8,128)(2,1)}, u32[]{:S(2)}, u32[]{:S(2)}) collective-permute-start(bf16[1088,1088]{1,0:T(8,128)(2,1)} %get-tuple-element.152), channel_id=1, source_target_pairs={{0,8},{8,0},{16,24},{24,16},{1,9},{9,1},{17,25},{25,17},{2,10},{10... | collective-permute-start | bytes 7102472 | tf_op jit(solution)/shard_map/ppermute | solution.py:85
  245.1 28.1 %collective-permute-start.22 = (bf16[2,1,1088,1088]{3,2,1,0:T(8,128)(2,1)}, bf16[2,1,1088,1088]{3,2,1,0:T(8,128)(2,1)}, u32[]{:S(2)}, u32[]{:S(2)}) collective-permute-start(bf16[2,1,1088,1088]{3,2,1,0:T(8,128)(2,1)} %constant_dynamic-slice_fusion.18), channel_id=1, source_target_pairs={{0,8},{8,0},{16,24},{24,16},{1,9},{9,1},{17,25},{25,17},{2,10},{10... | collective-permute-start | bytes 14204936 | tf_op jit(solution)/shard_map/ppermute | solution.py:85
  283.0 57.2 %collective-permute-start.27 = (bf16[1,1,1088,1088]{3,2,1,0:T(8,128)(2,1)}, bf16[1,1,1088,1088]{3,2,1,0:T(8,128)(2,1)}, u32[]{:S(2)}, u32[]{:S(2)}) collective-permute-start(bf16[1,1,1088,1088]{3,2,1,0:T(8,128)(2,1)} %constant_dynamic-slice_fusion.16), channel_id=1, source_target_pairs={{0,16},{8,24},{16,0},{24,8},{1,17},{9,25},{17,1},{25,9},{2,18},{10... | collective-permute-start | bytes 7102472 | tf_op jit(solution)/shard_map/ppermute | solution.py:85
  294.5 48.2 %collective-permute-start.28 = (bf16[2,1,272,4352]{3,2,1,0:T(8,128)(2,1)}, bf16[2,1,272,4352]{3,2,1,0:T(8,128)(2,1)}, u32[]{:S(2)}, u32[]{:S(2)}) collective-permute-start(bf16[2,1,272,4352]{3,2,1,0:T(8,128)(2,1)} %constant_dynamic-slice_fusion.15), channel_id=1, source_target_pairs={{0,8},{8,0},{16,24},{24,16},{1,9},{9,1},{17,25},{25,17},{2,10},{10... | collective-permute-start | bytes 14204936 | tf_op jit(solution)/shard_map/ppermute | solution.py:85
  348.6 29.4 %collective-permute-start.29 = (bf16[1,1,544,1088]{3,2,1,0:T(8,128)(2,1)S(1)}, bf16[1,1,544,1088]{3,2,1,0:T(8,128)(2,1)}, u32[]{:S(2)}, u32[]{:S(2)}) collective-permute-start(bf16[1,1,544,1088]{3,2,1,0:T(8,128)(2,1)S(1)} %constant_dynamic-slice_fusion.14), channel_id=1, source_target_pairs={{0,1},{1,0},{2,3},{3,2},{4,5},{5,4},{6,7},{7,6},{8,9},{9,8},{10,11... | collective-permute-start | bytes 3551240 | tf_op jit(solution)/shard_map/ppermute | solution.py:85
  351.7 53.2 %collective-permute-start.30 = (bf16[1,1,272,4352]{3,2,1,0:T(8,128)(2,1)}, bf16[1,1,272,4352]{3,2,1,0:T(8,128)(2,1)}, u32[]{:S(2)}, u32[]{:S(2)}) collective-permute-start(bf16[1,1,272,4352]{3,2,1,0:T(8,128)(2,1)} %constant_dynamic-slice_fusion.13), channel_id=1, source_target_pairs={{0,16},{8,24},{16,0},{24,8},{1,17},{9,25},{17,1},{25,9},{2,18},{10... | collective-permute-start | bytes 7102472 | tf_op jit(solution)/shard_map/ppermute | solution.py:85
  408.0 28.6 %collective-permute-start.31 = (bf16[1,1,272,1088]{3,2,1,0:T(8,128)(2,1)}, bf16[1,1,272,1088]{3,2,1,0:T(8,128)(2,1)}, u32[]{:S(2)}, u32[]{:S(2)}) collective-permute-start(bf16[1,1,272,1088]{3,2,1,0:T(8,128)(2,1)} %constant_dynamic-slice_fusion.12), channel_id=1, source_target_pairs={{0,2},{1,3},{2,0},{3,1},{4,6},{5,7},{6,4},{7,5},{8,10},{9,11},{10,... | collective-permute-start | bytes 1775624 | tf_op jit(solution)/shard_map/ppermute | solution.py:85
  410.7 27.4 %collective-permute-start.32 = (bf16[1,1,136,4352]{3,2,1,0:T(8,128)(2,1)}, bf16[1,1,136,4352]{3,2,1,0:T(8,128)(2,1)}, u32[]{:S(2)}, u32[]{:S(2)}) collective-permute-start(bf16[1,1,136,4352]{3,2,1,0:T(8,128)(2,1)} %constant_dynamic-slice_fusion.11), channel_id=1, source_target_pairs={{0,1},{1,0},{2,3},{3,2},{4,5},{5,4},{6,7},{7,6},{8,9},{9,8},{10,11... | collective-permute-start | bytes 3551240 | tf_op jit(solution)/shard_map/ppermute | solution.py:85
  412.9 27.2 %collective-permute-start.33 = (bf16[2,1,2,272,1088]{4,3,2,1,0:T(8,128)(2,1)}, bf16[2,1,2,272,1088]{4,3,2,1,0:T(8,128)(2,1)}, u32[]{:S(2)}, u32[]{:S(2)}) collective-permute-start(bf16[2,1,2,272,1088]{4,3,2,1,0:T(8,128)(2,1)} %constant_dynamic-slice_fusion.10), channel_id=1, source_target_pairs={{0,8},{8,0},{16,24},{24,16},{1,9},{9,1},{17,25},{25,17},{2,10},{10... | collective-permute-start | bytes 7102472 | tf_op jit(solution)/shard_map/ppermute | solution.py:85
  448.7 29.3 %collective-permute-start.35 = (bf16[1,1,136,2176]{3,2,1,0:T(8,128)(2,1)S(1)}, bf16[1,1,136,2176]{3,2,1,0:T(8,128)(2,1)S(1)}, u32[]{:S(2)}, u32[]{:S(2)}) collective-permute-start(bf16[1,1,136,2176]{3,2,1,0:T(8,128)(2,1)S(1)} %constant_dynamic-slice_fusion.8), channel_id=1, source_target_pairs={{0,2},{1,3},{2,0},{3,1},{4,6},{5,7},{6,4},{7,5},{8,10},{9,11},{10,... | collective-permute-start | bytes 1775624 | tf_op jit(solution)/shard_map/ppermute | solution.py:85
  449.2 26.8 %collective-permute-start.36 = (bf16[1,1,272,1088]{3,2,1,0:T(8,128)(2,1)S(1)}, bf16[1,1,272,1088]{3,2,1,0:T(8,128)(2,1)S(1)}, u32[]{:S(2)}, u32[]{:S(2)}) collective-permute-start(bf16[1,1,272,1088]{3,2,1,0:T(8,128)(2,1)S(1)} %add_convert_fusion.16), channel_id=1, source_target_pairs={{0,4},{1,5},{2,6},{3,7},{4,0},{5,1},{6,2},{7,3},{8,12},{9,13},{10,... | collective-permute-start | bytes 1775624 | tf_op jit(solution)/shard_map/ppermute | solution.py:85
  451.9 29.5 %collective-permute-start.34 = (bf16[1,1,2,272,1088]{4,3,2,1,0:T(8,128)(2,1)S(1)}, bf16[1,1,2,272,1088]{4,3,2,1,0:T(8,128)(2,1)S(1)}, u32[]{:S(2)}, u32[]{:S(2)}) collective-permute-start(bf16[1,1,2,272,1088]{4,3,2,1,0:T(8,128)(2,1)S(1)} %constant_dynamic-slice_fusion.9), channel_id=1, source_target_pairs={{0,16},{8,24},{16,0},{24,8},{1,17},{9,25},{17,1},{25,9},{2,18},{10... | collective-permute-start | bytes 3551240 | tf_op jit(solution)/shard_map/ppermute | solution.py:85
  482.7 20.9 %collective-permute-start.40 = (bf16[1,1,272,1088]{3,2,1,0:T(8,128)(2,1)}, bf16[1,1,272,1088]{3,2,1,0:T(8,128)(2,1)}, u32[]{:S(2)}, u32[]{:S(2)}) collective-permute-start(bf16[1,1,272,1088]{3,2,1,0:T(8,128)(2,1)} %add_convert_fusion.15), channel_id=1, source_target_pairs={{0,2},{1,3},{2,0},{3,1},{4,6},{5,7},{6,4},{7,5},{8,10},{9,11},{10,... | collective-permute-start | bytes 1775624 | tf_op jit(solution)/shard_map/ppermute | solution.py:85
  486.0 35.7 %collective-permute-start.37 = (bf16[2,1,2,272,1088]{4,3,2,1,0:T(8,128)(2,1)}, bf16[2,1,2,272,1088]{4,3,2,1,0:T(8,128)(2,1)}, u32[]{:S(2)}, u32[]{:S(2)}) collective-permute-start(bf16[2,1,2,272,1088]{4,3,2,1,0:T(8,128)(2,1)} %constant_dynamic-slice_fusion.7), channel_id=1, source_target_pairs={{0,8},{8,0},{16,24},{24,16},{1,9},{9,1},{17,25},{25,17},{2,10},{10... | collective-permute-start | bytes 7102472 | tf_op jit(solution)/shard_map/ppermute | solution.py:85
  490.6 30.1 %collective-permute-start.39 = (bf16[1,1,136,2176]{3,2,1,0:T(8,128)(2,1)}, bf16[1,1,136,2176]{3,2,1,0:T(8,128)(2,1)S(1)}, u32[]{:S(2)}, u32[]{:S(2)}) collective-permute-start(bf16[1,1,136,2176]{3,2,1,0:T(8,128)(2,1)} %add_convert_fusion.18), channel_id=1, source_target_pairs={{0,4},{1,5},{2,6},{3,7},{4,0},{5,1},{6,2},{7,3},{8,12},{9,13},{10,... | collective-permute-start | bytes 1775624 | tf_op jit(solution)/shard_map/ppermute | solution.py:85
  494.9 16.3 %collective-permute-start.38 = (bf16[1,1,2,136,1088]{4,3,2,1,0:T(8,128)(2,1)S(1)}, bf16[1,1,2,136,1088]{4,3,2,1,0:T(8,128)(2,1)S(1)}, u32[]{:S(2)}, u32[]{:S(2)}) collective-permute-start(bf16[1,1,2,136,1088]{4,3,2,1,0:T(8,128)(2,1)S(1)} %constant_dynamic-slice_fusion.6), channel_id=1, source_target_pairs={{0,1},{1,0},{2,3},{3,2},{4,5},{5,4},{6,7},{7,6},{8,9},{9,8},{10,11... | collective-permute-start | bytes 1775624 | tf_op jit(solution)/shard_map/ppermute | solution.py:85
  532.1 10.6 %collective-permute-start.42 = (bf16[1,1,1,136,1088]{4,3,2,1,0:T(8,128)(2,1)}, bf16[1,1,1,136,1088]{4,3,2,1,0:T(8,128)(2,1)}, u32[]{:S(2)}, u32[]{:S(2)}) collective-permute-start(bf16[1,1,1,136,1088]{4,3,2,1,0:T(8,128)(2,1)} %constant_dynamic-slice_fusion.4), channel_id=1, source_target_pairs={{0,2},{1,3},{2,0},{3,1},{4,6},{5,7},{6,4},{7,5},{8,10},{9,11},{10,... | collective-permute-start | bytes 887816 | tf_op jit(solution)/shard_map/ppermute | solution.py:85
  534.1 20.2 %collective-permute-start.43 = (bf16[1,1,136,2176]{3,2,1,0:T(8,128)(2,1)}, bf16[1,1,136,2176]{3,2,1,0:T(8,128)(2,1)}, u32[]{:S(2)}, u32[]{:S(2)}) collective-permute-start(bf16[1,1,136,2176]{3,2,1,0:T(8,128)(2,1)} %add_convert_fusion.17), channel_id=1, source_target_pairs={{0,2},{1,3},{2,0},{3,1},{4,6},{5,7},{6,4},{7,5},{8,10},{9,11},{10,... | collective-permute-start | bytes 1775624 | tf_op jit(solution)/shard_map/ppermute | solution.py:85
  538.1 29.1 %collective-permute-start.41 = (bf16[1,1,2,272,1088]{4,3,2,1,0:T(8,128)(2,1)}, bf16[1,1,2,272,1088]{4,3,2,1,0:T(8,128)(2,1)S(1)}, u32[]{:S(2)}, u32[]{:S(2)}) collective-permute-start(bf16[1,1,2,272,1088]{4,3,2,1,0:T(8,128)(2,1)} %constant_dynamic-slice_fusion.5), channel_id=1, source_target_pairs={{0,16},{8,24},{16,0},{24,8},{1,17},{9,25},{17,1},{25,9},{2,18},{10... | collective-permute-start | bytes 3551240 | tf_op jit(solution)/shard_map/ppermute | solution.py:85
  538.5 47.8 %collective-permute-start.57 = (bf16[1,1,544,1088]{3,2,1,0:T(8,128)(2,1)S(1)}, bf16[1,1,544,1088]{3,2,1,0:T(8,128)(2,1)S(1)}, u32[]{:S(2)}, u32[]{:S(2)}) collective-permute-start(bf16[1,1,544,1088]{3,2,1,0:T(8,128)(2,1)S(1)} %copy-done.24), channel_id=1, source_target_pairs={{0,1},{1,0},{2,3},{3,2},{4,5},{5,4},{6,7},{7,6},{8,9},{9,8},{10,11... | collective-permute-start | bytes 3551240 | tf_op jit(solution)/shard_map/ppermute | solution.py:85
  567.5 15.4 %collective-permute-start.45 = (bf16[1,1,1,136,1088]{4,3,2,1,0:T(8,128)(2,1)S(1)}, bf16[1,1,1,136,1088]{4,3,2,1,0:T(8,128)(2,1)S(1)}, u32[]{:S(2)}, u32[]{:S(2)}) collective-permute-start(bf16[1,1,1,136,1088]{4,3,2,1,0:T(8,128)(2,1)S(1)} %add_convert_fusion.22), channel_id=1, source_target_pairs={{0,4},{1,5},{2,6},{3,7},{4,0},{5,1},{6,2},{7,3},{8,12},{9,13},{10,... | collective-permute-start | bytes 887816 | tf_op jit(solution)/shard_map/ppermute | solution.py:85
  567.6 17.1 %collective-permute-start.44 = (bf16[1,1,2,136,1088]{4,3,2,1,0:T(8,128)(2,1)S(1)}, bf16[1,1,2,136,1088]{4,3,2,1,0:T(8,128)(2,1)S(1)}, u32[]{:S(2)}, u32[]{:S(2)}) collective-permute-start(bf16[1,1,2,136,1088]{4,3,2,1,0:T(8,128)(2,1)S(1)} %constant_dynamic-slice_fusion.3), channel_id=1, source_target_pairs={{0,1},{1,0},{2,3},{3,2},{4,5},{5,4},{6,7},{7,6},{8,9},{9,8},{10,11... | collective-permute-start | bytes 1775624 | tf_op jit(solution)/shard_map/ppermute | solution.py:85
  569.2 46.1 %collective-permute-start.56 = (bf16[1,1,136,4352]{3,2,1,0:T(8,128)(2,1)S(1)}, bf16[1,1,136,4352]{3,2,1,0:T(8,128)(2,1)S(1)}, u32[]{:S(2)}, u32[]{:S(2)}) collective-permute-start(bf16[1,1,136,4352]{3,2,1,0:T(8,128)(2,1)S(1)} %pad_maximum_fusion.5), channel_id=1, source_target_pairs={{0,1},{1,0},{2,3},{3,2},{4,5},{5,4},{6,7},{7,6},{8,9},{9,8},{10,11... | collective-permute-start | bytes 3551240 | tf_op jit(solution)/shard_map/ppermute | solution.py:85
  584.9 10.4 %collective-permute-start.48 = (bf16[1,1,1,136,1088]{4,3,2,1,0:T(8,128)(2,1)S(1)}, bf16[1,1,1,136,1088]{4,3,2,1,0:T(8,128)(2,1)S(1)}, u32[]{:S(2)}, u32[]{:S(2)}) collective-permute-start(bf16[1,1,1,136,1088]{4,3,2,1,0:T(8,128)(2,1)S(1)} %add_convert_fusion.21), channel_id=1, source_target_pairs={{0,2},{1,3},{2,0},{3,1},{4,6},{5,7},{6,4},{7,5},{8,10},{9,11},{10,... | collective-permute-start | bytes 887816 | tf_op jit(solution)/shard_map/ppermute | solution.py:85
  587.0 11.9 %collective-permute-start.47 = (bf16[1,1,1,136,1088]{4,3,2,1,0:T(8,128)(2,1)S(1)}, bf16[1,1,1,136,1088]{4,3,2,1,0:T(8,128)(2,1)S(1)}, u32[]{:S(2)}, u32[]{:S(2)}) collective-permute-start(bf16[1,1,1,136,1088]{4,3,2,1,0:T(8,128)(2,1)S(1)} %constant_dynamic-slice_fusion.2), channel_id=1, source_target_pairs={{0,2},{1,3},{2,0},{3,1},{4,6},{5,7},{6,4},{7,5},{8,10},{9,11},{10,... | collective-permute-start | bytes 887816 | tf_op jit(solution)/shard_map/ppermute | solution.py:85
  598.9 12.3 %collective-permute-start.51 = (f32[4,3264]{1,0:T(4,128)S(1)}, f32[4,3264]{1,0:T(4,128)S(1)}, u32[]{:S(2)}, u32[]{:S(2)}) collective-permute-start(f32[4,3264]{1,0:T(4,128)S(1)} %add.470), channel_id=1, source_target_pairs={{0,1},{1,0},{2,3},{3,2},{4,5},{5,4},{6,7},{7,6},{8,9},{9,8},{10,11... | collective-permute-start | bytes 156680 | tf_op jit(solution)/shard_map/ppermute | solution.py:85
  600.5 12.6 %collective-permute-start.50 = (bf16[1,1,1,136,1088]{4,3,2,1,0:T(8,128)(2,1)S(1)}, bf16[1,1,1,136,1088]{4,3,2,1,0:T(8,128)(2,1)S(1)}, u32[]{:S(2)}, u32[]{:S(2)}) collective-permute-start(bf16[1,1,1,136,1088]{4,3,2,1,0:T(8,128)(2,1)S(1)} %add_convert_fusion.20), channel_id=1, source_target_pairs={{0,4},{1,5},{2,6},{3,7},{4,0},{5,1},{6,2},{7,3},{8,12},{9,13},{10,... | collective-permute-start | bytes 887816 | tf_op jit(solution)/shard_map/ppermute | solution.py:85
  603.7 19.9 %collective-permute-start.55 = (bf16[1,1,2,136,1088]{4,3,2,1,0:T(8,128)(2,1)S(1)}, bf16[1,1,2,136,1088]{4,3,2,1,0:T(8,128)(2,1)S(1)}, u32[]{:S(2)}, u32[]{:S(2)}) collective-permute-start(bf16[1,1,2,136,1088]{4,3,2,1,0:T(8,128)(2,1)S(1)} %pad_maximum_fusion.10), channel_id=1, source_target_pairs={{0,1},{1,0},{2,3},{3,2},{4,5},{5,4},{6,7},{7,6},{8,9},{9,8},{10,11... | collective-permute-start | bytes 1775624 | tf_op jit(solution)/shard_map/ppermute | solution.py:85
  622.2 13.4 %collective-permute-start.54 = (bf16[1,1,2,136,1088]{4,3,2,1,0:T(8,128)(2,1)S(1)}, bf16[1,1,2,136,1088]{4,3,2,1,0:T(8,128)(2,1)S(1)}, u32[]{:S(2)}, u32[]{:S(2)}) collective-permute-start(bf16[1,1,2,136,1088]{4,3,2,1,0:T(8,128)(2,1)S(1)} %pad_maximum_fusion.11), channel_id=1, source_target_pairs={{0,1},{1,0},{2,3},{3,2},{4,5},{5,4},{6,7},{7,6},{8,9},{9,8},{10,11... | collective-permute-start | bytes 1775624 | tf_op jit(solution)/shard_map/ppermute | solution.py:85
  (104 other events, 1027.8 us)
